TPU v7x, 128 devices: a whole 4x4x4 slice. The times are simulated.
128 devices in a mesh: row: 8 (over y, z_hi), col: 16 (over z_lo, x, core).
Axes of the slice: x: 4, y: 4, z: 4 (z_hi: 2, z_lo: 2; z = z_hi * 2 + z_lo), core: 2. Of those that a mesh axis runs over, the one named last changes fastest.
Arguments:
- object_field: bfloat16 [2, 4096, 16384], P(None, 'row', 'col'), may hold values from -5 to 5
- probe_modes: bfloat16 [4, 2, 512, 512], replicated, may hold values from -5 to 5
- positions: int32 [128, 2], P(('row', 'col')), may hold values from 0 to 15872, as said below
- amplitudes: float32 [128, 512, 512], P(('row', 'col')), may hold values from 0.5 to 3
- live_slots: int32 [128], P(('row', 'col')), may hold values from 0 to 1, as said below
Outputs:
- object_grad: float32 [2, 4096, 16384], P(None, 'row', 'col')
- probe_grad: float32 [4, 2, 512, 512], P(None, None, ('row', 'col'))
Inputs may be any that keep to these rules, and one draw needn't show every extreme that they name: `positions`: every window lies inside the object, and the top-left pixel of slot p lies in tile (r, c), rows r * 512 to (r + 1) * 512 - 1 and columns c * 1024 to (c + 1) * 1024 - 1, where p = r * 16 + c. Slot 0's window starts at pixel (0, 0) and the last slot's window ends at the object's lower right corner. `live_slots`: each slot is live or not; in every draw at least one slot is live.
All inputs are finite; a program needn't handle non-finite values.
Results may differ from a plain program's by a relative error of at most 0.0093.
Values may be sent and summed in bfloat16 or wider, within the bound.
No kernel may reach another device: no remote copies, remote signals or barrier semaphores. Data moves between devices by JAX's collectives and lax.ppermute only.
A program may use at most 128 MiB of HBM per device.

v0:
```python
import math

import jax
import jax.numpy as jnp
from jax import lax
from jax.sharding import PartitionSpec as P


def passed_along(block, axis, distance):
    devices = range(lax.axis_size(axis))
    route = [(i - distance, i) for i in devices if i - distance in devices]
    return lax.ppermute(block, axis, route)


def tables(patch_size):
    pixel_index = jnp.arange(patch_size, dtype=jnp.int32)
    phase_step = pixel_index[:, None] * pixel_index[None, :] % patch_size
    angle_rad = phase_step.astype(jnp.float32) * (2.0 * math.pi / patch_size)
    norm_scale = 1.0 / math.sqrt(patch_size)
    cosine = (jnp.cos(angle_rad) * norm_scale).astype(jnp.bfloat16)
    sine_table = (jnp.sin(angle_rad) * norm_scale).astype(jnp.bfloat16)
    return (cosine, sine_table)


def band_matrix(cosine, sine_table, sign_value):
    upper_band = jnp.concatenate([cosine, sign_value * sine_table], axis=1)
    lower_band = jnp.concatenate([-sign_value * sine_table, cosine], axis=1)
    return jnp.concatenate([upper_band, lower_band], axis=0)


def transform(field_in, left_matrix, cosine, sine_table, sign_value):
    mode_count, patch_size = (field_in.shape[0], field_in.shape[-1])
    stacked = field_in.reshape(mode_count, 2 * patch_size, patch_size)
    first_pass = jnp.einsum("xy,myb->mxb", left_matrix, stacked, preferred_element_type=jnp.float32)
    first_pass = first_pass.astype(jnp.bfloat16).reshape(mode_count, 2, patch_size, patch_size)
    with_cos = jnp.einsum("mpab,bc->mpac", first_pass, cosine, preferred_element_type=jnp.float32)
    with_sin = jnp.einsum(
        "mpab,bc->mpac", first_pass, sine_table, preferred_element_type=jnp.float32
    )
    real_part = with_cos[:, 0] + sign_value * with_sin[:, 1]
    imag_part = with_cos[:, 1] - sign_value * with_sin[:, 0]
    return jnp.stack([real_part, imag_part], axis=1)


def exit_wave(probe_modes, patch_data):
    probe_real = probe_modes[:, 0].astype(jnp.float32)
    probe_imag = probe_modes[:, 1].astype(jnp.float32)
    patch_real = patch_data[0].astype(jnp.float32)
    patch_imag = patch_data[1].astype(jnp.float32)
    real_part = probe_real * patch_real - probe_imag * patch_imag
    imag_part = probe_real * patch_imag + probe_imag * patch_real
    return jnp.stack([real_part, imag_part], axis=1).astype(jnp.bfloat16)


def residue(far_field, amplitude, live_flag):
    intensity = jnp.sum(
        far_field[:, 0] * far_field[:, 0] + far_field[:, 1] * far_field[:, 1], axis=0
    )
    modulus = jnp.sqrt(jnp.maximum(intensity, 0.25))
    weight = live_flag.astype(jnp.float32) * (1.0 - amplitude / modulus)
    return (far_field * weight[None, None]).astype(jnp.bfloat16)


def object_term(probe_modes, exit_grad):
    probe_real = probe_modes[:, 0].astype(jnp.float32)
    probe_imag = probe_modes[:, 1].astype(jnp.float32)
    grad_real = exit_grad[:, 0]
    grad_imag = exit_grad[:, 1]
    real_part = jnp.sum(probe_real * grad_real + probe_imag * grad_imag, axis=0)
    imag_part = jnp.sum(probe_real * grad_imag - probe_imag * grad_real, axis=0)
    return jnp.stack([real_part, imag_part], axis=0)


def probe_term(patch_data, exit_grad):
    patch_real = patch_data[0].astype(jnp.float32)
    patch_imag = patch_data[1].astype(jnp.float32)
    grad_real = exit_grad[:, 0]
    grad_imag = exit_grad[:, 1]
    real_part = patch_real * grad_real + patch_imag * grad_imag
    imag_part = patch_real * grad_imag - patch_imag * grad_real
    return jnp.stack([real_part, imag_part], axis=1)


def deposit(grad_region, row_start, col_start, grad_term):
    zero_index = jnp.zeros((), jnp.int32)
    corner = (zero_index, row_start, col_start)
    current = lax.dynamic_slice(grad_region, corner, grad_term.shape)
    return lax.dynamic_update_slice(grad_region, current + grad_term, corner)


def take_out(grad_region, row_start, col_start, patch_size):
    zero_index = jnp.zeros((), jnp.int32)
    corner = (zero_index, row_start, col_start)
    piece = lax.dynamic_slice(grad_region, corner, (2, patch_size, patch_size))
    grad_region = lax.dynamic_update_slice(grad_region, jnp.zeros_like(piece), corner)
    return (grad_region, piece)


def per_device(object_field, probe_modes, positions, amplitudes, live_slots):
    mode_count, patch_size = (probe_modes.shape[0], probe_modes.shape[-1])
    tile_rows, tile_cols = (object_field.shape[1], object_field.shape[2])
    row_anchor = lax.axis_index("row") * tile_rows
    col_anchor = lax.axis_index("col") * tile_cols
    zero_index = jnp.zeros((), jnp.int32)
    left_corners = passed_along(positions, "col", 1)
    upper_corners = passed_along(positions, "row", 1)
    own_rows = jnp.clip(positions[:, 0] - row_anchor, 0, tile_rows - patch_size)
    own_cols = jnp.clip(positions[:, 1] - col_anchor, 0, tile_cols - patch_size)
    left_rows = jnp.clip(left_corners[:, 0] - row_anchor, 0, tile_rows - patch_size)
    upper_cols = jnp.clip(upper_corners[:, 1] - col_anchor, 0, tile_cols - patch_size)
    right_part = passed_along(object_field, "col", -1)
    upper_strip = jnp.concatenate([object_field, right_part], axis=2)
    lower_part = passed_along(upper_strip, "row", -1)
    region = jnp.concatenate(
        [
            upper_strip[:, :, : tile_cols + patch_size],
            lower_part[:, :patch_size, : tile_cols + patch_size],
        ],
        axis=1,
    )
    cosine, sine_table = tables(patch_size)
    forward_matrix = band_matrix(cosine, sine_table, 1.0)
    adjoint_matrix = band_matrix(cosine, sine_table, -1.0)
    offsets, patches, residues = ([], [], [])
    slot_index = 0
    top_offset = positions[slot_index, 0] - row_anchor
    left_offset = positions[slot_index, 1] - col_anchor
    patch_data = lax.dynamic_slice(
        region, (zero_index, top_offset, left_offset), (2, patch_size, patch_size)
    )
    far_field = transform(
        exit_wave(probe_modes, patch_data), forward_matrix, cosine, sine_table, 1.0
    )
    residues.append(residue(far_field, amplitudes[slot_index], live_slots[slot_index]))
    patches.append(patch_data)
    offsets.append((top_offset, left_offset))
    grad_region = jnp.zeros((2, tile_rows + patch_size, tile_cols + patch_size), jnp.float32)
    slot_index = 0
    exit_grad = transform(residues[slot_index], adjoint_matrix, cosine, sine_table, -1.0)
    grad_region = deposit(
        grad_region,
        offsets[slot_index][0],
        offsets[slot_index][1],
        object_term(probe_modes, exit_grad),
    )
    probe_local = probe_term(patches[slot_index], exit_grad)
    probe_grad = lax.psum_scatter(probe_local, ("row", "col"), scatter_dimension=2, tiled=True)
    row_edge = jnp.array(tile_rows, jnp.int32)
    col_edge = jnp.array(tile_cols, jnp.int32)
    slot_index = 0
    grad_region, piece = take_out(grad_region, row_edge, own_cols[slot_index], patch_size)
    lower_out = [piece]
    corner_grad = grad_region[:, tile_rows:, tile_cols:]
    got_lower, got_corner = passed_along((jnp.stack(lower_out, axis=0), corner_grad), "row", 1)
    upper_rows = grad_region[:, :tile_rows, :]
    slot_index = 0
    upper_rows = deposit(upper_rows, zero_index, upper_cols[slot_index], got_lower[slot_index])
    slot_index = 0
    upper_rows, piece = take_out(upper_rows, own_rows[slot_index], col_edge, patch_size)
    right_out = [piece]
    got_right, got_diagonal = passed_along((jnp.stack(right_out, axis=0), got_corner), "col", 1)
    object_grad = upper_rows[:, :, :tile_cols]
    slot_index = 0
    object_grad = deposit(object_grad, left_rows[slot_index], zero_index, got_right[slot_index])
    object_grad = object_grad.at[:, :patch_size, :patch_size].add(got_diagonal)
    return (object_grad, probe_grad)


def solution(mesh):
    placed = (
        P(None, "row", "col"),
        P(),
        P(("row", "col"), None),
        P(("row", "col"), None, None),
        P(("row", "col")),
    )
    return jax.shard_map(
        per_device,
        mesh=mesh,
        in_specs=placed,
        out_specs=(P(None, "row", "col"), P(None, None, ("row", "col"), None)),
        check_vma=False,
    )
```

profile of v0, /device:TPU:1, one launch (start us, length us, event | category | flops | bytes accessed | tf_op | source)
XLA Modules:
  0.0 540.0 jit_solution(7833156270979319623)
XLA Ops:
  7.2 3.3 collective-permute-start
  10.6 3.1 constant_dynamic-update-slice_fusion.1
  13.6 22.4 %collective-permute-done = bf16[2,512,1024]{2,1,0:T(8,128)(2,1)S(1)} collective-permute-done((bf16[2,512,1024]{2,1,0:T(8,128)(2,1)}, bf16[2,512,1024]{2,1,0:T(8,128)(2,1)S(1)}, u32[]{:S(2)}, u32[]{:S(2)}) %collective-permute-start) | collective-permute-done | bytes 2097184 | tf_op jit(solution)/shard_map/ppermute | solution.py:12
  36.0 1.5 constant_dynamic-update-slice_fusion
  42.0 4.0 fusion.42
  46.1 4.4 multiply_convert_fusion.4
  50.5 2.5 slice.112
  53.0 60.3 %collective-permute-done.1 = bf16[2,512,2048]{2,1,0:T(8,128)(2,1)} collective-permute-done((bf16[2,512,2048]{2,1,0:T(8,128)(2,1)}, bf16[2,512,2048]{2,1,0:T(8,128)(2,1)}, u32[]{:S(2)}, u32[]{:S(2)}) %collective-permute-start.1) | collective-permute-done | bytes 4194336 | tf_op jit(solution)/shard_map/ppermute | solution.py:12
  113.3 2.1 slice.113
  115.4 1.8 fusion.25
  117.6 1.5 fusion.1
  119.5 12.0 %convert_bitcast_fusion.1 = bf16[4,1024,512]{1,2,0:T(8,128)(2,1)} fusion(bf16[4,1024,512]{2,1,0:T(8,128)(2,1)S(1)} %bitcast.79, bf16[512,512]{1,0:T(8,128)(2,1)S(1)} %get-tuple-element.30, bf16[512,512]{1,0:T(8,128)(2,1)S(1)} %fusion.42, bf16[512,512]{1,0:T(8,128)(2,1)S(1)} %get-tuple-element.29), kind=kOutput, calls=%fused_computation.34 | convolution fusion | flops 4305453056 | bytes 9961472 | tf_op jit(solution)/shard_map/xy,myb->mxb/dot_general | solution.py:34
  131.5 6.4 %copy.26 = bf16[4,1024,512]{2,1,0:T(8,128)(2,1)} copy(bf16[4,1024,512]{1,2,0:T(8,128)(2,1)} %convert_bitcast_fusion.1) | data formatting | bytes 8388608 | tf_op jit(solution)/shard_map/reshape | solution.py:35
  137.9 7.6 %fusion.36 = f32[4,2,512,512]{3,2,1,0:T(8,128)S(1)} fusion(bf16[4,2,512,512]{3,2,1,0:T(8,128)(2,1)} %bitcast.80), kind=kOutput, calls=%fused_computation.75 | convolution fusion | flops 2151677952 | bytes 12582912 | tf_op jit(solution)/shard_map/mpab,bc->mpac/dot_general | solution.py:36
  145.5 8.4 %fusion.40 = f32[4,2,512,512]{3,2,1,0:T(8,128)} fusion(bf16[4,2,512,512]{3,2,1,0:T(8,128)(2,1)S(1)} %bitcast.81), kind=kOutput, calls=%fused_computation.79 | convolution fusion | flops 2151677952 | bytes 12582912 | tf_op jit(solution)/shard_map/mpab,bc->mpac/dot_general | solution.py:37
  154.0 4.7 add_reduce_fusion
  158.7 4.3 pad_maximum_fusion
  163.0 8.9 %copy.18 = f32[4,1024,512]{1,2,0:T(8,128)} copy(f32[4,1024,512]{2,1,0:T(8,128)} %bitcast.77) | data formatting | bytes 16777216 | tf_op jit(solution)/shard_map/stack | solution.py:42
  171.9 2.4 fusion.27
  174.3 1.6 copy.17
  177.3 15.8 %convert_bitcast_fusion = bf16[4,1024,512]{1,2,0:T(8,128)(2,1)} fusion(f32[4,1024,512]{1,2,0:T(8,128)} %copy.18, f32[1024,512]{0,1:T(8,128)S(1)} %bitcast.86, bf16[512,512]{1,0:T(8,128)(2,1)S(1)} %copy-done.11, bf16[512,512]{1,0:T(8,128)(2,1)S(1)} %copy-done.9, bf16[512,512]{1,0:T(8,128)(2,1)S(1)} %copy-done.7), kind=kOutput, calls=%fused_computation.31 | convolution fusion | flops 4309647360 | bytes 16252928 | tf_op jit(solution)/shard_map/xy,myb->mxb/dot_general | solution.py:34
  193.0 6.3 %copy.27 = bf16[4,1024,512]{2,1,0:T(8,128)(2,1)} copy(bf16[4,1024,512]{1,2,0:T(8,128)(2,1)} %convert_bitcast_fusion) | data formatting | bytes 8388608 | tf_op jit(solution)/shard_map/reshape | solution.py:35
  199.3 10.7 %fusion.34 = f32[4,2,512,512]{3,2,1,0:T(8,128)} fusion(bf16[4,2,512,512]{3,2,1,0:T(8,128)(2,1)} %bitcast.82), kind=kOutput, calls=%fused_computation.73 | convolution fusion | flops 2151677952 | bytes 12582912 | tf_op jit(solution)/shard_map/mpab,bc->mpac/dot_general | solution.py:36
  210.0 8.6 %fusion.38 = f32[4,2,512,512]{3,2,1,0:T(8,128)} fusion(bf16[4,2,512,512]{3,2,1,0:T(8,128)(2,1)S(1)} %bitcast.83), kind=kOutput, calls=%fused_computation.77 | convolution fusion | flops 2151677952 | bytes 12582912 | tf_op jit(solution)/shard_map/mpab,bc->mpac/dot_general | solution.py:37
  218.6 8.8 %multiply_add_fusion = (f32[4,1,512,512]{3,2,1,0:T(8,128)}, f32[4,1,512,512]{3,2,1,0:T(8,128)S(1)}, f32[4,1,512,512]{3,2,1,0:T(8,128)S(1)}) fusion(f32[512,512]{1,0:T(8,128)S(1)} %get-tuple-element.26, f32[512,512]{1,0:T(8,128)S(1)} %get-tuple-element.25, f32[4,2,512,512]{3,2,1,0:T(8,128)} %fusion.38, f32[4,2,512,512]{3,2,1,0:T(8,128)} %fusion.34), kind=kLoop, calls=%fused_computation.30 | loop fusion | flops 7340032 | bytes 31457280 | tf_op jit(solution)/shard_map/add | solution.py:79
  227.4 3.6 fusion.5
  231.2 6.1 %broadcast_in_dim.2 = f32[2,1024,1536]{2,1,0:T(8,128)} broadcast(f32[]{:T(128)} %constant.62.clone.1), dimensions={} | broadcast | bytes 12582916 | tf_op jit(solution)/shard_map/broadcast_in_dim | solution.py:137
  237.3 14.2 %dynamic_update_slice.15 = f32[2,1024,1536]{2,1,0:T(8,128)} dynamic-update-slice(f32[2,1024,1536]{2,1,0:T(8,128)} %broadcast_in_dim.2, f32[2,512,512]{2,1,0:T(8,128)S(1)} %pad_maximum_fusion.9, s32[]{:T(128)} %constant.63.clone.1, s32[]{:T(128)S(6)} %select_n.49, s32[]{:T(128)S(6)} %select_n.50) | dynamic-update-slice | bytes 4194308 | tf_op jit(solution)/shard_map/dynamic_update_slice | solution.py:88
  251.5 3.8 dynamic-slice_bitcast_fusion
  255.3 7.6 %collective-permute-start.3 = (f32[1,2,512,512]{3,2,1,0:T(8,128)}, f32[1,2,512,512]{3,2,1,0:T(8,128)}, u32[]{:S(2)}, u32[]{:S(2)}) collective-permute-start(f32[1,2,512,512]{3,2,1,0:T(8,128)} %dynamic-slice_bitcast_fusion), channel_id=1, source_target_pairs={{0,16},{16,32},{32,48},{48,64},{64,80},{80,96},{96,112},{1,17},{17... | collective-permute-start | bytes 6291464 | tf_op jit(solution)/shard_map/ppermute | solution.py:12
  262.9 6.4 %pad_maximum_fusion.1 = f32[4,2,512,512]{3,2,1,0:T(8,128)} fusion(f32[4,1,512,512]{3,2,1,0:T(8,128)} %get-tuple-element.22, f32[4,1,512,512]{3,2,1,0:T(8,128)S(1)} %copy-done.3), kind=kLoop, calls=%fused_computation.1 | loop fusion | flops 2097152 | bytes 16777216 | tf_op jit(solution)/shard_map/stack | solution.py:81
  269.6 13.3 %dynamic_update_slice.16 = f32[2,1024,1536]{2,1,0:T(8,128)} dynamic-update-slice(f32[2,1024,1536]{2,1,0:T(8,128)} %dynamic_update_slice.15, f32[2,512,512]{2,1,0:T(8,128)S(1)} %broadcast.78, s32[]{:T(128)} %constant.63.clone.1, s32[]{:T(128)} %constant.66.clone.1, s32[]{:T(128)S(6)} %select_n.52) | dynamic-update-slice | bytes 4194308 | tf_op jit(solution)/shard_map/dynamic_update_slice | solution.py:95
  282.9 3.1 slice.126
  286.0 2.6 collective-permute-start.5
  288.6 1.8 collective-permute-start.2
  290.4 55.5 %collective-permute-done.2 = s32[1,2]{1,0:T(1,128)S(1)} collective-permute-done((s32[1,2]{1,0:T(1,128)S(1)}, s32[1,2]{1,0:T(1,128)S(1)}, u32[]{:S(2)}, u32[]{:S(2)}) %collective-permute-start.2) | collective-permute-done | bytes 40 | tf_op jit(solution)/shard_map/ppermute | solution.py:12
  347.2 3.2 slice.124
  350.4 2.6 copy-done
  353.1 2.2 bitcast_add_fusion
  355.3 10.6 %dynamic_update_slice.17 = f32[2,512,1536]{2,1,0:T(8,128)} dynamic-update-slice(f32[2,512,1536]{2,1,0:T(8,128)} %copy-done, f32[2,512,512]{2,1,0:T(8,128)S(1)} %bitcast_add_fusion, s32[]{:T(128)} %constant.63.clone.1, s32[]{:T(128)} %constant.63.clone.1, s32[]{:T(128)S(6)} %select_n.53) | dynamic-update-slice | bytes 4194308 | tf_op jit(solution)/shard_map/dynamic_update_slice | solution.py:88
  365.9 3.2 slice_bitcast_fusion
  369.0 42.4 %collective-permute-start.4 = (f32[1,2,512,512]{3,2,1,0:T(8,128)}, f32[1,2,512,512]{3,2,1,0:T(8,128)S(1)}, u32[]{:S(2)}, u32[]{:S(2)}) collective-permute-start(f32[1,2,512,512]{3,2,1,0:T(8,128)} %slice_bitcast_fusion), channel_id=1, source_target_pairs={{0,1},{1,2},{2,3},{3,4},{4,5},{5,6},{6,7},{7,8},{8,9},{9,10},{10,1... | collective-permute-start | bytes 6291464 | tf_op jit(solution)/shard_map/ppermute | solution.py:12
  411.5 1.9 collective-permute-start.6
  413.4 4.8 slice.125
  418.2 105.2 %all-reduce.3.cloned.1.call-done = f32[4,2,512,512]{3,2,1,0:T(8,128)} async-done(((f32[4,2,512,512]{3,2,1,0:T(8,128)}), f32[4,2,512,512]{3,2,1,0:T(8,128)}) %all-reduce.3.cloned.1.call-update) | async-done | bytes 8388624
  523.5 1.5 constant_dynamic-slice_fusion
  525.0 3.4 fusion.31
  528.4 4.3 add_dynamic-update-slice_fusion
  (40 shorter events, 5.0 us)
Async XLA Ops:
  7.2 31.7 %copy-start.12 = (s32[1,2]{1,0:T(1,128)S(1)}, s32[1,2]{1,0:T(1,128)}, u32[]{:S(2)}) copy-start(s32[1,2]{1,0:T(1,128)} %param.9) | copy-start | bytes 28
  7.2 516.3 %all-reduce.3.cloned.1.call-start = ((), (), s32[]{:S(2)}) async-start(), calls=%async_computation | async-start | bytes 16777216
  7.2 28.8 %collective-permute-start = (bf16[2,512,1024]{2,1,0:T(8,128)(2,1)}, bf16[2,512,1024]{2,1,0:T(8,128)(2,1)S(1)}, u32[]{:S(2)}, u32[]{:S(2)}) collective-permute-start(bf16[2,512,1024]{2,1,0:T(8,128)(2,1)} %param.7), channel_id=1, source_target_pairs={{1,0},{2,1},{3,2},{4,3},{5,4},{6,5},{7,6},{8,7},{9,8},{10,9},{11,1... | collective-permute-start | bytes 6291464 | tf_op jit(solution)/shard_map/ppermute | solution.py:12
  37.5 75.8 %collective-permute-start.1 = (bf16[2,512,2048]{2,1,0:T(8,128)(2,1)}, bf16[2,512,2048]{2,1,0:T(8,128)(2,1)}, u32[]{:S(2)}, u32[]{:S(2)}) collective-permute-start(bf16[2,512,2048]{2,1,0:T(8,128)(2,1)} %constant_dynamic-update-slice_fusion), channel_id=1, source_target_pairs={{16,0},{32,16},{48,32},{64,48},{80,64},{96,80},{112,96},{17,1},{33... | collective-permute-start | bytes 12582920 | tf_op jit(solution)/shard_map/ppermute | solution.py:12
  46.1 73.4 %copy-start.6 = (bf16[512,512]{1,0:T(8,128)(2,1)}, bf16[512,512]{1,0:T(8,128)(2,1)S(1)}, u32[]{:S(2)}) copy-start(bf16[512,512]{1,0:T(8,128)(2,1)S(1)} %fusion.42) | copy-start | bytes 1572868
  50.5 69.0 %copy-start.8 = (bf16[512,512]{1,0:T(8,128)(2,1)}, bf16[512,512]{1,0:T(8,128)(2,1)S(1)}, u32[]{:S(2)}) copy-start(bf16[512,512]{1,0:T(8,128)(2,1)S(1)} %get-tuple-element.29) | copy-start | bytes 1572868
  50.5 69.0 %copy-start.10 = (bf16[512,512]{1,0:T(8,128)(2,1)}, bf16[512,512]{1,0:T(8,128)(2,1)S(1)}, u32[]{:S(2)}) copy-start(bf16[512,512]{1,0:T(8,128)(2,1)S(1)} %get-tuple-element.30) | copy-start | bytes 1572868
  115.4 2.2 copy-start.1
  137.9 7.6 %copy-start.4 = (bf16[4,1024,512]{2,1,0:T(8,128)(2,1)S(1)}, bf16[4,1024,512]{2,1,0:T(8,128)(2,1)}, u32[]{:S(2)}) copy-start(bf16[4,1024,512]{2,1,0:T(8,128)(2,1)} %copy.26) | copy-start | bytes 12582916
  175.9 1.2 copy-start.7
  175.9 1.2 copy-start.9
  175.9 1.3 copy-start.11
  199.3 10.7 %copy-start.5 = (bf16[4,1024,512]{2,1,0:T(8,128)(2,1)S(1)}, bf16[4,1024,512]{2,1,0:T(8,128)(2,1)}, u32[]{:S(2)}) copy-start(bf16[4,1024,512]{2,1,0:T(8,128)(2,1)} %copy.27) | copy-start | bytes 12582916
  218.6 8.8 %copy-start.2 = (bf16[4,2,512,512]{3,2,1,0:T(8,128)(2,1)S(1)}, bf16[4,2,512,512]{3,2,1,0:T(8,128)(2,1)}, u32[]{:S(2)}) copy-start(bf16[4,2,512,512]{3,2,1,0:T(8,128)(2,1)} %param.8) | copy-start | bytes 12582916
  251.5 11.4 %copy-start.3 = (f32[4,1,512,512]{3,2,1,0:T(8,128)S(1)}, f32[4,1,512,512]{3,2,1,0:T(8,128)}, u32[]{:S(2)}) copy-start(f32[4,1,512,512]{3,2,1,0:T(8,128)} %get-tuple-element.16) | copy-start | bytes 12582916
  255.3 95.1 %collective-permute-start.3 = (f32[1,2,512,512]{3,2,1,0:T(8,128)}, f32[1,2,512,512]{3,2,1,0:T(8,128)}, u32[]{:S(2)}, u32[]{:S(2)}) collective-permute-start(f32[1,2,512,512]{3,2,1,0:T(8,128)} %dynamic-slice_bitcast_fusion), channel_id=1, source_target_pairs={{0,16},{16,32},{32,48},{48,64},{64,80},{80,96},{96,112},{1,17},{17... | collective-permute-start | bytes 6291464 | tf_op jit(solution)/shard_map/ppermute | solution.py:12
  286.0 125.5 %collective-permute-start.5 = (f32[2,512,512]{2,1,0:T(8,128)}, f32[2,512,512]{2,1,0:T(8,128)}, u32[]{:S(2)}, u32[]{:S(2)}) collective-permute-start(f32[2,512,512]{2,1,0:T(8,128)} %slice.126), channel_id=1, source_target_pairs={{0,16},{16,32},{32,48},{48,64},{64,80},{80,96},{96,112},{1,17},{17... | collective-permute-start | bytes 6291464 | tf_op jit(solution)/shard_map/ppermute | solution.py:12
  288.6 57.3 %collective-permute-start.2 = (s32[1,2]{1,0:T(1,128)S(1)}, s32[1,2]{1,0:T(1,128)S(1)}, u32[]{:S(2)}, u32[]{:S(2)}) collective-permute-start(s32[1,2]{1,0:T(1,128)S(1)} %copy-done.12), channel_id=1, source_target_pairs={{0,16},{16,32},{32,48},{48,64},{64,80},{80,96},{96,112},{1,17},{17... | collective-permute-start | bytes 32 | tf_op jit(solution)/shard_map/ppermute | solution.py:12
  350.4 2.7 copy-start
  369.0 156.0 %collective-permute-start.4 = (f32[1,2,512,512]{3,2,1,0:T(8,128)}, f32[1,2,512,512]{3,2,1,0:T(8,128)S(1)}, u32[]{:S(2)}, u32[]{:S(2)}) collective-permute-start(f32[1,2,512,512]{3,2,1,0:T(8,128)} %slice_bitcast_fusion), channel_id=1, source_target_pairs={{0,1},{1,2},{2,3},{3,4},{4,5},{5,6},{6,7},{7,8},{8,9},{9,10},{10,1... | collective-permute-start | bytes 6291464 | tf_op jit(solution)/shard_map/ppermute | solution.py:12
  411.5 116.9 %collective-permute-start.6 = (f32[2,512,512]{2,1,0:T(8,128)}, f32[2,512,512]{2,1,0:T(8,128)}, u32[]{:S(2)}, u32[]{:S(2)}) collective-permute-start(f32[2,512,512]{2,1,0:T(8,128)} %collective-permute-done.5), channel_id=1, source_target_pairs={{0,1},{1,2},{2,3},{3,4},{4,5},{5,6},{6,7},{7,8},{8,9},{9,10},{10,1... | collective-permute-start | bytes 6291464 | tf_op jit(solution)/shard_map/ppermute | solution.py:12
Sparse Core Ops, SparseCore 0:
  269.5 253.9 all-reduce.2
where the time goes:
time: 551 us; the launch traced here: 540 us
  waiting for transfers between devices  244 us (44%)
  local copies, waits for them, and re-layouts  102 us (19%)
  matrix products  63.2 us (11%)
  starting transfers between devices  61 us (11%)
  other arithmetic  52.7 us (10%)
  between operations  18.1 us (3%)
    ppermute x7, waiting for transfers between devices, passed_along(): return lax.ppermute(block, axis, route)  138 us
    unnamed x2, waiting for transfers between devices  105 us
    ppermute x7, starting transfers between devices, passed_along(): return lax.ppermute(block, axis, route)  61 us
    dot_general x2, matrix products, transform(): jnp.einsum('xy,myb->mxb', left_matrix, stacked, preferred_element_type=jn...  27.8 us
    dynamic_update_slice x2, local copies, waits for them, and re-layouts, deposit(): return lax.dynamic_update_slice(grad_region, current + grad_term, corner)  24.7 us
    dot_general x2, matrix products, transform(): jnp.einsum('mpab,bc->mpac', first_pass, cosine, preferred_element_type=jn...  18.3 us
    dot_general x2, matrix products, transform(): jnp.einsum('mpab,bc->mpac', first_pass, sine_table, preferred_element_typ...  17 us
    dynamic_update_slice x1, local copies, waits for them, and re-layouts, take_out(): lax.dynamic_update_slice(grad_region, jnp.zeros_like(piece), corner)  13.3 us
  transfers between devices with their start and end apart: 8, of which 4 were waited for; matrix products, arithmetic and copies ran while one was open for 12% of the time, Pallas kernels for 0%

commit v1 on v0

v1 whole, which is shorter than its diff:
```python
import functools
import math

import jax
import jax.numpy as jnp
import ml_dtypes
import numpy as np
from jax import lax
from jax.experimental import pallas as pl
from jax.experimental.pallas import tpu as pltpu
from jax.sharding import PartitionSpec as P

W = 512
Q = W // 4
AXES = ("row", "col")
MIB = 1024 * 1024
F32 = jnp.float32
BF16 = jnp.bfloat16


def block_tables():
    step = np.arange(W).astype(np.float32) * np.float32(2.0 * math.pi / W)
    scale = np.float32(1.0 / math.sqrt(W))
    cos_of = (np.cos(step) * scale).astype(ml_dtypes.bfloat16).astype(np.float32)
    sin_of = (np.sin(step) * scale).astype(ml_dtypes.bfloat16).astype(np.float32)
    short = np.arange(Q)
    forward, adjoint = [], []
    for part in range(4):
        phase = np.outer(4 * short + part, short) % W
        c, s = cos_of[phase], sin_of[phase]
        forward.append(np.block([[c, s], [-s, c]]))
        adjoint.append(np.block([[c.T, -s.T], [s.T, c.T]]))
    forward = np.stack(forward).astype(ml_dtypes.bfloat16)
    adjoint = np.stack(adjoint).astype(ml_dtypes.bfloat16)
    swap = lambda t: np.ascontiguousarray(t.transpose(0, 2, 1))
    return forward, swap(forward), adjoint, swap(adjoint)


def fold(parts, sign):
    (ar, ai), (br, bi), (cr, ci), (dr, di) = parts
    pr, pi, mr, mi = ar + cr, ai + ci, ar - cr, ai - ci
    qr, qi, nr, ni = br + dr, bi + di, br - dr, bi - di
    if sign < 0:
        nr, ni = -nr, -ni
    return (
        (pr + qr, pi + qi),
        (mr + ni, mi - nr),
        (pr - qr, pi - qi),
        (mr - ni, mi + nr),
    )


def dot(a, b):
    return jnp.dot(a, b, preferred_element_type=F32)


def amplitude_kernel(amp_ref, pick_ref, out_ref, sorted_ref):
    rows = amp_ref[...]
    high = rows.astype(BF16)
    rest = rows - high.astype(F32)
    middle = rest.astype(BF16)
    low = (rest - middle.astype(F32)).astype(BF16)
    for c in range(4):
        pick = pick_ref[:, c * Q : (c + 1) * Q]
        sorted_ref[c] = (dot(high, pick) + dot(middle, pick)) + dot(low, pick)
    for c in range(4):
        for r in range(4):
            out_ref[r * Q : (r + 1) * Q, c * Q : (c + 1) * Q] = sorted_ref[c, pl.ds(r, Q, stride=4), :]


def amplitude_parts(amp):
    source = np.arange(W)
    pick = np.zeros((W, W), ml_dtypes.bfloat16)
    pick[source, (source % 4) * Q + source // 4] = 1
    return pl.pallas_call(
        amplitude_kernel,
        out_shape=jax.ShapeDtypeStruct((W, W), F32),
        scratch_shapes=[pltpu.VMEM((4, W, Q), F32)],
        compiler_params=pltpu.CompilerParams(vmem_limit_bytes=16 * MIB),
        cost_estimate=pl.CostEstimate(flops=6 * W**3, bytes_accessed=3 * MIB, transcendentals=0),
        name="amplitude_parts",
    )(amp, jnp.asarray(pick))


def columns_kernel(start_ref, tile_ref, right_ref, out_ref):
    start = start_ref[0]
    first = start // 128
    shift = start % 128
    back = (128 - shift) % 128
    lane = lax.broadcasted_iota(jnp.int32, (32, 128), 1)
    keep = lane < 128 - shift

    def rows_step(step, carry):
        rows = pl.ds(pl.multiple_of(step * 32, 32), 32)
        for part in range(2):
            turned = []
            for k in range(5):
                block = first + k
                in_tile = pl.ds(pl.multiple_of(jnp.minimum(block, 7) * 128, 128), 128)
                in_right = pl.ds(pl.multiple_of(jnp.clip(block - 8, 0, 3) * 128, 128), 128)
                a = tile_ref[part, rows, in_tile].astype(F32)
                b = right_ref[part, rows, in_right].astype(F32)
                turned.append(pltpu.roll(jnp.where(block < 8, a, b), back, 1))
            for k in range(4):
                value = jnp.where(keep, turned[k], turned[k + 1])
                out_ref[part, rows, k * 128 : (k + 1) * 128] = value.astype(BF16)
        return carry

    lax.fori_loop(0, tile_ref.shape[1] // 32, rows_step, 0)


def window_columns(start, tile, right, name):
    rows = tile.shape[1]
    vmem = pl.BlockSpec(memory_space=pltpu.VMEM)
    return pl.pallas_call(
        columns_kernel,
        out_shape=jax.ShapeDtypeStruct((2, rows, W), BF16),
        in_specs=[pl.BlockSpec(memory_space=pltpu.SMEM), vmem, vmem],
        out_specs=vmem,
        compiler_params=pltpu.CompilerParams(vmem_limit_bytes=16 * MIB),
        cost_estimate=pl.CostEstimate(flops=4 * MIB, bytes_accessed=4 * MIB, transcendentals=0),
        name=name,
    )(start, tile, right)


def wave_kernel(
    info_ref, own_ref, below_ref, probe_ref, amp_ref, lf_ref, rf_ref, la_ref, ra_ref,
    up_ref, low_ref, send_ref, keep_ref,
    tall, patch, folded, mid, far, wide,
):
    row_start = info_ref[0]
    first_mode = info_ref[1]
    live = info_ref[2].astype(F32)

    def loop(count, body, unroll=1):
        lax.fori_loop(0, count, lambda i, c: (body(i), c)[1], 0, unroll=unroll)

    def rows16(step, base=0):
        return pl.ds(pl.multiple_of(base + step * 16, 16), 16)

    lane_blocks = [(part, k, slice(k * 128, (k + 1) * 128)) for part in range(2) for k in range(4)]

    def stack_rows(step):
        rows = rows16(step)
        for part, k, lanes in lane_blocks:
            tall[part, k, rows, :] = own_ref[part, rows, lanes].astype(F32)
            tall[part, k, rows16(step, W), :] = below_ref[part, rows, lanes].astype(F32)

    loop(W // 16, stack_rows)

    def take_rows(step):
        for part, k, lanes in lane_blocks:
            patch[part, rows16(step), lanes] = tall[part, k, pl.ds(row_start + step * 16, 16), :]

    loop(W // 16, take_rows)

    def forward(m):
        mode = lax.rem(m + first_mode, 4)

        def exit_fold(step):
            for lanes in (slice(0, 128), slice(128, 256), slice(256, 384), slice(384, 512)):
                parts = []
                for q in range(4):
                    rows = rows16(step, q * Q)
                    pr = probe_ref[mode, 0, rows, lanes].astype(F32)
                    pi = probe_ref[mode, 1, rows, lanes].astype(F32)
                    xr, xi = patch[0, rows, lanes], patch[1, rows, lanes]
                    er = (pr * xr - pi * xi).astype(BF16).astype(F32)
                    ei = (pr * xi + pi * xr).astype(BF16).astype(F32)
                    parts.append((er, ei))
                for r, (zr, zi) in enumerate(fold(parts, 1)):
                    folded[r, rows16(step), lanes] = zr.astype(BF16)
                    folded[r, rows16(step, Q), lanes] = zi.astype(BF16)

        loop(Q // 16, exit_fold)
        for r in range(4):
            mid[r] = dot(lf_ref[r], folded[r])

        def column_fold(step):
            for r in range(4):
                parts = []
                for q in range(4):
                    lanes = slice(q * 128, (q + 1) * 128)
                    yr = mid[r, rows16(step), lanes].astype(BF16).astype(F32)
                    yi = mid[r, rows16(step, Q), lanes].astype(BF16).astype(F32)
                    parts.append((yr, yi))
                for c, (wr, wi) in enumerate(fold(parts, 1)):
                    wide[c, rows16(step, r * Q), 0:128] = wr.astype(BF16)
                    wide[c, rows16(step, r * Q), 128:256] = wi.astype(BF16)

        loop(Q // 16, column_fold)
        for c in range(4):
            far[m, :, c * 256 : (c + 1) * 256] = dot(wide[c], rf_ref[c])

    loop(4, forward)

    def residual(step):
        rows = rows16(step)
        for c in range(4):
            re, im = slice(c * 256, c * 256 + 128), slice(c * 256 + 128, c * 256 + 256)
            lanes = slice(c * 128, (c + 1) * 128)
            fields = [(far[m, rows, re], far[m, rows, im]) for m in range(4)]
            intensity = sum(fr * fr + fi * fi for fr, fi in fields)
            modulus = jnp.sqrt(jnp.maximum(intensity, 0.25))
            ratio = live * (1.0 - amp_ref[rows, lanes] / modulus)
            for m, (fr, fi) in enumerate(fields):
                far[m, rows, re] = fr * ratio
                far[m, rows, im] = fi * ratio

    loop(W // 16, residual)

    up_ref[...] = jnp.zeros_like(up_ref)

    def adjoint(m, out_ref, slot):
        mode = lax.rem(m + first_mode, 4)

        def pack(step):
            for r in range(4):
                for c in range(4):
                    rows = rows16(step, r * Q)
                    lanes = slice(c * 128, (c + 1) * 128)
                    folded[r, rows16(step), lanes] = far[m, rows, c * 256 : c * 256 + 128].astype(BF16)
                    folded[r, rows16(step, Q), lanes] = far[m, rows, c * 256 + 128 : c * 256 + 256].astype(BF16)

        loop(Q // 16, pack)
        for r in range(4):
            mid[r] = dot(la_ref[r], folded[r])

        def row_unfold(step):
            for c in range(4):
                lanes = slice(c * 128, (c + 1) * 128)
                parts = [(mid[r, rows16(step), lanes], mid[r, rows16(step, Q), lanes]) for r in range(4)]
                for q, (yr, yi) in enumerate(fold(parts, -1)):
                    wide[c, rows16(step, q * Q), 0:128] = yr.astype(BF16)
                    wide[c, rows16(step, q * Q), 128:256] = yi.astype(BF16)

        loop(Q // 16, row_unfold)
        for c in range(4):
            far[m, :, c * 256 : (c + 1) * 256] = dot(wide[c], ra_ref[c])

        def terms(step):
            rows = rows16(step)
            parts = [
                (far[m, rows, c * 256 : c * 256 + 128], far[m, rows, c * 256 + 128 : c * 256 + 256])
                for c in range(4)
            ]
            for q, (gr, gi) in enumerate(fold(parts, -1)):
                lanes = slice(q * 128, (q + 1) * 128)
                pr = probe_ref[mode, 0, rows, lanes].astype(F32)
                pi = probe_ref[mode, 1, rows, lanes].astype(F32)
                up_ref[0, rows, lanes] += pr * gr + pi * gi
                up_ref[1, rows, lanes] += pr * gi - pi * gr
                xr, xi = patch[0, rows, lanes], patch[1, rows, lanes]
                out_ref[slot, 0, rows, lanes] = (xr * gr + xi * gi).astype(out_ref.dtype)
                out_ref[slot, 1, rows, lanes] = (xr * gi - xi * gr).astype(out_ref.dtype)

        loop(W // 16, terms)

    loop(2, lambda m: adjoint(m, send_ref, m))
    loop(2, lambda m: adjoint(m + 2, keep_ref, m))

    def clear(step):
        for part, k, lanes in lane_blocks:
            tall[part, k, rows16(step), :] = jnp.zeros((16, 128), F32)
            tall[part, k, rows16(step, W), :] = jnp.zeros((16, 128), F32)

    loop(W // 16, clear)

    def put_rows(step):
        for part, k, lanes in lane_blocks:
            tall[part, k, pl.ds(row_start + step * 16, 16), :] = up_ref[part, rows16(step), lanes]

    loop(W // 16, put_rows)

    def split_rows(step):
        rows = rows16(step)
        for part, k, lanes in lane_blocks:
            up_ref[part, rows, lanes] = tall[part, k, rows, :]
            low_ref[part, rows, lanes] = tall[part, k, rows16(step, W), :].astype(BF16)

    loop(W // 16, split_rows)


def wave(info, own, below, probe, amp):
    tables = [jnp.asarray(t) for t in block_tables()]
    vmem = pl.BlockSpec(memory_space=pltpu.VMEM)
    return pl.pallas_call(
        wave_kernel,
        out_shape=(
            jax.ShapeDtypeStruct((2, W, W), F32),
            jax.ShapeDtypeStruct((2, W, W), BF16),
            jax.ShapeDtypeStruct((2, 2, W, W), BF16),
            jax.ShapeDtypeStruct((2, 2, W, W), F32),
        ),
        in_specs=[pl.BlockSpec(memory_space=pltpu.SMEM)] + [vmem] * 8,
        out_specs=(vmem,) * 4,
        scratch_shapes=[
            pltpu.VMEM((2, 4, 2 * W, 128), F32),
            pltpu.VMEM((2, W, W), F32),
            pltpu.VMEM((4, 256, W), BF16),
            pltpu.VMEM((4, 256, W), F32),
            pltpu.VMEM((4, W, 1024), F32),
            pltpu.VMEM((4, W, 256), BF16),
        ],
        compiler_params=pltpu.CompilerParams(vmem_limit_bytes=52 * MIB),
        cost_estimate=pl.CostEstimate(flops=20 * 10**9, bytes_accessed=20 * MIB, transcendentals=W * W),
        name="wave",
    )(info, own, below, probe, amp, *tables)


def merge_kernel(starts_ref, own_ref, above_ref, out_ref, over_ref, strip):
    lane = lax.broadcasted_iota(jnp.int32, (32, 128), 1)
    zero = jnp.zeros((32, 128), F32)

    def rows_step(step, carry):
        rows = pl.ds(pl.multiple_of(step * 32, 32), 32)
        for part in range(2):
            for k in range(12):
                strip[:, k * 128 : (k + 1) * 128] = zero
            for source, ref in enumerate((own_ref, above_ref)):
                start = starts_ref[source]
                first, shift = start // 128, start % 128
                early = lane < shift
                before = zero
                for k in range(5):
                    if k < 4:
                        value = ref[part, rows, k * 128 : (k + 1) * 128].astype(F32)
                        turned = pltpu.roll(value, shift, 1)
                    else:
                        turned = zero
                    lanes = pl.ds(pl.multiple_of((first + k) * 128, 128), 128)
                    strip[:, lanes] += jnp.where(early, before, turned)
                    before = turned
            out_ref[part, rows, :] = strip[:, :1024]
            over_ref[part, rows, :] = strip[:, 1024:].astype(BF16)
        return carry

    lax.fori_loop(0, own_ref.shape[1] // 32, rows_step, 0)


def merge(starts, own, above):
    vmem = pl.BlockSpec(memory_space=pltpu.VMEM)
    return pl.pallas_call(
        merge_kernel,
        out_shape=(jax.ShapeDtypeStruct((2, W, 1024), F32), jax.ShapeDtypeStruct((2, W, W), BF16)),
        in_specs=[pl.BlockSpec(memory_space=pltpu.SMEM), vmem, vmem],
        out_specs=(vmem, vmem),
        scratch_shapes=[pltpu.VMEM((32, 1536), F32)],
        compiler_params=pltpu.CompilerParams(vmem_limit_bytes=24 * MIB),
        cost_estimate=pl.CostEstimate(flops=8 * MIB, bytes_accessed=8 * MIB, transcendentals=0),
        name="merge",
    )(starts, own, above)


def add_left_kernel(tile_ref, got_ref, out_ref):
    out_ref[...] = tile_ref[...] + got_ref[...].astype(F32)


def add_left(tile, got):
    spec = pl.BlockSpec((2, 128, W), lambda i: (0, i, 0))
    return pl.pallas_call(
        add_left_kernel,
        grid=(4,),
        out_shape=jax.ShapeDtypeStruct(tile.shape, F32),
        in_specs=[spec, spec],
        out_specs=spec,
        input_output_aliases={0: 0},
        compiler_params=pltpu.CompilerParams(vmem_limit_bytes=16 * MIB),
        cost_estimate=pl.CostEstimate(flops=MIB, bytes_accessed=5 * MIB, transcendentals=0),
        name="add_left",
    )(tile, got)


def place_of(index):
    row, col = divmod(index, 16)
    return [col // 2 % 4, row // 2, row % 2 * 2 + col // 8, col % 2]


def index_of(x, y, z, core):
    x, y, z, core = x % 4, y % 4, z % 4, core % 2
    return (y * 2 + z // 2) * 16 + (z % 2 * 4 + x) * 2 + core


def moved(value, axis, distance):
    route = []
    for index in range(128):
        place = place_of(index)
        place[axis] += distance
        route.append((index, index_of(*place)))
    return lax.ppermute(value, AXES, route)


def ring_sum(value, axis, here):
    total = lax.dynamic_index_in_dim(value, here, 0, keepdims=False).astype(F32)
    for distance in (2, 1, 3):
        block = lax.dynamic_index_in_dim(value, (here + distance) % 4, 0, keepdims=False)
        total = total + moved(block.astype(BF16), axis, distance).astype(F32)
    return total


def quarters(value):
    shape = value.shape
    return jnp.moveaxis(value.reshape(shape[0], shape[1], 4, shape[2] // 4, shape[3]), 2, 0)


def probe_sum(send, keep, row, col):
    x, y, z, core = col // 2 % 4, row // 2, row % 2 * 2 + col // 8, col % 2
    total = keep + moved(send, 3, 1).astype(F32)
    total = ring_sum(quarters(total), 1, y)
    total = ring_sum(quarters(total), 2, z)
    total = ring_sum(quarters(total), 0, x)
    mine = lax.dynamic_slice_in_dim(total, core * 4, 4, 2)
    other = moved(lax.dynamic_slice_in_dim(total, (1 - core) * 4, 4, 2), 3, 1)
    even = core == 0
    return jnp.concatenate([jnp.where(even, mine, other), jnp.where(even, other, mine)], axis=0)


def per_device(object_field, probe_modes, positions, amplitudes, live_slots):
    row, col = lax.axis_index("row"), lax.axis_index("col")
    tile_rows, tile_cols = object_field.shape[1:]
    upper = lax.ppermute(positions, "row", [(i, i + 1) for i in range(7)])
    right = lax.ppermute(object_field[:, :, :W], "col", [(i + 1, i) for i in range(15)])
    own_start = positions[0, 1] - col * tile_cols
    upper_start = jnp.clip(upper[0, 1] - col * tile_cols, 0, tile_cols - 1)
    row_start = positions[0, 0] - row * tile_rows
    chosen = window_columns(upper_start[None], object_field, right, "upper_columns")
    below = lax.ppermute(chosen, "row", [(i + 1, i) for i in range(7)])
    own = window_columns(own_start[None], object_field, right, "own_columns")
    amp = amplitude_parts(amplitudes[0])
    info = jnp.stack([row_start, 2 * (1 - col % 2), live_slots[0]]).astype(jnp.int32)
    up, low, send, keep = wave(info, own, below, probe_modes, amp)
    above = lax.ppermute(low, "row", [(i, i + 1) for i in range(7)])
    probe_grad = probe_sum(send, keep, row, col)
    tile, over = merge(jnp.stack([own_start, upper_start]), up, above)
    from_left = lax.ppermute(over, "col", [(i, i + 1) for i in range(15)])
    return add_left(tile, from_left), probe_grad


def solution(mesh):
    placed = (
        P(None, "row", "col"),
        P(),
        P(("row", "col"), None),
        P(("row", "col"), None, None),
        P(("row", "col")),
    )
    return jax.shard_map(
        per_device,
        mesh=mesh,
        in_specs=placed,
        out_specs=(P(None, "row", "col"), P(None, None, ("row", "col"), None)),
        check_vma=False,
    )
```

time: 551 us -> 163 us (0.30)
  the two profiles are of different devices: /device:TPU:1 before, /device:TPU:11 now
where the time goes in v1:
time: 163 us; the launch traced here: 162 us
  starting transfers between devices  55.3 us (34%)
  Pallas kernels  43.3 us (27%)
  waiting for transfers between devices  42.7 us (26%)
  local copies, waits for them, and re-layouts  12 us (7%)
  other arithmetic  5.78 us (4%)
  between operations  3.35 us (2%)
    ppermute x11, starting transfers between devices, moved(): return lax.ppermute(value, AXES, route)  31 us
    pallas_call x1, Pallas kernels, wave(): pl.pallas_call(wave_kernel, out_shape=(jax.ShapeDtypeStruct((2, W, W), F3...  26.8 us
    ppermute x1, waiting for transfers between devices, per_device(): above = lax.ppermute(low, 'row', [(i, i + 1) for i in range(7)])  13.6 us
    ppermute x1, waiting for transfers between devices, per_device(): below = lax.ppermute(chosen, 'row', [(i + 1, i) for i in range(7)])  13.3 us
    ppermute x11, waiting for transfers between devices, moved(): return lax.ppermute(value, AXES, route)  8.69 us
    unnamed x22, local copies, waits for them, and re-layouts  7.07 us
    pallas_call x1, Pallas kernels, merge(): pl.pallas_call(merge_kernel, out_shape=(jax.ShapeDtypeStruct((2, W, 1024)...  6.27 us
    ppermute x1, starting transfers between devices, per_device(): above = lax.ppermute(low, 'row', [(i, i + 1) for i in range(7)])  6.06 us
  transfers between devices with their start and end apart: 16, of which 8 were waited for; matrix products, arithmetic and copies ran while one was open for 5% of the time, Pallas kernels for 8%

profile of v1, /device:TPU:11, one launch (start us, length us, event | category | flops | bytes accessed | tf_op | source)
XLA Modules:
  0.0 162.3 jit_solution(17883189376082586382)
XLA Ops:
  0.6 0.0 copy-start.1
  0.6 0.0 copy-start.10
  0.7 2.4 %slice.15 = bf16[2,512,512]{2,1,0:T(8,128)(2,1)} slice(bf16[2,512,1024]{2,1,0:T(8,128)(2,1)} %tile_ref.3), slice={[0:2], [0:512], [0:512]} | slice | bytes 2097152 | tf_op jit(solution)/shard_map/slice | solution.py:422
  3.1 2.6 %collective-permute-start.1 = (bf16[2,512,512]{2,1,0:T(8,128)(2,1)}, bf16[2,512,512]{2,1,0:T(8,128)(2,1)S(1)}, u32[]{:S(2)}, u32[]{:S(2)}) collective-permute-start(bf16[2,512,512]{2,1,0:T(8,128)(2,1)} %slice.15), channel_id=1, source_target_pairs={{1,0},{2,1},{3,2},{4,3},{5,4},{6,5},{7,6},{8,7},{9,8},{10,9},{11,1... | collective-permute-start | bytes 3145736 | tf_op jit(solution)/shard_map/ppermute | solution.py:422
  5.6 5.5 %collective-permute-start = (s32[1,2]{1,0:T(1,128)}, s32[1,2]{1,0:T(1,128)S(1)}, u32[]{:S(2)}, u32[]{:S(2)}) collective-permute-start(s32[1,2]{1,0:T(1,128)} %param.12), channel_id=1, source_target_pairs={{0,16},{16,32},{32,48},{48,64},{64,80},{80,96},{96,112},{1,17},{17... | collective-permute-start | bytes 32 | tf_op jit(solution)/shard_map/ppermute | solution.py:421
  11.2 1.3 collective-permute-done
  12.5 0.6 slice.13
  13.7 5.7 %collective-permute-done.1.right_ref = bf16[2,512,512]{2,1,0:T(8,128)(2,1)S(1)} collective-permute-done((bf16[2,512,512]{2,1,0:T(8,128)(2,1)}, bf16[2,512,512]{2,1,0:T(8,128)(2,1)S(1)}, u32[]{:S(2)}, u32[]{:S(2)}) %collective-permute-start.1) | collective-permute-done | bytes 1048608 | tf_op jit(solution)/shard_map/ppermute | solution.py:422
  19.4 1.6 copy-done
  21.0 2.8 %upper_columns.1 = bf16[2,512,512]{2,1,0:T(8,128)(2,1)} custom-call(s32[1]{0:T(128)} %bitcast.3.start_ref, bf16[2,512,1024]{2,1,0:T(8,128)(2,1)S(1)} %copy-done, bf16[2,512,512]{2,1,0:T(8,128)(2,1)S(1)} %collective-permute-done.1.right_ref), custom_call_target="tpu_custom_call" | custom-call | flops 4194304 | bytes 4194304 | tf_op jit(solution)/shard_map/upper_columns/pallas_call | solution.py:115
  23.8 5.4 %collective-permute-start.2 = (bf16[2,512,512]{2,1,0:T(8,128)(2,1)}, bf16[2,512,512]{2,1,0:T(8,128)(2,1)}, u32[]{:S(2)}, u32[]{:S(2)}) collective-permute-start(bf16[2,512,512]{2,1,0:T(8,128)(2,1)} %upper_columns.1), channel_id=1, source_target_pairs={{16,0},{32,16},{48,32},{64,48},{80,64},{96,80},{112,96},{17,1},{33... | collective-permute-start | bytes 3145736 | tf_op jit(solution)/shard_map/ppermute | solution.py:427
  29.9 0.6 fusion.16
  31.6 0.0 copy-start.4
  31.6 1.2 copy-done.4
  32.8 1.0 copy-done.7
  33.9 1.8 %amplitude_parts.1.amp_ref = f32[512,512]{1,0:T(8,128)S(1)} custom-call(f32[512,512]{1,0:T(8,128)S(1)} %bitcast.78, bf16[512,512]{1,0:T(8,128)(2,1)S(1)} %copy-done.7), custom_call_target="tpu_custom_call" | custom-call | flops 805306368 | bytes 3145728 | tf_op jit(solution)/shard_map/amplitude_parts/pallas_call | solution.py:75
  35.8 0.1 pad_add_fusion.1.info_ref
  35.8 1.8 %own_columns.1.own_ref = bf16[2,512,512]{2,1,0:T(8,128)(2,1)S(1)} custom-call(s32[1]{0:T(128)} %bitcast.1.start_ref, bf16[2,512,1024]{2,1,0:T(8,128)(2,1)S(1)} %copy-done.1, bf16[2,512,512]{2,1,0:T(8,128)(2,1)S(1)} %collective-permute-done.1.right_ref), custom_call_target="tpu_custom_call" | custom-call | flops 4194304 | bytes 4194304 | tf_op jit(solution)/shard_map/own_columns/pallas_call | solution.py:115
  37.7 1.1 copy-done.3
  38.7 13.3 %collective-permute-done.2.below_ref = bf16[2,512,512]{2,1,0:T(8,128)(2,1)} collective-permute-done((bf16[2,512,512]{2,1,0:T(8,128)(2,1)}, bf16[2,512,512]{2,1,0:T(8,128)(2,1)}, u32[]{:S(2)}, u32[]{:S(2)}) %collective-permute-start.2) | collective-permute-done | bytes 1048608 | tf_op jit(solution)/shard_map/ppermute | solution.py:427
  52.1 26.8 %wave.1 = (f32[2,512,512]{2,1,0:T(8,128)}, bf16[2,512,512]{2,1,0:T(8,128)(2,1)}, bf16[2,2,512,512]{3,2,1,0:T(8,128)(2,1)}, f32[2,2,512,512]{3,2,1,0:T(8,128)}) custom-call(s32[3]{0:T(128)S(1)} %pad_add_fusion.1.info_ref, bf16[2,512,512]{2,1,0:T(8,128)(2,1)} %copy-done.3, bf16[2,512,512]{2,1,0:T(8,128)(2,1)} %collective-permute-done.2.below_ref, ...), custom_call_target="tpu_custom_call" | custom-call | flops 20000000000 | bytes 20971520 | tf_op jit(solution)/shard_map/wave/pallas_call | solution.py:287
  78.9 0.0 collective-permute-start.5
  78.9 6.1 %collective-permute-start.3 = (bf16[2,512,512]{2,1,0:T(8,128)(2,1)}, bf16[2,512,512]{2,1,0:T(8,128)(2,1)S(1)}, u32[]{:S(2)}, u32[]{:S(2)}) collective-permute-start(bf16[2,512,512]{2,1,0:T(8,128)(2,1)} %get-tuple-element.9), channel_id=1, source_target_pairs={{0,16},{16,32},{32,48},{48,64},{64,80},{80,96},{96,112},{1,17},{17... | collective-permute-start | bytes 3145736 | tf_op jit(solution)/shard_map/ppermute | solution.py:432
  84.9 2.9 %convert_add_fusion = f32[2,2,512,512]{3,2,1,0:T(8,128)S(1)} fusion(f32[2,2,512,512]{3,2,1,0:T(8,128)} %get-tuple-element.12, bf16[2,2,512,512]{3,2,1,0:T(8,128)(2,1)S(1)} %collective-permute-done.5), kind=kLoop, calls=%fused_computation | loop fusion | flops 2097152 | bytes 10485760 | tf_op jit(solution)/shard_map/add | solution.py:408
  87.9 2.1 %copy-done.9 = f32[2,2,512,512]{3,2,1,0:T(8,128)} copy-done((f32[2,2,512,512]{3,2,1,0:T(8,128)}, f32[2,2,512,512]{3,2,1,0:T(8,128)S(1)}, u32[]{:S(2)}) %copy-start.9) | copy-done | bytes 4194328
  90.0 1.2 fusion.2
  91.2 0.3 collective-permute-start.6
  91.5 1.1 collective-permute-start.7
  92.6 1.7 %collective-permute-start.8 = (bf16[2,2,128,512]{3,2,1,0:T(8,128)(2,1)}, bf16[2,2,128,512]{3,2,1,0:T(8,128)(2,1)}, u32[]{:S(2)}, u32[]{:S(2)}) collective-permute-start(bf16[2,2,128,512]{3,2,1,0:T(8,128)(2,1)} %get-tuple-element.16), channel_id=1, source_target_pairs={{0,96},{1,97},{2,98},{3,99},{4,100},{5,101},{6,102},{7,103},{8,104... | collective-permute-start | bytes 1572872 | tf_op jit(solution)/shard_map/ppermute | solution.py:390
  94.3 0.1 pad_add_fusion.starts_ref
  94.4 13.6 %collective-permute-done.3.above_ref = bf16[2,512,512]{2,1,0:T(8,128)(2,1)S(1)} collective-permute-done((bf16[2,512,512]{2,1,0:T(8,128)(2,1)}, bf16[2,512,512]{2,1,0:T(8,128)(2,1)S(1)}, u32[]{:S(2)}, u32[]{:S(2)}) %collective-permute-start.3) | collective-permute-done | bytes 1048608 | tf_op jit(solution)/shard_map/ppermute | solution.py:432
  108.0 6.3 %merge.1 = (f32[2,512,1024]{2,1,0:T(8,128)}, bf16[2,512,512]{2,1,0:T(8,128)(2,1)}) custom-call(s32[2]{0:T(128)S(1)} %pad_add_fusion.starts_ref, f32[2,512,512]{2,1,0:T(8,128)S(1)} %copy-done.2, bf16[2,512,512]{2,1,0:T(8,128)(2,1)S(1)} %collective-permute-done.3.above_ref), custom_call_target="tpu_custom_call" | custom-call | flops 8388608 | bytes 8388608 | tf_op jit(solution)/shard_map/merge/pallas_call | solution.py:343
  114.3 4.8 %collective-permute-start.4 = (bf16[2,512,512]{2,1,0:T(8,128)(2,1)}, bf16[2,512,512]{2,1,0:T(8,128)(2,1)S(1)}, u32[]{:S(2)}, u32[]{:S(2)}) collective-permute-start(bf16[2,512,512]{2,1,0:T(8,128)(2,1)} %get-tuple-element.11), channel_id=1, source_target_pairs={{0,1},{1,2},{2,3},{3,4},{4,5},{5,6},{6,7},{7,8},{8,9},{9,10},{10,1... | collective-permute-start | bytes 3145736 | tf_op jit(solution)/shard_map/ppermute | solution.py:435
  119.1 2.0 %fusion.1 = f32[2,2,128,512]{3,2,1,0:T(8,128)S(1)} fusion(bf16[2,2,128,512]{3,2,1,0:T(8,128)(2,1)} %collective-permute-done.8, bf16[2,2,128,512]{3,2,1,0:T(8,128)(2,1)} %collective-permute-done.7, bf16[2,2,128,512]{3,2,1,0:T(8,128)(2,1)} %collective-permute-done.6, f32[2,2,4,128,512]{4,3,2,1,0:T(8,128)} %bitcast.80, s32[]{:T(128)S(6)} %select_n.123), kind=kLoop, calls=%fused_computation.6 | loop fusion | flops 1572864 | bytes 3670020 | tf_op jit(solution)/shard_map/add | solution.py:397
  121.1 0.1 fusion.9
  121.1 1.4 collective-permute-start.10
  122.6 10.9 %collective-permute-start.11 = (bf16[2,2,32,512]{3,2,1,0:T(8,128)(2,1)S(1)}, bf16[2,2,32,512]{3,2,1,0:T(8,128)(2,1)S(1)}, u32[]{:S(2)}, u32[]{:S(2)}) collective-permute-start(bf16[2,2,32,512]{3,2,1,0:T(8,128)(2,1)S(1)} %get-tuple-element.18), channel_id=1, source_target_pairs={{0,24},{1,25},{2,26},{3,27},{4,28},{5,29},{6,30},{7,31},{8,0},{9,1... | collective-permute-start | bytes 393224 | tf_op jit(solution)/shard_map/ppermute | solution.py:390
  133.4 1.1 collective-permute-start.9
  134.5 1.2 collective-permute-done.10
  135.7 4.7 %collective-permute-done.9 = bf16[2,2,32,512]{3,2,1,0:T(8,128)(2,1)S(1)} collective-permute-done((bf16[2,2,32,512]{3,2,1,0:T(8,128)(2,1)S(1)}, bf16[2,2,32,512]{3,2,1,0:T(8,128)(2,1)S(1)}, u32[]{:S(2)}, u32[]{:S(2)}) %collective-permute-start.9) | collective-permute-done | bytes 131104 | tf_op jit(solution)/shard_map/ppermute | solution.py:390
  140.5 0.1 fusion.7
  140.6 0.2 collective-permute-start.12
  140.7 12.0 %collective-permute-start.13 = (bf16[2,2,8,512]{3,2,1,0:T(8,128)(2,1)S(1)}, bf16[2,2,8,512]{3,2,1,0:T(8,128)(2,1)S(1)}, u32[]{:S(2)}, u32[]{:S(2)}) collective-permute-start(bf16[2,2,8,512]{3,2,1,0:T(8,128)(2,1)S(1)} %get-tuple-element.22), channel_id=1, source_target_pairs={{0,2},{1,3},{2,4},{3,5},{4,6},{5,7},{6,0},{7,1},{8,10},{9,11},{10,... | collective-permute-start | bytes 98312 | tf_op jit(solution)/shard_map/ppermute | solution.py:390
  152.8 1.0 collective-permute-done.13
  153.8 1.7 %collective-permute-done.14 = bf16[2,2,8,512]{3,2,1,0:T(8,128)(2,1)S(1)} collective-permute-done((bf16[2,2,8,512]{3,2,1,0:T(8,128)(2,1)S(1)}, bf16[2,2,8,512]{3,2,1,0:T(8,128)(2,1)S(1)}, u32[]{:S(2)}, u32[]{:S(2)}) %collective-permute-start.14) | collective-permute-done | bytes 32800 | tf_op jit(solution)/shard_map/ppermute | solution.py:390
  155.6 2.3 %collective-permute-start.15 = (f32[2,2,4,512]{3,2,1,0:T(4,128)S(1)}, f32[2,2,4,512]{3,2,1,0:T(4,128)S(1)}, u32[]{:S(2)}, u32[]{:S(2)}) collective-permute-start(f32[2,2,4,512]{3,2,1,0:T(4,128)S(1)} %constant_dynamic-slice_fusion), channel_id=1, source_target_pairs={{0,1},{1,0},{2,3},{3,2},{4,5},{5,4},{6,7},{7,6},{8,9},{9,8},{10,11... | collective-permute-start | bytes 98312 | tf_op jit(solution)/shard_map/ppermute | solution.py:390
  157.9 3.8 %add_left.1 = f32[2,512,1024]{2,1,0:T(8,128)} custom-call(f32[2,512,1024]{2,1,0:T(8,128)} %get-tuple-element.10.tile_ref, bf16[2,512,512]{2,1,0:T(8,128)(2,1)S(1)} %collective-permute-done.4.got_ref), custom_call_target="tpu_custom_call", output_to_operand_aliasing={{}: (0, {})} | custom-call | flops 1048576 | bytes 5242880 | tf_op jit(solution)/shard_map/add_left/pallas_call | solution.py:361
  161.7 0.6 pad_maximum_fusion
  (27 shorter events, 0.1 us)
Async XLA Ops:
  0.6 35.2 %copy-start.1 = (bf16[2,512,1024]{2,1,0:T(8,128)(2,1)S(1)}, bf16[2,512,1024]{2,1,0:T(8,128)(2,1)}, u32[]{:S(2)}) copy-start(bf16[2,512,1024]{2,1,0:T(8,128)(2,1)} %tile_ref.3) | copy-start | bytes 6291460
  0.6 29.2 %copy-start.10 = (s32[1,2]{1,0:T(1,128)S(1)}, s32[1,2]{1,0:T(1,128)}, u32[]{:S(2)}) copy-start(s32[1,2]{1,0:T(1,128)} %param.12) | copy-start | bytes 28
  3.1 16.4 %collective-permute-start.1 = (bf16[2,512,512]{2,1,0:T(8,128)(2,1)}, bf16[2,512,512]{2,1,0:T(8,128)(2,1)S(1)}, u32[]{:S(2)}, u32[]{:S(2)}) collective-permute-start(bf16[2,512,512]{2,1,0:T(8,128)(2,1)} %slice.15), channel_id=1, source_target_pairs={{1,0},{2,1},{3,2},{4,3},{5,4},{6,5},{7,6},{8,7},{9,8},{10,9},{11,1... | collective-permute-start | bytes 3145736 | tf_op jit(solution)/shard_map/ppermute | solution.py:422
  5.6 6.8 %collective-permute-start = (s32[1,2]{1,0:T(1,128)}, s32[1,2]{1,0:T(1,128)S(1)}, u32[]{:S(2)}, u32[]{:S(2)}) collective-permute-start(s32[1,2]{1,0:T(1,128)} %param.12), channel_id=1, source_target_pairs={{0,16},{16,32},{32,48},{48,64},{64,80},{80,96},{96,112},{1,17},{17... | collective-permute-start | bytes 32 | tf_op jit(solution)/shard_map/ppermute | solution.py:421
  19.4 1.6 copy-start
  23.8 28.3 %collective-permute-start.2 = (bf16[2,512,512]{2,1,0:T(8,128)(2,1)}, bf16[2,512,512]{2,1,0:T(8,128)(2,1)}, u32[]{:S(2)}, u32[]{:S(2)}) collective-permute-start(bf16[2,512,512]{2,1,0:T(8,128)(2,1)} %upper_columns.1), channel_id=1, source_target_pairs={{16,0},{32,16},{48,32},{64,48},{80,64},{96,80},{112,96},{17,1},{33... | collective-permute-start | bytes 3145736 | tf_op jit(solution)/shard_map/ppermute | solution.py:427
  31.6 1.2 copy-start.4
  32.8 1.0 copy-start.7
  33.9 18.2 %copy-start.5 = (bf16[4,256,256]{2,1,0:T(8,128)(2,1)S(1)}, bf16[4,256,256]{2,1,0:T(8,128)(2,1)}, u32[]{:S(2)}) copy-start(bf16[4,256,256]{2,1,0:T(8,128)(2,1)} %constant.149.clone.lf_ref.ra_ref) | copy-start | bytes 1572868
  33.9 18.2 %copy-start.6 = (bf16[4,256,256]{2,1,0:T(8,128)(2,1)S(1)}, bf16[4,256,256]{2,1,0:T(8,128)(2,1)}, u32[]{:S(2)}) copy-start(bf16[4,256,256]{2,1,0:T(8,128)(2,1)} %constant.150.clone.rf_ref.la_ref) | copy-start | bytes 1572868
  35.7 16.3 %copy-start.8 = (f32[512,512]{1,0:T(8,128)}, f32[512,512]{1,0:T(8,128)S(1)}, u32[]{:S(2)}) copy-start(f32[512,512]{1,0:T(8,128)S(1)} %amplitude_parts.1.amp_ref) | copy-start | bytes 3145732
  37.7 1.1 copy-start.3
  78.9 6.1 %collective-permute-start.5 = (bf16[2,2,512,512]{3,2,1,0:T(8,128)(2,1)}, bf16[2,2,512,512]{3,2,1,0:T(8,128)(2,1)S(1)}, u32[]{:S(2)}, u32[]{:S(2)}) collective-permute-start(bf16[2,2,512,512]{3,2,1,0:T(8,128)(2,1)} %get-tuple-element.13), channel_id=1, source_target_pairs={{0,1},{1,0},{2,3},{3,2},{4,5},{5,4},{6,7},{7,6},{8,9},{9,8},{10,11... | collective-permute-start | bytes 6291464 | tf_op jit(solution)/shard_map/ppermute | solution.py:390
  78.9 29.2 %collective-permute-start.3 = (bf16[2,512,512]{2,1,0:T(8,128)(2,1)}, bf16[2,512,512]{2,1,0:T(8,128)(2,1)S(1)}, u32[]{:S(2)}, u32[]{:S(2)}) collective-permute-start(bf16[2,512,512]{2,1,0:T(8,128)(2,1)} %get-tuple-element.9), channel_id=1, source_target_pairs={{0,16},{16,32},{32,48},{48,64},{64,80},{80,96},{96,112},{1,17},{17... | collective-permute-start | bytes 3145736 | tf_op jit(solution)/shard_map/ppermute | solution.py:432
  87.9 2.1 %copy-start.9 = (f32[2,2,512,512]{3,2,1,0:T(8,128)}, f32[2,2,512,512]{3,2,1,0:T(8,128)S(1)}, u32[]{:S(2)}) copy-start(f32[2,2,512,512]{3,2,1,0:T(8,128)S(1)} %convert_add_fusion) | copy-start | bytes 12582916
  87.9 20.2 %copy-start.2 = (f32[2,512,512]{2,1,0:T(8,128)S(1)}, f32[2,512,512]{2,1,0:T(8,128)}, u32[]{:S(2)}) copy-start(f32[2,512,512]{2,1,0:T(8,128)} %get-tuple-element.8.own_ref) | copy-start | bytes 6291460
  91.2 27.8 %collective-permute-start.6 = (bf16[2,2,128,512]{3,2,1,0:T(8,128)(2,1)}, bf16[2,2,128,512]{3,2,1,0:T(8,128)(2,1)}, u32[]{:S(2)}, u32[]{:S(2)}) collective-permute-start(bf16[2,2,128,512]{3,2,1,0:T(8,128)(2,1)} %get-tuple-element.14), channel_id=1, source_target_pairs={{0,64},{1,65},{2,66},{3,67},{4,68},{5,69},{6,70},{7,71},{8,72},{9,... | collective-permute-start | bytes 1572872 | tf_op jit(solution)/shard_map/ppermute | solution.py:390
  91.5 27.6 %collective-permute-start.7 = (bf16[2,2,128,512]{3,2,1,0:T(8,128)(2,1)}, bf16[2,2,128,512]{3,2,1,0:T(8,128)(2,1)}, u32[]{:S(2)}, u32[]{:S(2)}) collective-permute-start(bf16[2,2,128,512]{3,2,1,0:T(8,128)(2,1)} %get-tuple-element.15), channel_id=1, source_target_pairs={{0,32},{1,33},{2,34},{3,35},{4,36},{5,37},{6,38},{7,39},{8,40},{9,... | collective-permute-start | bytes 1572872 | tf_op jit(solution)/shard_map/ppermute | solution.py:390
  92.6 26.4 %collective-permute-start.8 = (bf16[2,2,128,512]{3,2,1,0:T(8,128)(2,1)}, bf16[2,2,128,512]{3,2,1,0:T(8,128)(2,1)}, u32[]{:S(2)}, u32[]{:S(2)}) collective-permute-start(bf16[2,2,128,512]{3,2,1,0:T(8,128)(2,1)} %get-tuple-element.16), channel_id=1, source_target_pairs={{0,96},{1,97},{2,98},{3,99},{4,100},{5,101},{6,102},{7,103},{8,104... | collective-permute-start | bytes 1572872 | tf_op jit(solution)/shard_map/ppermute | solution.py:390
  114.3 43.6 %collective-permute-start.4 = (bf16[2,512,512]{2,1,0:T(8,128)(2,1)}, bf16[2,512,512]{2,1,0:T(8,128)(2,1)S(1)}, u32[]{:S(2)}, u32[]{:S(2)}) collective-permute-start(bf16[2,512,512]{2,1,0:T(8,128)(2,1)} %get-tuple-element.11), channel_id=1, source_target_pairs={{0,1},{1,2},{2,3},{3,4},{4,5},{5,6},{6,7},{7,8},{8,9},{9,10},{10,1... | collective-permute-start | bytes 3145736 | tf_op jit(solution)/shard_map/ppermute | solution.py:435
  121.1 14.6 %collective-permute-start.10 = (bf16[2,2,32,512]{3,2,1,0:T(8,128)(2,1)S(1)}, bf16[2,2,32,512]{3,2,1,0:T(8,128)(2,1)S(1)}, u32[]{:S(2)}, u32[]{:S(2)}) collective-permute-start(bf16[2,2,32,512]{3,2,1,0:T(8,128)(2,1)S(1)} %get-tuple-element.19), channel_id=1, source_target_pairs={{0,8},{1,9},{2,10},{3,11},{4,12},{5,13},{6,14},{7,15},{8,16},{9,17... | collective-permute-start | bytes 393224 | tf_op jit(solution)/shard_map/ppermute | solution.py:390
  122.6 13.2 %collective-permute-start.11 = (bf16[2,2,32,512]{3,2,1,0:T(8,128)(2,1)S(1)}, bf16[2,2,32,512]{3,2,1,0:T(8,128)(2,1)S(1)}, u32[]{:S(2)}, u32[]{:S(2)}) collective-permute-start(bf16[2,2,32,512]{3,2,1,0:T(8,128)(2,1)S(1)} %get-tuple-element.18), channel_id=1, source_target_pairs={{0,24},{1,25},{2,26},{3,27},{4,28},{5,29},{6,30},{7,31},{8,0},{9,1... | collective-permute-start | bytes 393224 | tf_op jit(solution)/shard_map/ppermute | solution.py:390
  133.4 7.0 %collective-permute-start.9 = (bf16[2,2,32,512]{3,2,1,0:T(8,128)(2,1)S(1)}, bf16[2,2,32,512]{3,2,1,0:T(8,128)(2,1)S(1)}, u32[]{:S(2)}, u32[]{:S(2)}) collective-permute-start(bf16[2,2,32,512]{3,2,1,0:T(8,128)(2,1)S(1)} %get-tuple-element.17), channel_id=1, source_target_pairs={{0,16},{1,17},{2,18},{3,19},{4,20},{5,21},{6,22},{7,23},{8,24},{9,... | collective-permute-start | bytes 393224 | tf_op jit(solution)/shard_map/ppermute | solution.py:390
  140.6 12.2 %collective-permute-start.12 = (bf16[2,2,8,512]{3,2,1,0:T(8,128)(2,1)S(1)}, bf16[2,2,8,512]{3,2,1,0:T(8,128)(2,1)S(1)}, u32[]{:S(2)}, u32[]{:S(2)}) collective-permute-start(bf16[2,2,8,512]{3,2,1,0:T(8,128)(2,1)S(1)} %get-tuple-element.20), channel_id=1, source_target_pairs={{0,4},{1,5},{2,6},{3,7},{4,0},{5,1},{6,2},{7,3},{8,12},{9,13},{10,... | collective-permute-start | bytes 98312 | tf_op jit(solution)/shard_map/ppermute | solution.py:390
  140.7 13.1 %collective-permute-start.13 = (bf16[2,2,8,512]{3,2,1,0:T(8,128)(2,1)S(1)}, bf16[2,2,8,512]{3,2,1,0:T(8,128)(2,1)S(1)}, u32[]{:S(2)}, u32[]{:S(2)}) collective-permute-start(bf16[2,2,8,512]{3,2,1,0:T(8,128)(2,1)S(1)} %get-tuple-element.22), channel_id=1, source_target_pairs={{0,2},{1,3},{2,4},{3,5},{4,6},{5,7},{6,0},{7,1},{8,10},{9,11},{10,... | collective-permute-start | bytes 98312 | tf_op jit(solution)/shard_map/ppermute | solution.py:390
  152.8 2.8 %collective-permute-start.14 = (bf16[2,2,8,512]{3,2,1,0:T(8,128)(2,1)S(1)}, bf16[2,2,8,512]{3,2,1,0:T(8,128)(2,1)S(1)}, u32[]{:S(2)}, u32[]{:S(2)}) collective-permute-start(bf16[2,2,8,512]{3,2,1,0:T(8,128)(2,1)S(1)} %get-tuple-element.21), channel_id=1, source_target_pairs={{0,6},{1,7},{2,0},{3,1},{4,2},{5,3},{6,4},{7,5},{8,14},{9,15},{10,... | collective-permute-start | bytes 98312 | tf_op jit(solution)/shard_map/ppermute | solution.py:390
  155.6 6.1 %collective-permute-start.15 = (f32[2,2,4,512]{3,2,1,0:T(4,128)S(1)}, f32[2,2,4,512]{3,2,1,0:T(4,128)S(1)}, u32[]{:S(2)}, u32[]{:S(2)}) collective-permute-start(f32[2,2,4,512]{3,2,1,0:T(4,128)S(1)} %constant_dynamic-slice_fusion), channel_id=1, source_target_pairs={{0,1},{1,0},{2,3},{3,2},{4,5},{5,4},{6,7},{7,6},{8,9},{9,8},{10,11... | collective-permute-start | bytes 98312 | tf_op jit(solution)/shard_map/ppermute | solution.py:390

commit v2 on v1

v2 whole, which is shorter than its diff:
```python
import functools
import math

import jax
import jax.numpy as jnp
import ml_dtypes
import numpy as np
from jax import lax
from jax.experimental import pallas as pl
from jax.experimental.pallas import tpu as pltpu
from jax.sharding import PartitionSpec as P

W = 512
Q = W // 4
HALF = W // 2
WEIGHT = 100 * 10**9
MIB = 1024 * 1024
F32 = jnp.float32
BF16 = jnp.bfloat16


def block_tables():
    step = np.arange(W).astype(np.float32) * np.float32(2.0 * math.pi / W)
    scale = np.float32(1.0 / math.sqrt(W))
    cos_of = (np.cos(step) * scale).astype(ml_dtypes.bfloat16).astype(np.float32)
    sin_of = (np.sin(step) * scale).astype(ml_dtypes.bfloat16).astype(np.float32)
    short = np.arange(Q)
    forward, adjoint = [], []
    for part in range(4):
        phase = np.outer(4 * short + part, short) % W
        c, s = cos_of[phase], sin_of[phase]
        forward.append(np.block([[c, s], [-s, c]]))
        adjoint.append(np.block([[c.T, -s.T], [s.T, c.T]]))
    forward = np.stack(forward).astype(ml_dtypes.bfloat16)
    adjoint = np.stack(adjoint).astype(ml_dtypes.bfloat16)
    swap = lambda t: np.ascontiguousarray(t.transpose(0, 2, 1))
    return forward, swap(forward), adjoint, swap(adjoint)


def fold(parts, sign):
    (ar, ai), (br, bi), (cr, ci), (dr, di) = parts
    pr, pi, mr, mi = ar + cr, ai + ci, ar - cr, ai - ci
    qr, qi, nr, ni = br + dr, bi + di, br - dr, bi - di
    if sign < 0:
        nr, ni = -nr, -ni
    return (
        (pr + qr, pi + qi),
        (mr + ni, mi - nr),
        (pr - qr, pi - qi),
        (mr - ni, mi + nr),
    )


def dot(a, b):
    return jnp.dot(a, b, preferred_element_type=F32)


def amplitude_kernel(amp_ref, pick_ref, out_ref, sorted_ref):
    rows = amp_ref[...]
    high = rows.astype(BF16)
    rest = rows - high.astype(F32)
    middle = rest.astype(BF16)
    low = (rest - middle.astype(F32)).astype(BF16)
    for c in range(4):
        pick = pick_ref[:, c * Q : (c + 1) * Q]
        sorted_ref[c] = (dot(high, pick) + dot(middle, pick)) + dot(low, pick)
    for c in range(4):
        for r in range(4):
            out_ref[r * Q : (r + 1) * Q, c * Q : (c + 1) * Q] = sorted_ref[c, pl.ds(r, Q, stride=4), :]


def amplitude_parts(amp):
    source = np.arange(W)
    pick = np.zeros((W, W), ml_dtypes.bfloat16)
    pick[source, (source % 4) * Q + source // 4] = 1
    return pl.pallas_call(
        amplitude_kernel,
        out_shape=jax.ShapeDtypeStruct((W, W), F32),
        scratch_shapes=[pltpu.VMEM((4, W, Q), F32)],
        compiler_params=pltpu.CompilerParams(vmem_limit_bytes=16 * MIB),
        cost_estimate=pl.CostEstimate(flops=6 * W**3, bytes_accessed=3 * MIB, transcendentals=0),
        name="amplitude_parts",
    )(amp, jnp.asarray(pick))


def lane_index(block, rows):
    return lax.broadcasted_iota(jnp.int32, (rows, 128), 1) + block * 128


def strip_block(tile_ref, right_ref, part, rows, right_rows, block, start):
    lane = lane_index(block, 16)
    lanes = slice(block * 128, block * 128 + 128)
    first = tile_ref[part, rows, lanes].astype(F32)
    second = tile_ref[part, rows, W + block * 128 : W + block * 128 + 128].astype(F32)
    beyond = right_ref[part, right_rows, lanes].astype(F32)
    return jnp.where(lane >= start, first, jnp.where(lane >= start - W, second, beyond))


def row_steps(count, size, body):
    def step_of(step, carry):
        body(pl.ds(pl.multiple_of(step * size, size), size))
        return carry

    lax.fori_loop(0, count // size, step_of, 0)


def columns_kernel(start_ref, tile_ref, right_ref, out_ref):
    def body(rows):
        for part in range(2):
            for block in range(4):
                value = strip_block(tile_ref, right_ref, part, rows, rows, block, start_ref[0])
                out_ref[part, rows, block * 128 : block * 128 + 128] = value.astype(BF16)

    row_steps(out_ref.shape[1], 16, body)


def window_columns(start, tile, right, chunk):
    rows = right.shape[1]
    whole = pl.BlockSpec((2, rows, W), lambda i: (0, 0, 0))
    return pl.pallas_call(
        columns_kernel,
        grid=(1,),
        out_shape=jax.ShapeDtypeStruct((2, rows, W), BF16),
        in_specs=[
            pl.BlockSpec(memory_space=pltpu.SMEM),
            pl.BlockSpec((2, rows, 1024), lambda i: (0, chunk, 0)),
            whole,
        ],
        out_specs=whole,
        compiler_params=pltpu.CompilerParams(vmem_limit_bytes=16 * MIB),
        cost_estimate=pl.CostEstimate(flops=WEIGHT, bytes_accessed=2 * MIB, transcendentals=0),
        name="window_columns",
    )(start, tile, right)


def copy_kernel(tile_ref, out_ref):
    out_ref[...] = tile_ref[...]


def left_columns(tile, chunk, rows):
    return pl.pallas_call(
        copy_kernel,
        grid=(1,),
        out_shape=jax.ShapeDtypeStruct((2, rows, W), BF16),
        in_specs=[pl.BlockSpec((2, rows, W), lambda i: (0, chunk, 0))],
        out_specs=pl.BlockSpec((2, rows, W), lambda i: (0, 0, 0)),
        compiler_params=pltpu.CompilerParams(vmem_limit_bytes=16 * MIB),
        cost_estimate=pl.CostEstimate(flops=0, bytes_accessed=MIB, transcendentals=0),
        name="left_columns",
    )(tile)


def wave_kernel(
    info_ref, own0_ref, own1_ref, below0_ref, below1_ref, probe_hbm, amp_hbm, lf_ref, rf_ref, la_ref, ra_ref,
    up_ref, low_ref, send_hbm, keep_hbm,
    tall, patch, folded0, folded1, mid0, mid1, wide0, wide1, far, waves, probe, amp, terms_out,
    probe_sem, amp_sem, out_sem,
):
    row_start = info_ref[0]
    first_mode = info_ref[1]
    live = info_ref[2].astype(F32)
    col_start = info_ref[3]
    turn_block, turn = col_start % W // 128, col_start % 128
    folded, mid, wide = (folded0, folded1), (mid0, mid1), (wide0, wide1)

    def loop(count, body, unroll=1):
        lax.fori_loop(0, count, lambda i, c: (body(i), c)[1], 0, unroll=unroll)

    def rows16(step, base=0):
        if isinstance(step, int):
            return slice(base + step * 16, base + step * 16 + 16)
        return pl.ds(pl.multiple_of(base + step * 16, 16), 16)

    def probe_copy(m):
        mode = lax.rem(m + first_mode, 4)
        return pltpu.make_async_copy(probe_hbm.at[mode], probe.at[m], probe_sem.at[m])

    def terms_copy(m):
        target = send_hbm.at[m] if m < 2 else keep_hbm.at[m - 2]
        return pltpu.make_async_copy(terms_out.at[m], target, out_sem.at[m])

    amp_copy = pltpu.make_async_copy(amp_hbm, amp, amp_sem)
    for m in range(4):
        probe_copy(m).start()
    amp_copy.start()

    blocks = [slice(k * 128, (k + 1) * 128) for k in range(4)]
    lane_blocks = [(part, k, blocks[k]) for part in range(2) for k in range(4)]

    def stack_rows(step):
        for part, k, lanes in lane_blocks:
            for h, ref in enumerate((own0_ref, own1_ref, below0_ref, below1_ref)):
                tall[part, k, rows16(step, h * HALF), :] = ref[part, rows16(step), lanes].astype(F32)

    loop(HALF // 16, stack_rows, 2)
    lane16 = lax.broadcasted_iota(jnp.int32, (16, 128), 1)

    def take_rows(step):
        for part in range(2):
            turned = []
            for k in range(4):
                value = tall[part, (turn_block + k) % 4, pl.ds(row_start + step * 16, 16), :]
                turned.append(pltpu.roll(value, (128 - turn) % 128, 1))
            for k, lanes in enumerate(blocks):
                value = jnp.where(lane16 < 128 - turn, turned[k], turned[(k + 1) % 4])
                patch[part, rows16(step), lanes] = value

    loop(W // 16, take_rows, 4)

    def exit_fold(m, quarter):
        for step in (quarter * 2, quarter * 2 + 1):
            for lanes in blocks:
                parts = []
                for q in range(4):
                    rows = rows16(step, q * Q)
                    pr = probe[m, 0, rows, lanes].astype(F32)
                    pi = probe[m, 1, rows, lanes].astype(F32)
                    xr, xi = patch[0, rows, lanes], patch[1, rows, lanes]
                    er = (pr * xr - pi * xi).astype(BF16).astype(F32)
                    ei = (pr * xi + pi * xr).astype(BF16).astype(F32)
                    parts.append((er, ei))
                for r, (zr, zi) in enumerate(fold(parts, 1)):
                    folded[m % 2][r, rows16(step), lanes] = zr.astype(BF16)
                    folded[m % 2][r, rows16(step, Q), lanes] = zi.astype(BF16)

    def column_fold(m, r):
        for step in range(Q // 16):
            parts = []
            for lanes in blocks:
                yr = mid[m % 2][r, rows16(step), lanes].astype(BF16).astype(F32)
                yi = mid[m % 2][r, rows16(step, Q), lanes].astype(BF16).astype(F32)
                parts.append((yr, yi))
            for c, (wr, wi) in enumerate(fold(parts, 1)):
                wide[m % 2][c, rows16(step, r * Q), 0:128] = wr.astype(BF16)
                wide[m % 2][c, rows16(step, r * Q), 128:256] = wi.astype(BF16)

    def forward_step(tick, i):
        if tick < 4:
            exit_fold(tick, i)
        if 0 <= tick - 1 < 4:
            mid[(tick - 1) % 2][i] = dot(lf_ref[i], folded[(tick - 1) % 2][i])
        if 0 <= tick - 2 < 4:
            column_fold(tick - 2, i)
        if 0 <= tick - 3 < 4:
            far[tick - 3, i] = dot(wide[(tick - 3) % 2][i], rf_ref[i])

    for tick in range(7):
        if tick < 4:
            probe_copy(tick).wait()
        [forward_step(tick, i) for i in range(4)]

    amp_copy.wait()

    def residual(step):
        r, inner = step // 8, step % 8
        rows = rows16(step)
        for c, lanes in enumerate(blocks):
            fields = [(far[m, c, rows, 0:128], far[m, c, rows, 128:256]) for m in range(4)]
            intensity = sum(fr * fr + fi * fi for fr, fi in fields)
            ratio = live * (1.0 - amp[rows, lanes] * lax.rsqrt(jnp.maximum(intensity, 0.25)))
            for m, (fr, fi) in enumerate(fields):
                waves[m, r, rows16(inner), lanes] = (fr * ratio).astype(BF16)
                waves[m, r, rows16(inner, Q), lanes] = (fi * ratio).astype(BF16)

    loop(W // 16, residual, 2)

    def row_unfold(m, c):
        lanes = blocks[c]
        for step in range(Q // 16):
            parts = [
                (mid[m % 2][r, rows16(step), lanes], mid[m % 2][r, rows16(step, Q), lanes])
                for r in range(4)
            ]
            for q, (yr, yi) in enumerate(fold(parts, -1)):
                wide[m % 2][c, rows16(step, q * Q), 0:128] = yr.astype(BF16)
                wide[m % 2][c, rows16(step, q * Q), 128:256] = yi.astype(BF16)

    def terms(m, quarter):
        for step in range(8):
            rows = rows16(quarter * 8 + step)
            parts = [(far[m, c, rows, 0:128], far[m, c, rows, 128:256]) for c in range(4)]
            for lanes, (gr, gi) in zip(blocks, fold(parts, -1)):
                pr = probe[m, 0, rows, lanes].astype(F32)
                pi = probe[m, 1, rows, lanes].astype(F32)
                object_r, object_i = pr * gr + pi * gi, pr * gi - pi * gr
                if m:
                    object_r = object_r + up_ref[0, rows, lanes]
                    object_i = object_i + up_ref[1, rows, lanes]
                up_ref[0, rows, lanes] = object_r
                up_ref[1, rows, lanes] = object_i
                xr, xi = patch[0, rows, lanes], patch[1, rows, lanes]
                terms_out[m, 0, rows, lanes] = (xr * gr + xi * gi).astype(BF16)
                terms_out[m, 1, rows, lanes] = (xr * gi - xi * gr).astype(BF16)

    def adjoint_step(tick, i):
        if tick < 4:
            mid[tick % 2][i] = dot(la_ref[i], waves[tick, i])
        if 0 <= tick - 1 < 4:
            row_unfold(tick - 1, i)
        if 0 <= tick - 2 < 4:
            far[tick - 2, i] = dot(wide[(tick - 2) % 2][i], ra_ref[i])
        if 0 <= tick - 3 < 4:
            terms(tick - 3, i)

    for tick in range(7):
        [adjoint_step(tick, i) for i in range(4)]
        if tick >= 3:
            terms_copy(tick - 3).start()

    def clear(step):
        for part, k, lanes in lane_blocks:
            tall[part, k, rows16(step), :] = jnp.zeros((16, 128), F32)
            tall[part, k, rows16(step, W), :] = jnp.zeros((16, 128), F32)

    loop(W // 16, clear, 2)

    def put_rows(step):
        for part in range(2):
            turned = [pltpu.roll(up_ref[part, rows16(step), lanes], turn, 1) for lanes in blocks]
            for k in range(4):
                value = jnp.where(lane16 < turn, turned[(k + 3) % 4], turned[k])
                tall[part, (turn_block + k) % 4, pl.ds(row_start + step * 16, 16), :] = value

    loop(W // 16, put_rows, 4)

    def split_rows(step):
        rows = rows16(step)
        for part, k, lanes in lane_blocks:
            up_ref[part, rows, lanes] = tall[part, k, rows, :]
            low_ref[part, rows, lanes] = tall[part, k, rows16(step, W), :].astype(BF16)

    loop(W // 16, split_rows, 2)
    for m in range(4):
        terms_copy(m).wait()


def wave(info, own0, own1, below0, below1, probe, amp):
    tables = [jnp.asarray(t) for t in block_tables()]
    vmem = pl.BlockSpec(memory_space=pltpu.VMEM)
    hbm = pl.BlockSpec(memory_space=pl.ANY)
    return pl.pallas_call(
        wave_kernel,
        out_shape=(
            jax.ShapeDtypeStruct((2, W, W), F32),
            jax.ShapeDtypeStruct((2, W, W), BF16),
            jax.ShapeDtypeStruct((2, 2, W, W), BF16),
            jax.ShapeDtypeStruct((2, 2, W, W), BF16),
        ),
        in_specs=[pl.BlockSpec(memory_space=pltpu.SMEM), vmem, vmem, vmem, vmem, hbm, hbm] + [vmem] * 4,
        out_specs=(vmem, vmem, hbm, hbm),
        scratch_shapes=[
            pltpu.VMEM((2, 4, 2 * W, 128), F32),
            pltpu.VMEM((2, W, W), F32),
            pltpu.VMEM((4, 256, W), BF16),
            pltpu.VMEM((4, 256, W), BF16),
            pltpu.VMEM((4, 256, W), F32),
            pltpu.VMEM((4, 256, W), F32),
            pltpu.VMEM((4, W, 256), BF16),
            pltpu.VMEM((4, W, 256), BF16),
            pltpu.VMEM((4, 4, W, 256), F32),
            pltpu.VMEM((4, 4, 256, W), BF16),
            pltpu.VMEM((4, 2, W, W), BF16),
            pltpu.VMEM((W, W), F32),
            pltpu.VMEM((4, 2, W, W), BF16),
            pltpu.SemaphoreType.DMA((4,)),
            pltpu.SemaphoreType.DMA,
            pltpu.SemaphoreType.DMA((4,)),
        ],
        compiler_params=pltpu.CompilerParams(vmem_limit_bytes=54 * MIB),
        cost_estimate=pl.CostEstimate(flops=20 * 10**9, bytes_accessed=20 * MIB, transcendentals=W * W),
        name="wave",
    )(info, own0, own1, below0, below1, probe, amp, *tables)


def over_kernel(starts_ref, up_ref, above_ref, after_ref, out_ref):
    def body(rows):
        for part in range(2):
            for block in range(4):
                lanes = slice(block * 128, block * 128 + 128)
                total = jnp.zeros((16, 128), F32)
                for source, ref in enumerate((up_ref, above_ref)):
                    passes = lane_index(block, 16) < starts_ref[source] - W
                    total = total + jnp.where(passes, ref[part, rows, lanes].astype(F32), 0.0)
                out_ref[part, rows, lanes] = total.astype(BF16)

    row_steps(out_ref.shape[1], 16, body)


def overflow(starts, up, above, after):
    whole = pl.BlockSpec((2, 128, W), lambda i: (0, i, 0))
    return pl.pallas_call(
        over_kernel,
        grid=(4,),
        out_shape=jax.ShapeDtypeStruct((2, W, W), BF16),
        in_specs=[
            pl.BlockSpec(memory_space=pltpu.SMEM),
            whole,
            whole,
            pl.BlockSpec(memory_space=pl.ANY),
        ],
        out_specs=whole,
        compiler_params=pltpu.CompilerParams(vmem_limit_bytes=16 * MIB),
        cost_estimate=pl.CostEstimate(flops=WEIGHT, bytes_accessed=2 * MIB, transcendentals=0),
        name="overflow",
    )(starts, up, above, after)


def finish_kernel(starts_ref, up_ref, above_ref, left_ref, after_ref, out_ref):
    masks = []
    for block in range(4):
        lane = lane_index(block, 16)
        for source in range(2):
            start = starts_ref[source]
            masks.append((lane >= start, jnp.logical_and(lane < start, lane >= start - W)))

    def body(rows):
        for part in range(2):
            for block in range(4):
                lanes = slice(block * 128, block * 128 + 128)
                low = left_ref[part, rows, lanes].astype(F32)
                high = jnp.zeros((16, 128), F32)
                for source, ref in enumerate((up_ref, above_ref)):
                    in_first, in_second = masks[block * 2 + source]
                    value = ref[part, rows, lanes].astype(F32)
                    low = low + jnp.where(in_first, value, 0.0)
                    high = high + jnp.where(in_second, value, 0.0)
                out_ref[part, rows, lanes] = low
                out_ref[part, rows, W + block * 128 : W + block * 128 + 128] = high

    row_steps(out_ref.shape[1], 16, body)


def finish(starts, up, above, left, after):
    size = 64
    spec = lambda columns: pl.BlockSpec((2, size, columns), lambda i: (0, i, 0))
    return pl.pallas_call(
        finish_kernel,
        grid=(W // size,),
        out_shape=jax.ShapeDtypeStruct((2, W, 1024), F32),
        in_specs=[pl.BlockSpec(memory_space=pltpu.SMEM)] + [spec(W)] * 3 + [pl.BlockSpec(memory_space=pl.ANY)],
        out_specs=spec(1024),
        compiler_params=pltpu.CompilerParams(vmem_limit_bytes=16 * MIB),
        cost_estimate=pl.CostEstimate(flops=4 * MIB, bytes_accessed=8 * MIB, transcendentals=0),
        name="finish",
    )(starts, up, above, left, after)


def chip_sum_kernel(keep_ref, got_ref, out_ref):
    def body(rows):
        for mode in range(2):
            for part in range(2):
                total = keep_ref[mode, part, rows, :].astype(F32) + got_ref[mode, part, rows, :].astype(F32)
                short = pl.ds(pl.multiple_of(rows.start // 4, 16), 16)
                for x in range(4):
                    group = [total[x * 8 : x * 8 + 8], total[32 + x * 8 : 40 + x * 8]]
                    out_ref[x, mode, part, short, :] = jnp.concatenate(group, axis=0).astype(BF16)

    row_steps(Q, 64, body)


def chip_sum(keep, got):
    spec = pl.BlockSpec((2, 2, Q, W), lambda i: (0, 0, i, 0))
    return pl.pallas_call(
        chip_sum_kernel,
        grid=(4,),
        out_shape=jax.ShapeDtypeStruct((4, 2, 2, Q, W), BF16),
        in_specs=[spec, spec],
        out_specs=pl.BlockSpec((4, 2, 2, Q // 4, W), lambda i: (0, 0, 0, i, 0)),
        compiler_params=pltpu.CompilerParams(vmem_limit_bytes=16 * MIB),
        cost_estimate=pl.CostEstimate(flops=WEIGHT, bytes_accessed=6 * MIB, transcendentals=0),
        name="chip_sum",
    )(keep, got)


ROW = ("y", "z_hi")
COL = ("z_lo", "x", "core")


def chips_sum(send, keep):
    got = lax.ppermute(send, "core", [(0, 1), (1, 0)])
    blocks = chip_sum(keep, got)
    return blocks, lax.all_to_all(blocks, "x", 0, 0, tiled=True)


def row_blocks_kernel(got_ref, out_ref):
    upper = lax.broadcasted_iota(jnp.int32, (8, W), 0) < 4

    def body(rows):
        totals = []
        for mode in range(2):
            for part in range(2):
                totals.append(sum(got_ref[k, mode, part, rows, :].astype(F32) for k in range(4)))
        for half in range(2):
            pieces = [total[half * 8 : half * 8 + 8] for total in totals]
            turned = [pltpu.roll(piece, 4, 0) for piece in pieces]
            for core in range(2):
                pair = []
                for k in (0, 2):
                    if core == 0:
                        pair.append(jnp.where(upper, pieces[k], turned[k + 1]))
                    else:
                        pair.append(jnp.where(upper, turned[k], pieces[k + 1]))
                place = rows.start // 4 + half * 2 + core
                out_ref[place] = jnp.concatenate(pair, axis=0).astype(BF16)

    row_steps(got_ref.shape[3], 16, body)


def row_blocks(got):
    return pl.pallas_call(
        row_blocks_kernel,
        grid=(4,),
        out_shape=jax.ShapeDtypeStruct((32, 16, W), BF16),
        in_specs=[pl.BlockSpec((4, 2, 2, Q // 4, W), lambda i: (0, 0, 0, i, 0))],
        out_specs=pl.BlockSpec((8, 16, W), lambda i: (i, 0, 0)),
        compiler_params=pltpu.CompilerParams(vmem_limit_bytes=16 * MIB),
        cost_estimate=pl.CostEstimate(flops=MIB, bytes_accessed=3 * MIB, transcendentals=0),
        name="row_blocks",
    )(got)


def rows_sum(blocks):
    got = lax.all_to_all(blocks, ("y", "z_hi", "z_lo", "core"), 0, 0, tiled=True)
    return got.astype(F32).reshape(16, 2, 16, W).sum(0).reshape(4, 2, 4, W)


def per_device(object_field, probe_modes, positions, amplitudes, live_slots):
    row, col = lax.axis_index(ROW), lax.axis_index(COL)
    tile_rows, tile_cols = object_field.shape[1:]
    to_left = [(i + 1, i) for i in range(15)]
    to_right = [(i, i + 1) for i in range(15)]
    to_upper = [(i + 1, i) for i in range(7)]
    to_lower = [(i, i + 1) for i in range(7)]
    upper = lax.ppermute(positions, ROW, to_lower)
    right = [lax.ppermute(left_columns(object_field, h, HALF), COL, to_left) for h in range(2)]
    own_start = positions[:, 1] - col * tile_cols
    upper_start = jnp.clip(upper[:, 1] - col * tile_cols, 0, tile_cols - 1)
    row_start = positions[0, 0] - row * tile_rows
    chosen = [window_columns(upper_start, object_field, right[h], h) for h in range(2)]
    below = [lax.ppermute(chosen[h], ROW, to_upper) for h in range(2)]
    own = [window_columns(own_start, object_field, right[h], h) for h in range(2)]
    amp = amplitude_parts(amplitudes[0])
    first_mode = 2 * (1 - lax.axis_index("core"))
    info = jnp.stack([row_start, first_mode, live_slots[0], own_start[0]]).astype(jnp.int32)
    up, low, send, keep = wave(info, *own, *below, probe_modes, amp)
    above = lax.ppermute(low, ROW, to_lower)
    chip_terms, chips_terms = chips_sum(send, keep)
    starts = jnp.concatenate([own_start, upper_start])
    left = lax.ppermute(overflow(starts, up, above, chip_terms), COL, to_right)
    row_terms = row_blocks(chips_terms)
    probe_grad = rows_sum(row_terms)
    return finish(starts, up, above, left, row_terms), probe_grad


def solution(mesh):
    chips = jax.sharding.Mesh(mesh.devices.reshape(4, 2, 2, 4, 2), ROW + COL)
    slots = ROW + COL
    placed = (P(None, ROW, COL), P(), P(slots, None), P(slots, None, None), P(slots))
    return jax.shard_map(
        per_device,
        mesh=chips,
        in_specs=placed,
        out_specs=(P(None, ROW, COL), P(None, None, slots, None)),
        check_vma=False,
    )
```

time: 163 us -> 142 us (0.87)
  the two profiles are of different devices: /device:TPU:11 before, /device:TPU:56 now
where the time goes in v2:
time: 142 us; the launch traced here: 141 us
  waiting for transfers between devices  46.9 us (33%)
  Pallas kernels  40 us (28%)
  starting transfers between devices  33.8 us (24%)
  local copies, waits for them, and re-layouts  16 us (11%)
  between operations  3.44 us (2%)
    pallas_call x1, Pallas kernels, wave(): pl.pallas_call(wave_kernel, out_shape=(jax.ShapeDtypeStruct((2, W, W), F3...  19.4 us
    ppermute x1, waiting for transfers between devices, per_device(): above = lax.ppermute(low, ROW, to_lower)  18.2 us
    unnamed x26, local copies, waits for them, and re-layouts  14.2 us
    ppermute x2, waiting for transfers between devices, per_device(): below = [lax.ppermute(chosen[h], ROW, to_upper) for h in range(2)]  14.1 us
    ppermute x1, waiting for transfers between devices, per_device(): left = lax.ppermute(overflow(starts, up, above, chip_terms), COL, to_right)  11.2 us
    ppermute x2, starting transfers between devices, per_device(): below = [lax.ppermute(chosen[h], ROW, to_upper) for h in range(2)]  7.51 us
    pallas_call x4, Pallas kernels, window_columns(): pl.pallas_call(columns_kernel, grid=(1,), out_shape=jax.ShapeDtypeStruct(...  7.27 us
    all_to_all x1, starting transfers between devices, rows_sum(): lax.all_to_all(blocks, ('y', 'z_hi', 'z_lo', 'core'), 0, 0, tiled=True)  6.91 us
  transfers between devices with their start and end apart: 10, of which 6 were waited for; matrix products, arithmetic and copies ran while one was open for 1% of the time, Pallas kernels for 15%

profile of v2, /device:TPU:56, one launch (start us, length us, event | category | flops | bytes accessed | tf_op | source)
XLA Modules:
  0.0 140.9 jit_solution(5137729328671355368)
XLA Ops:
  0.6 0.0 copy-start
  0.6 1.6 %copy-done = bf16[2,512,1024]{2,1,0:T(8,128)(2,1)S(1)} copy-done((bf16[2,512,1024]{2,1,0:T(8,128)(2,1)S(1)}, bf16[2,512,1024]{2,1,0:T(8,128)(2,1)}, u32[]{:S(2)}) %copy-start) | copy-done | bytes 2097176
  2.3 3.7 %collective-permute-start.1 = (bf16[2,256,512]{2,1,0:T(8,128)(2,1)S(1)}, bf16[2,256,512]{2,1,0:T(8,128)(2,1)}, u32[]{:S(2)}, u32[]{:S(2)}) collective-permute-start(bf16[2,256,512]{2,1,0:T(8,128)(2,1)S(1)} %left_columns.2), channel_id=1, source_target_pairs={{1,0},{2,1},{3,2},{4,3},{5,4},{6,5},{7,6},{8,7},{9,8},{10,9},{11,1... | collective-permute-start | bytes 1572872 | tf_op jit(solution)/shard_map/ppermute | solution.py:535
  5.9 5.2 %collective-permute-start = (s32[1,2]{1,0:T(1,128)S(1)}, s32[1,2]{1,0:T(1,128)S(1)}, u32[]{:S(2)}, u32[]{:S(2)}) collective-permute-start(s32[1,2]{1,0:T(1,128)S(1)} %copy-done.12), channel_id=1, source_target_pairs={{0,16},{16,32},{32,48},{48,64},{64,80},{80,96},{96,112},{1,17},{17... | collective-permute-start | bytes 32 | tf_op jit(solution)/shard_map/ppermute | solution.py:534
  11.2 0.0 copy-start.1
  11.2 3.0 %collective-permute-start.2 = (bf16[2,256,512]{2,1,0:T(8,128)(2,1)S(1)}, bf16[2,256,512]{2,1,0:T(8,128)(2,1)}, u32[]{:S(2)}, u32[]{:S(2)}) collective-permute-start(bf16[2,256,512]{2,1,0:T(8,128)(2,1)S(1)} %left_columns.3), channel_id=1, source_target_pairs={{1,0},{2,1},{3,2},{4,3},{5,4},{6,5},{7,6},{8,7},{9,8},{10,9},{11,1... | collective-permute-start | bytes 1572872 | tf_op jit(solution)/shard_map/ppermute | solution.py:535
  14.9 0.6 fusion
  16.8 0.0 copy-start.6
  16.8 1.2 copy-done.6
  18.0 1.0 copy-done.7
  19.0 1.8 %amplitude_parts.1.amp_hbm = f32[512,512]{1,0:T(8,128)S(1)} custom-call(f32[512,512]{1,0:T(8,128)S(1)} %bitcast.9, bf16[512,512]{1,0:T(8,128)(2,1)S(1)} %copy-done.7), custom_call_target="tpu_custom_call" | custom-call | flops 805306368 | bytes 3145728 | tf_op jit(solution)/shard_map/amplitude_parts/pallas_call | solution.py:76
  20.9 1.0 copy-done.8
  21.9 0.6 pad_add_fusion.1.info_ref
  22.5 0.0 collective-permute-done
  22.5 0.6 slice.10
  23.7 0.0 collective-permute-done.1.right_ref
  23.7 2.2 %window_columns.6 = bf16[2,256,512]{2,1,0:T(8,128)(2,1)} custom-call(s32[1]{0:T(128)S(6)} %min.6.start_ref, bf16[2,512,1024]{2,1,0:T(8,128)(2,1)S(1)} %copy-done.1, bf16[2,256,512]{2,1,0:T(8,128)(2,1)} %collective-permute-done.1.right_ref), custom_call_target="tpu_custom_call" | custom-call | flops 99999997952 | bytes 2097152 | tf_op jit(solution)/shard_map/window_columns/pallas_call | solution.py:120
  26.0 2.1 %collective-permute-start.3 = (bf16[2,256,512]{2,1,0:T(8,128)(2,1)}, bf16[2,256,512]{2,1,0:T(8,128)(2,1)}, u32[]{:S(2)}, u32[]{:S(2)}) collective-permute-start(bf16[2,256,512]{2,1,0:T(8,128)(2,1)} %window_columns.6), channel_id=1, source_target_pairs={{16,0},{32,16},{48,32},{64,48},{80,64},{96,80},{112,96},{17,1},{33... | collective-permute-start | bytes 1572872 | tf_op jit(solution)/shard_map/ppermute | solution.py:540
  28.0 2.2 %window_columns.7 = bf16[2,256,512]{2,1,0:T(8,128)(2,1)} custom-call(s32[1]{0:T(128)S(6)} %min.6.start_ref, bf16[2,512,1024]{2,1,0:T(8,128)(2,1)S(1)} %copy-done.1, bf16[2,256,512]{2,1,0:T(8,128)(2,1)} %collective-permute-done.2.right_ref), custom_call_target="tpu_custom_call" | custom-call | flops 99999997952 | bytes 2097152 | tf_op jit(solution)/shard_map/window_columns/pallas_call | solution.py:120
  30.3 5.4 %collective-permute-start.4 = (bf16[2,256,512]{2,1,0:T(8,128)(2,1)}, bf16[2,256,512]{2,1,0:T(8,128)(2,1)}, u32[]{:S(2)}, u32[]{:S(2)}) collective-permute-start(bf16[2,256,512]{2,1,0:T(8,128)(2,1)} %window_columns.7), channel_id=1, source_target_pairs={{16,0},{32,16},{48,32},{64,48},{80,64},{96,80},{112,96},{17,1},{33... | collective-permute-start | bytes 1572872 | tf_op jit(solution)/shard_map/ppermute | solution.py:540
  35.7 1.4 %window_columns.4.own0_ref = bf16[2,256,512]{2,1,0:T(8,128)(2,1)S(1)} custom-call(s32[1]{0:T(128)S(6)} %sub.17.start_ref, bf16[2,512,1024]{2,1,0:T(8,128)(2,1)S(1)} %copy-done.1, bf16[2,256,512]{2,1,0:T(8,128)(2,1)} %collective-permute-done.1.right_ref), custom_call_target="tpu_custom_call" | custom-call | flops 99999997952 | bytes 2097152 | tf_op jit(solution)/shard_map/window_columns/pallas_call | solution.py:120
  37.1 0.8 copy-done.10
  37.9 1.4 %window_columns.5.own1_ref = bf16[2,256,512]{2,1,0:T(8,128)(2,1)S(1)} custom-call(s32[1]{0:T(128)S(6)} %sub.17.start_ref, bf16[2,512,1024]{2,1,0:T(8,128)(2,1)S(1)} %copy-done.1, bf16[2,256,512]{2,1,0:T(8,128)(2,1)} %collective-permute-done.2.right_ref), custom_call_target="tpu_custom_call" | custom-call | flops 99999997952 | bytes 2097152 | tf_op jit(solution)/shard_map/window_columns/pallas_call | solution.py:120
  39.3 0.8 copy-done.11
  40.2 4.3 %collective-permute-done.3.below0_ref = bf16[2,256,512]{2,1,0:T(8,128)(2,1)} collective-permute-done((bf16[2,256,512]{2,1,0:T(8,128)(2,1)}, bf16[2,256,512]{2,1,0:T(8,128)(2,1)}, u32[]{:S(2)}, u32[]{:S(2)}) %collective-permute-start.3) | collective-permute-done | bytes 524320 | tf_op jit(solution)/shard_map/ppermute | solution.py:540
  44.5 9.7 %collective-permute-done.4.below1_ref = bf16[2,256,512]{2,1,0:T(8,128)(2,1)} collective-permute-done((bf16[2,256,512]{2,1,0:T(8,128)(2,1)}, bf16[2,256,512]{2,1,0:T(8,128)(2,1)}, u32[]{:S(2)}, u32[]{:S(2)}) %collective-permute-start.4) | collective-permute-done | bytes 524320 | tf_op jit(solution)/shard_map/ppermute | solution.py:540
  54.2 19.4 %wave.1 = (f32[2,512,512]{2,1,0:T(8,128)}, bf16[2,512,512]{2,1,0:T(8,128)(2,1)}, bf16[2,2,512,512]{3,2,1,0:T(8,128)(2,1)}, bf16[2,2,512,512]{3,2,1,0:T(8,128)(2,1)}) custom-call(s32[4]{0:T(128)} %pad_add_fusion.1.info_ref, bf16[2,256,512]{2,1,0:T(8,128)(2,1)} %copy-done.10, bf16[2,256,512]{2,1,0:T(8,128)(2,1)} %copy-done.11, ...), custom_call_target="tpu_custom_call" | custom-call | flops 20000000000 | bytes 20971520 | tf_op jit(solution)/shard_map/wave/pallas_call | solution.py:341
  73.6 0.1 collective-permute-start.6
  73.7 0.1 pad_add_fusion.starts_ref
  73.8 1.9 %collective-permute-start.5 = (bf16[2,512,512]{2,1,0:T(8,128)(2,1)}, bf16[2,512,512]{2,1,0:T(8,128)(2,1)S(1)}, u32[]{:S(2)}, u32[]{:S(2)}) collective-permute-start(bf16[2,512,512]{2,1,0:T(8,128)(2,1)} %get-tuple-element.7), channel_id=1, source_target_pairs={{0,16},{16,32},{32,48},{48,64},{64,80},{80,96},{96,112},{1,17},{17... | collective-permute-start | bytes 3145736 | tf_op jit(solution)/shard_map/ppermute | solution.py:546
  75.7 2.4 %collective-permute-done.6.got_ref = bf16[2,2,512,512]{3,2,1,0:T(8,128)(2,1)S(1)} collective-permute-done((bf16[2,2,512,512]{3,2,1,0:T(8,128)(2,1)}, bf16[2,2,512,512]{3,2,1,0:T(8,128)(2,1)S(1)}, u32[]{:S(2)}, u32[]{:S(2)}) %collective-permute-start.6) | collective-permute-done | bytes 2097184 | tf_op jit(solution)/shard_map/ppermute | solution.py:480
  78.1 1.6 %copy-done.9 = bf16[2,2,512,512]{3,2,1,0:T(8,128)(2,1)S(1)} copy-done((bf16[2,2,512,512]{3,2,1,0:T(8,128)(2,1)S(1)}, bf16[2,2,512,512]{3,2,1,0:T(8,128)(2,1)}, u32[]{:S(2)}) %copy-start.9) | copy-done | bytes 2097176
  79.7 1.0 chip_sum.1.after_ref
  80.7 1.3 copy-done.4
  82.0 3.6 %all-to-all-start = ((bf16[4,2,2,128,512]{4,3,2,1,0:T(8,128)(2,1)}), bf16[4,2,2,128,512]{4,3,2,1,0:T(8,128)(2,1)S(1)}, u32[]{:S(2)}, u32[]{:S(2)}) async-start(bf16[4,2,2,128,512]{4,3,2,1,0:T(8,128)(2,1)} %copy-done.4), calls=%async_computation | async-start | bytes 4194304 | tf_op jit(solution)/shard_map/all_to_all | solution.py:482
  85.6 18.2 %collective-permute-done.5.above_ref = bf16[2,512,512]{2,1,0:T(8,128)(2,1)S(1)} collective-permute-done((bf16[2,512,512]{2,1,0:T(8,128)(2,1)}, bf16[2,512,512]{2,1,0:T(8,128)(2,1)S(1)}, u32[]{:S(2)}, u32[]{:S(2)}) %collective-permute-start.5) | collective-permute-done | bytes 1048608 | tf_op jit(solution)/shard_map/ppermute | solution.py:546
  103.8 1.6 %copy-done.2 = f32[2,512,512]{2,1,0:T(8,128)S(1)} copy-done((f32[2,512,512]{2,1,0:T(8,128)S(1)}, f32[2,512,512]{2,1,0:T(8,128)}, u32[]{:S(2)}) %copy-start.2) | copy-done | bytes 2097176
  105.4 1.6 %copy-done.5 = bf16[4,2,2,128,512]{4,3,2,1,0:T(8,128)(2,1)S(1)} copy-done((bf16[4,2,2,128,512]{4,3,2,1,0:T(8,128)(2,1)S(1)}, bf16[4,2,2,128,512]{4,3,2,1,0:T(8,128)(2,1)}, u32[]{:S(2)}) %copy-start.5) | copy-done | bytes 2097176
  107.0 2.6 %overflow.1 = bf16[2,512,512]{2,1,0:T(8,128)(2,1)} custom-call(s32[2]{0:T(128)S(1)} %pad_add_fusion.starts_ref, f32[2,512,512]{2,1,0:T(8,128)S(1)} %copy-done.2, bf16[2,512,512]{2,1,0:T(8,128)(2,1)S(1)} %collective-permute-done.5.above_ref, bf16[4,2,2,128,512]{4,3,2,1,0:T(8,128)(2,1)S(1)} %copy-done.5), custom_call_target="tpu_custom_call" | custom-call | flops 99999997952 | bytes 2097152 | tf_op jit(solution)/shard_map/overflow/pallas_call | solution.py:391
  109.6 1.9 %collective-permute-start.7 = (bf16[2,512,512]{2,1,0:T(8,128)(2,1)}, bf16[2,512,512]{2,1,0:T(8,128)(2,1)}, u32[]{:S(2)}, u32[]{:S(2)}) collective-permute-start(bf16[2,512,512]{2,1,0:T(8,128)(2,1)} %overflow.1), channel_id=1, source_target_pairs={{0,1},{1,2},{2,3},{3,4},{4,5},{5,6},{6,7},{7,8},{8,9},{9,10},{10,1... | collective-permute-start | bytes 3145736 | tf_op jit(solution)/shard_map/ppermute | solution.py:549
  111.5 1.0 all-to-all-done.got_ref
  112.5 1.7 %row_blocks.1.after_ref = bf16[32,16,512]{2,1,0:T(8,128)(2,1)} custom-call(bf16[4,2,2,128,512]{4,3,2,1,0:T(8,128)(2,1)S(1)} %all-to-all-done.got_ref), custom_call_target="tpu_custom_call" | custom-call | flops 1048576 | bytes 3145728 | tf_op jit(solution)/shard_map/row_blocks/pallas_call | solution.py:510
  114.3 6.9 %all-to-all-start.1 = ((bf16[32,16,512]{2,1,0:T(8,128)(2,1)}), bf16[32,16,512]{2,1,0:T(8,128)(2,1)S(1)}, u32[]{:S(2)}, u32[]{:S(2)}) async-start(bf16[32,16,512]{2,1,0:T(8,128)(2,1)} %row_blocks.1.after_ref), calls=%async_computation.1 | async-start | bytes 1048576 | tf_op jit(solution)/shard_map/all_to_all | solution.py:523
  121.2 11.2 %collective-permute-done.7.left_ref = bf16[2,512,512]{2,1,0:T(8,128)(2,1)} collective-permute-done((bf16[2,512,512]{2,1,0:T(8,128)(2,1)}, bf16[2,512,512]{2,1,0:T(8,128)(2,1)}, u32[]{:S(2)}, u32[]{:S(2)}) %collective-permute-start.7) | collective-permute-done | bytes 1048608 | tf_op jit(solution)/shard_map/ppermute | solution.py:549
  132.4 1.6 %copy-done.3 = f32[2,512,512]{2,1,0:T(8,128)S(1)} copy-done((f32[2,512,512]{2,1,0:T(8,128)S(1)}, f32[2,512,512]{2,1,0:T(8,128)}, u32[]{:S(2)}) %copy-start.3) | copy-done | bytes 2097176
  134.0 6.2 %finish.1 = f32[2,512,1024]{2,1,0:T(8,128)} custom-call(s32[2]{0:T(128)S(1)} %pad_add_fusion.starts_ref, f32[2,512,512]{2,1,0:T(8,128)S(1)} %copy-done.3, bf16[2,512,512]{2,1,0:T(8,128)(2,1)S(1)} %collective-permute-done.5.above_ref, bf16[2,512,512]{2,1,0:T(8,128)(2,1)} %collective-permute-done.7.left_ref, bf16[32,16,512]{2,1,0:T(8,128)(2,1)} %row_blocks.1.after_ref), custom_call_target="tpu_custom_call" | custom-call | flops 4194304 | bytes 8388608 | tf_op jit(solution)/shard_map/finish/pallas_call | solution.py:436
  140.2 0.1 convert_reduce_fusion
  140.3 0.7 reshape.15
  (16 shorter events, 0.1 us)
Async XLA Ops:
  0.6 1.6 %copy-start = (bf16[2,512,1024]{2,1,0:T(8,128)(2,1)S(1)}, bf16[2,512,1024]{2,1,0:T(8,128)(2,1)}, u32[]{:S(2)}) copy-start(bf16[2,512,1024]{2,1,0:T(8,128)(2,1)} %tile_ref.11) | copy-start | bytes 6291460
  2.2 3.7 %copy-start.12 = (s32[1,2]{1,0:T(1,128)S(1)}, s32[1,2]{1,0:T(1,128)}, u32[]{:S(2)}) copy-start(s32[1,2]{1,0:T(1,128)} %param.12) | copy-start | bytes 28
  2.3 21.5 %collective-permute-start.1 = (bf16[2,256,512]{2,1,0:T(8,128)(2,1)S(1)}, bf16[2,256,512]{2,1,0:T(8,128)(2,1)}, u32[]{:S(2)}, u32[]{:S(2)}) collective-permute-start(bf16[2,256,512]{2,1,0:T(8,128)(2,1)S(1)} %left_columns.2), channel_id=1, source_target_pairs={{1,0},{2,1},{3,2},{4,3},{5,4},{6,5},{7,6},{8,7},{9,8},{10,9},{11,1... | collective-permute-start | bytes 1572872 | tf_op jit(solution)/shard_map/ppermute | solution.py:535
  5.9 16.5 %collective-permute-start = (s32[1,2]{1,0:T(1,128)S(1)}, s32[1,2]{1,0:T(1,128)S(1)}, u32[]{:S(2)}, u32[]{:S(2)}) collective-permute-start(s32[1,2]{1,0:T(1,128)S(1)} %copy-done.12), channel_id=1, source_target_pairs={{0,16},{16,32},{32,48},{48,64},{64,80},{80,96},{96,112},{1,17},{17... | collective-permute-start | bytes 32 | tf_op jit(solution)/shard_map/ppermute | solution.py:534
  11.2 12.6 %copy-start.1 = (bf16[2,512,1024]{2,1,0:T(8,128)(2,1)S(1)}, bf16[2,512,1024]{2,1,0:T(8,128)(2,1)}, u32[]{:S(2)}) copy-start(bf16[2,512,1024]{2,1,0:T(8,128)(2,1)} %tile_ref.11) | copy-start | bytes 6291460
  11.2 16.9 %collective-permute-start.2 = (bf16[2,256,512]{2,1,0:T(8,128)(2,1)S(1)}, bf16[2,256,512]{2,1,0:T(8,128)(2,1)}, u32[]{:S(2)}, u32[]{:S(2)}) collective-permute-start(bf16[2,256,512]{2,1,0:T(8,128)(2,1)S(1)} %left_columns.3), channel_id=1, source_target_pairs={{1,0},{2,1},{3,2},{4,3},{5,4},{6,5},{7,6},{8,7},{9,8},{10,9},{11,1... | collective-permute-start | bytes 1572872 | tf_op jit(solution)/shard_map/ppermute | solution.py:535
  16.8 1.2 copy-start.6
  18.0 1.0 copy-start.7
  20.9 1.0 copy-start.8
  26.0 18.6 %collective-permute-start.3 = (bf16[2,256,512]{2,1,0:T(8,128)(2,1)}, bf16[2,256,512]{2,1,0:T(8,128)(2,1)}, u32[]{:S(2)}, u32[]{:S(2)}) collective-permute-start(bf16[2,256,512]{2,1,0:T(8,128)(2,1)} %window_columns.6), channel_id=1, source_target_pairs={{16,0},{32,16},{48,32},{64,48},{80,64},{96,80},{112,96},{17,1},{33... | collective-permute-start | bytes 1572872 | tf_op jit(solution)/shard_map/ppermute | solution.py:540
  30.3 24.0 %collective-permute-start.4 = (bf16[2,256,512]{2,1,0:T(8,128)(2,1)}, bf16[2,256,512]{2,1,0:T(8,128)(2,1)}, u32[]{:S(2)}, u32[]{:S(2)}) collective-permute-start(bf16[2,256,512]{2,1,0:T(8,128)(2,1)} %window_columns.7), channel_id=1, source_target_pairs={{16,0},{32,16},{48,32},{64,48},{80,64},{96,80},{112,96},{17,1},{33... | collective-permute-start | bytes 1572872 | tf_op jit(solution)/shard_map/ppermute | solution.py:540
  37.1 0.8 copy-start.10
  39.3 0.8 copy-start.11
  73.6 4.5 %collective-permute-start.6 = (bf16[2,2,512,512]{3,2,1,0:T(8,128)(2,1)}, bf16[2,2,512,512]{3,2,1,0:T(8,128)(2,1)S(1)}, u32[]{:S(2)}, u32[]{:S(2)}) collective-permute-start(bf16[2,2,512,512]{3,2,1,0:T(8,128)(2,1)} %get-tuple-element.9), channel_id=1, source_target_pairs={{0,1},{1,0},{2,3},{3,2},{4,5},{5,4},{6,7},{7,6},{8,9},{9,8},{10,11... | collective-permute-start | bytes 6291464 | tf_op jit(solution)/shard_map/ppermute | solution.py:480
  73.8 30.1 %collective-permute-start.5 = (bf16[2,512,512]{2,1,0:T(8,128)(2,1)}, bf16[2,512,512]{2,1,0:T(8,128)(2,1)S(1)}, u32[]{:S(2)}, u32[]{:S(2)}) collective-permute-start(bf16[2,512,512]{2,1,0:T(8,128)(2,1)} %get-tuple-element.7), channel_id=1, source_target_pairs={{0,16},{16,32},{32,48},{48,64},{64,80},{80,96},{96,112},{1,17},{17... | collective-permute-start | bytes 3145736 | tf_op jit(solution)/shard_map/ppermute | solution.py:546
  78.1 1.6 %copy-start.9 = (bf16[2,2,512,512]{3,2,1,0:T(8,128)(2,1)S(1)}, bf16[2,2,512,512]{3,2,1,0:T(8,128)(2,1)}, u32[]{:S(2)}) copy-start(bf16[2,2,512,512]{3,2,1,0:T(8,128)(2,1)} %get-tuple-element.8.keep_ref) | copy-start | bytes 6291460
  80.7 1.3 copy-start.4
  82.0 30.5 %all-to-all-start = ((bf16[4,2,2,128,512]{4,3,2,1,0:T(8,128)(2,1)}), bf16[4,2,2,128,512]{4,3,2,1,0:T(8,128)(2,1)S(1)}, u32[]{:S(2)}, u32[]{:S(2)}) async-start(bf16[4,2,2,128,512]{4,3,2,1,0:T(8,128)(2,1)} %copy-done.4), calls=%async_computation | async-start | bytes 4194304 | tf_op jit(solution)/shard_map/all_to_all | solution.py:482
  103.8 1.6 %copy-start.2 = (f32[2,512,512]{2,1,0:T(8,128)S(1)}, f32[2,512,512]{2,1,0:T(8,128)}, u32[]{:S(2)}) copy-start(f32[2,512,512]{2,1,0:T(8,128)} %get-tuple-element.6.up_ref) | copy-start | bytes 6291460
  105.4 1.6 %copy-start.5 = (bf16[4,2,2,128,512]{4,3,2,1,0:T(8,128)(2,1)S(1)}, bf16[4,2,2,128,512]{4,3,2,1,0:T(8,128)(2,1)}, u32[]{:S(2)}) copy-start(bf16[4,2,2,128,512]{4,3,2,1,0:T(8,128)(2,1)} %copy-done.4) | copy-start | bytes 6291460
  109.6 22.8 %collective-permute-start.7 = (bf16[2,512,512]{2,1,0:T(8,128)(2,1)}, bf16[2,512,512]{2,1,0:T(8,128)(2,1)}, u32[]{:S(2)}, u32[]{:S(2)}) collective-permute-start(bf16[2,512,512]{2,1,0:T(8,128)(2,1)} %overflow.1), channel_id=1, source_target_pairs={{0,1},{1,2},{2,3},{3,4},{4,5},{5,6},{6,7},{7,8},{8,9},{9,10},{10,1... | collective-permute-start | bytes 3145736 | tf_op jit(solution)/shard_map/ppermute | solution.py:549
  114.3 25.9 %all-to-all-start.1 = ((bf16[32,16,512]{2,1,0:T(8,128)(2,1)}), bf16[32,16,512]{2,1,0:T(8,128)(2,1)S(1)}, u32[]{:S(2)}, u32[]{:S(2)}) async-start(bf16[32,16,512]{2,1,0:T(8,128)(2,1)} %row_blocks.1.after_ref), calls=%async_computation.1 | async-start | bytes 1048576 | tf_op jit(solution)/shard_map/all_to_all | solution.py:523
  132.4 1.6 %copy-start.3 = (f32[2,512,512]{2,1,0:T(8,128)S(1)}, f32[2,512,512]{2,1,0:T(8,128)}, u32[]{:S(2)}) copy-start(f32[2,512,512]{2,1,0:T(8,128)} %get-tuple-element.6.up_ref) | copy-start | bytes 6291460

commit v3 on v2

v3 whole, which is shorter than its diff:
```python
import functools
import math

import jax
import jax.numpy as jnp
import ml_dtypes
import numpy as np
from jax import lax
from jax.experimental import pallas as pl
from jax.experimental.pallas import tpu as pltpu
from jax.sharding import PartitionSpec as P

W = 512
Q = W // 4
HALF = W // 2
WEIGHT = 100 * 10**9
MIB = 1024 * 1024
F32 = jnp.float32
BF16 = jnp.bfloat16


def block_tables():
    step = np.arange(W).astype(np.float32) * np.float32(2.0 * math.pi / W)
    scale = np.float32(1.0 / math.sqrt(W))
    cos_of = (np.cos(step) * scale).astype(ml_dtypes.bfloat16).astype(np.float32)
    sin_of = (np.sin(step) * scale).astype(ml_dtypes.bfloat16).astype(np.float32)
    short = np.arange(Q)
    forward = []
    for part in range(4):
        phase = np.outer(4 * short + part, short) % W
        c, s = cos_of[phase], sin_of[phase]
        forward.append(np.block([[c, s], [-s, c]]))
    forward = np.stack(forward).astype(ml_dtypes.bfloat16)
    return forward, np.ascontiguousarray(forward.transpose(0, 2, 1))


def fold(parts, sign):
    (ar, ai), (br, bi), (cr, ci), (dr, di) = parts
    pr, pi, mr, mi = ar + cr, ai + ci, ar - cr, ai - ci
    qr, qi, nr, ni = br + dr, bi + di, br - dr, bi - di
    if sign < 0:
        nr, ni = -nr, -ni
    return (
        (pr + qr, pi + qi),
        (mr + ni, mi - nr),
        (pr - qr, pi - qi),
        (mr - ni, mi + nr),
    )


def dot(a, b):
    return jnp.dot(a, b, preferred_element_type=F32)


def amplitude_kernel(amp_ref, pick_ref, after_ref, out_ref, sorted_ref):
    rows = amp_ref[...]
    high = rows.astype(BF16)
    rest = rows - high.astype(F32)
    middle = rest.astype(BF16)
    low = (rest - middle.astype(F32)).astype(BF16)
    for c in range(4):
        pick = pick_ref[:, c * Q : (c + 1) * Q]
        sorted_ref[c] = (dot(high, pick) + dot(middle, pick)) + dot(low, pick)
    for c in range(4):
        for r in range(4):
            out_ref[r * Q : (r + 1) * Q, c * Q : (c + 1) * Q] = sorted_ref[c, pl.ds(r, Q, stride=4), :]


def amplitude_parts(amp, after):
    source = np.arange(W)
    pick = np.zeros((W, W), ml_dtypes.bfloat16)
    pick[source, (source % 4) * Q + source // 4] = 1
    return pl.pallas_call(
        amplitude_kernel,
        out_shape=jax.ShapeDtypeStruct((W, W), F32),
        in_specs=[pl.BlockSpec(memory_space=pltpu.VMEM)] * 2 + [pl.BlockSpec(memory_space=pl.ANY)],
        scratch_shapes=[pltpu.VMEM((4, W, Q), F32)],
        compiler_params=pltpu.CompilerParams(vmem_limit_bytes=16 * MIB),
        cost_estimate=pl.CostEstimate(flops=6 * W**3, bytes_accessed=3 * MIB, transcendentals=0),
        name="amplitude_parts",
    )(amp, jnp.asarray(pick), after)


def overflow(own_start, up, upper_start, above):
    lane = lax.broadcasted_iota(jnp.int32, up.shape, 2)
    own = jnp.where(lane < own_start - W, up.astype(F32), 0.0)
    return (own + jnp.where(lane < upper_start - W, above.astype(F32), 0.0)).astype(BF16)


def lane_index(block, rows):
    return lax.broadcasted_iota(jnp.int32, (rows, 128), 1) + block * 128


def row_steps(count, size, body, unroll=1):
    def step_of(step, carry):
        body(pl.ds(pl.multiple_of(step * size, size), size))
        return carry

    lax.fori_loop(0, count // size, step_of, 0, unroll=unroll)


def columns_kernel(corner_ref, anchor_ref, tile_ref, right_ref, out_ref):
    start = jnp.clip(corner_ref[0, 1] - anchor_ref[0], 0, 2 * W - 1)
    masks = [(lane_index(k, 16) >= start, lane_index(k, 16) >= start - W) for k in range(4)]

    def body(rows):
        for part in range(2):
            for k, (in_first, in_second) in enumerate(masks):
                lanes = slice(k * 128, k * 128 + 128)
                first = tile_ref[part, rows, lanes].astype(F32)
                second = tile_ref[part, rows, W + k * 128 : W + k * 128 + 128].astype(F32)
                beyond = right_ref[part, rows, lanes].astype(F32)
                value = jnp.where(in_first, first, jnp.where(in_second, second, beyond))
                out_ref[part, rows, lanes] = value.astype(BF16)

    row_steps(out_ref.shape[1], 16, body, 2)


def cut_columns(corner, anchor, tile, right, chunk):
    rows = right.shape[1]
    whole = pl.BlockSpec((2, rows, W), lambda i: (0, 0, 0))
    return pl.pallas_call(
        columns_kernel,
        grid=(1,),
        out_shape=jax.ShapeDtypeStruct((2, rows, W), BF16),
        in_specs=[
            pl.BlockSpec(memory_space=pltpu.SMEM),
            pl.BlockSpec(memory_space=pltpu.SMEM),
            pl.BlockSpec((2, rows, 2 * W), lambda i: (0, chunk, 0)),
            whole,
        ],
        out_specs=whole,
        compiler_params=pltpu.CompilerParams(vmem_limit_bytes=16 * MIB),
        cost_estimate=pl.CostEstimate(flops=WEIGHT, bytes_accessed=2 * MIB, transcendentals=0),
        name="cut_columns",
    )(corner, anchor, tile, right)


def copy_kernel(tile_ref, out_ref):
    out_ref[...] = tile_ref[...]


def left_columns(tile, chunk, rows):
    return pl.pallas_call(
        copy_kernel,
        grid=(1,),
        out_shape=jax.ShapeDtypeStruct((2, rows, W), BF16),
        in_specs=[pl.BlockSpec((2, rows, W), lambda i: (0, chunk, 0))],
        out_specs=pl.BlockSpec((2, rows, W), lambda i: (0, 0, 0)),
        compiler_params=pltpu.CompilerParams(vmem_limit_bytes=16 * MIB),
        cost_estimate=pl.CostEstimate(flops=0, bytes_accessed=MIB, transcendentals=0),
        name="left_columns",
    )(tile)


def wave_kernel(
    info_ref, own0_ref, own1_ref, below0_ref, below1_ref, probe_hbm, amp_hbm, forward_ref, adjoint_ref,
    up_ref, low_ref, send_hbm, keep_hbm,
    tall, patch, folded0, folded1, mid0, mid1, wide0, wide1, far, waves, probe, amp, terms_out, object_sum,
    probe_sem, amp_sem, out_sem,
):
    row_start = info_ref[0]
    core = info_ref[1]
    live = info_ref[2].astype(F32)
    col_start = info_ref[3]
    turn_block, turn = col_start % W // 128, col_start % 128
    folded, mid, wide = (folded0, folded1), (mid0, mid1), (wide0, wide1)

    def loop(count, body, unroll=1):
        lax.fori_loop(0, count, lambda i, c: (body(i), c)[1], 0, unroll=unroll)

    def rows16(step, base=0):
        if isinstance(step, int):
            return slice(base + step * 16, base + step * 16 + 16)
        return pl.ds(pl.multiple_of(base + step * 16, 16), 16)

    def probe_copy(m):
        return pltpu.make_async_copy(probe_hbm.at[m], probe.at[m], probe_sem.at[m])

    def send_copy(m):
        return pltpu.make_async_copy(terms_out.at[m, 1 - core], send_hbm.at[m], out_sem.at[m])

    def keep_copy(m):
        return pltpu.make_async_copy(terms_out.at[m, core], keep_hbm.at[m], out_sem.at[4 + m])

    amp_copy = pltpu.make_async_copy(amp_hbm, amp, amp_sem)
    for m in range(4):
        probe_copy(m).start()
    amp_copy.start()

    blocks = [slice(k * 128, (k + 1) * 128) for k in range(4)]
    lane_blocks = [(part, k, blocks[k]) for part in range(2) for k in range(4)]

    def stack_rows(step):
        for part, k, lanes in lane_blocks:
            for h, ref in enumerate((own0_ref, own1_ref, below0_ref, below1_ref)):
                tall[part, k, rows16(step, h * HALF), :] = ref[part, rows16(step), lanes].astype(F32)

    loop(HALF // 16, stack_rows, 2)
    lane16 = lax.broadcasted_iota(jnp.int32, (16, 128), 1)

    def take_rows(step):
        for part in range(2):
            turned = []
            for k in range(4):
                value = tall[part, (turn_block + k) % 4, pl.ds(row_start + step * 16, 16), :]
                turned.append(pltpu.roll(value, (128 - turn) % 128, 1))
            for k, lanes in enumerate(blocks):
                value = jnp.where(lane16 < 128 - turn, turned[k], turned[(k + 1) % 4])
                patch[part, rows16(step), lanes] = value

    loop(W // 16, take_rows, 4)

    def exit_fold(m, quarter):
        for step in (quarter * 2, quarter * 2 + 1):
            for lanes in blocks:
                parts = []
                for q in range(4):
                    rows = rows16(step, q * Q)
                    pr = probe[m, 0, rows, lanes].astype(F32)
                    pi = probe[m, 1, rows, lanes].astype(F32)
                    xr, xi = patch[0, rows, lanes], patch[1, rows, lanes]
                    er = (pr * xr - pi * xi).astype(BF16).astype(F32)
                    ei = (pr * xi + pi * xr).astype(BF16).astype(F32)
                    parts.append((er, ei))
                for r, (zr, zi) in enumerate(fold(parts, 1)):
                    folded[m % 2][r, rows16(step), lanes] = zr.astype(BF16)
                    folded[m % 2][r, rows16(step, Q), lanes] = zi.astype(BF16)

    def column_fold(m, r):
        for step in range(Q // 16):
            parts = []
            for lanes in blocks:
                yr = mid[m % 2][r, rows16(step), lanes].astype(BF16).astype(F32)
                yi = mid[m % 2][r, rows16(step, Q), lanes].astype(BF16).astype(F32)
                parts.append((yr, yi))
            for c, (wr, wi) in enumerate(fold(parts, 1)):
                wide[m % 2][c, rows16(step, r * Q), 0:128] = wr.astype(BF16)
                wide[m % 2][c, rows16(step, r * Q), 128:256] = wi.astype(BF16)

    def forward_step(tick, i):
        if tick < 4:
            exit_fold(tick, i)
        if 0 <= tick - 1 < 4:
            mid[(tick - 1) % 2][i] = dot(forward_ref[i], folded[(tick - 1) % 2][i])
        if 0 <= tick - 2 < 4:
            column_fold(tick - 2, i)
        if 0 <= tick - 3 < 4:
            far[tick - 3, i] = dot(wide[(tick - 3) % 2][i], adjoint_ref[i])

    for tick in range(7):
        if tick < 4:
            probe_copy(tick).wait()
        [forward_step(tick, i) for i in range(4)]

    amp_copy.wait()

    def residual(step):
        r, inner = step // 8, step % 8
        rows = rows16(step)
        for c, lanes in enumerate(blocks):
            fields = [(far[m, c, rows, 0:128], far[m, c, rows, 128:256]) for m in range(4)]
            intensity = sum(fr * fr + fi * fi for fr, fi in fields)
            ratio = live * (1.0 - amp[rows, lanes] * lax.rsqrt(jnp.maximum(intensity, 0.25)))
            for m, (fr, fi) in enumerate(fields):
                waves[m, r, rows16(inner), lanes] = (fr * ratio).astype(BF16)
                waves[m, r, rows16(inner, Q), lanes] = (fi * ratio).astype(BF16)

    loop(W // 16, residual, 2)

    def row_unfold(m, c):
        lanes = blocks[c]
        for step in range(Q // 16):
            parts = [
                (mid[m % 2][r, rows16(step), lanes], mid[m % 2][r, rows16(step, Q), lanes])
                for r in range(4)
            ]
            for q, (yr, yi) in enumerate(fold(parts, -1)):
                wide[m % 2][c, rows16(step, q * Q), 0:128] = yr.astype(BF16)
                wide[m % 2][c, rows16(step, q * Q), 128:256] = yi.astype(BF16)

    upper8 = lax.broadcasted_iota(jnp.int32, (8, 128), 0) < 4

    def by_core(value):
        pieces = [value[k * 8 : k * 8 + 8] for k in range(4)]
        turned = [pltpu.roll(piece, 4, 0) for piece in pieces]
        first = [jnp.where(upper8, pieces[k], turned[k + 1]) for k in (0, 2)]
        second = [jnp.where(upper8, turned[k], pieces[k + 1]) for k in (0, 2)]
        return [jnp.concatenate(half, axis=0).astype(BF16) for half in (first, second)]

    def terms(m, quarter):
        for step in range(4):
            start = quarter * 128 + step * 32
            rows, short = slice(start, start + 32), slice(start // 2, start // 2 + 16)
            parts = [(far[m, c, rows, 0:128], far[m, c, rows, 128:256]) for c in range(4)]
            for lanes, (gr, gi) in zip(blocks, fold(parts, -1)):
                pr = probe[m, 0, rows, lanes].astype(F32)
                pi = probe[m, 1, rows, lanes].astype(F32)
                object_r, object_i = pr * gr + pi * gi, pr * gi - pi * gr
                if m:
                    object_r = object_r + object_sum[0, rows, lanes]
                    object_i = object_i + object_sum[1, rows, lanes]
                object_sum[0, rows, lanes] = object_r
                object_sum[1, rows, lanes] = object_i
                xr, xi = patch[0, rows, lanes], patch[1, rows, lanes]
                for part, term in enumerate((xr * gr + xi * gi, xr * gi - xi * gr)):
                    for half, value in enumerate(by_core(term)):
                        terms_out[m, half, part, short, lanes] = value

    def adjoint_step(tick, i):
        if tick < 4:
            mid[tick % 2][i] = dot(adjoint_ref[i], waves[tick, i])
        if 0 <= tick - 1 < 4:
            row_unfold(tick - 1, i)
        if 0 <= tick - 2 < 4:
            far[tick - 2, i] = dot(wide[(tick - 2) % 2][i], forward_ref[i])
        if 0 <= tick - 3 < 4:
            terms(tick - 3, i)

    for tick in range(7):
        [adjoint_step(tick, i) for i in range(4)]
        if tick >= 3:
            send_copy(tick - 3).start()
            keep_copy(tick - 3).start()

    def clear(step):
        for part, k, lanes in lane_blocks:
            tall[part, k, rows16(step), :] = jnp.zeros((16, 128), F32)
            tall[part, k, rows16(step, W), :] = jnp.zeros((16, 128), F32)

    loop(W // 16, clear, 2)

    def put_rows(step):
        for part in range(2):
            turned = [pltpu.roll(object_sum[part, rows16(step), lanes], turn, 1) for lanes in blocks]
            for k in range(4):
                value = jnp.where(lane16 < turn, turned[(k + 3) % 4], turned[k])
                tall[part, (turn_block + k) % 4, pl.ds(row_start + step * 16, 16), :] = value

    loop(W // 16, put_rows, 4)

    def split_rows(step):
        rows = rows16(step)
        for part, k, lanes in lane_blocks:
            up_ref[part, rows, lanes] = tall[part, k, rows, :].astype(BF16)
            low_ref[part, rows, lanes] = tall[part, k, rows16(step, W), :].astype(BF16)

    loop(W // 16, split_rows, 2)
    for m in range(4):
        send_copy(m).wait()
        keep_copy(m).wait()


def wave(info, own0, own1, below0, below1, probe, amp):
    tables = [jnp.asarray(t) for t in block_tables()]
    vmem = pl.BlockSpec(memory_space=pltpu.VMEM)
    hbm = pl.BlockSpec(memory_space=pl.ANY)
    return pl.pallas_call(
        wave_kernel,
        out_shape=(
            jax.ShapeDtypeStruct((2, W, W), BF16),
            jax.ShapeDtypeStruct((2, W, W), BF16),
            jax.ShapeDtypeStruct((4, 2, HALF, W), BF16),
            jax.ShapeDtypeStruct((4, 2, HALF, W), BF16),
        ),
        in_specs=[pl.BlockSpec(memory_space=pltpu.SMEM), vmem, vmem, vmem, vmem, hbm, hbm, vmem, vmem],
        out_specs=(vmem, vmem, hbm, hbm),
        scratch_shapes=[
            pltpu.VMEM((2, 4, 2 * W, 128), F32),
            pltpu.VMEM((2, W, W), F32),
            pltpu.VMEM((4, 256, W), BF16),
            pltpu.VMEM((4, 256, W), BF16),
            pltpu.VMEM((4, 256, W), F32),
            pltpu.VMEM((4, 256, W), F32),
            pltpu.VMEM((4, W, 256), BF16),
            pltpu.VMEM((4, W, 256), BF16),
            pltpu.VMEM((4, 4, W, 256), F32),
            pltpu.VMEM((4, 4, 256, W), BF16),
            pltpu.VMEM((4, 2, W, W), BF16),
            pltpu.VMEM((W, W), F32),
            pltpu.VMEM((4, 2, 2, HALF, W), BF16),
            pltpu.VMEM((2, W, W), F32),
            pltpu.SemaphoreType.DMA((4,)),
            pltpu.SemaphoreType.DMA,
            pltpu.SemaphoreType.DMA((8,)),
        ],
        compiler_params=pltpu.CompilerParams(vmem_limit_bytes=54 * MIB),
        cost_estimate=pl.CostEstimate(flops=20 * 10**9, bytes_accessed=20 * MIB, transcendentals=W * W),
        name="wave",
    )(info, own0, own1, below0, below1, probe, amp, *tables)


def second_kernel(starts_ref, up_ref, above_ref, out_ref):
    masks = []
    for block in range(4):
        lane = lane_index(block, 16)
        for source in range(2):
            start = starts_ref[source]
            masks.append(jnp.logical_and(lane < start, lane >= start - W))

    def body(rows):
        for part in range(2):
            for block in range(4):
                lanes = slice(block * 128, block * 128 + 128)
                own = jnp.where(masks[block * 2], up_ref[part, rows, lanes].astype(F32), 0.0)
                above = above_ref[part, rows, lanes].astype(F32)
                out_ref[part, rows, lanes] = own + jnp.where(masks[block * 2 + 1], above, 0.0)

    row_steps(out_ref.shape[1], 16, body, 2)


def first_kernel(starts_ref, up_ref, above_ref, left_ref, tile_ref, after_ref, out_ref):
    masks = [lane_index(block, 16) >= starts_ref[source] for block in range(4) for source in range(2)]

    def body(rows):
        for part in range(2):
            for block in range(4):
                lanes = slice(block * 128, block * 128 + 128)
                own = jnp.where(masks[block * 2], up_ref[part, rows, lanes].astype(F32), 0.0)
                above = jnp.where(masks[block * 2 + 1], above_ref[part, rows, lanes].astype(F32), 0.0)
                out_ref[part, rows, lanes] = own + above + left_ref[part, rows, lanes].astype(F32)

    row_steps(out_ref.shape[1], 16, body, 2)


def finish(starts, up, above, left, after):
    size = 128
    smem = pl.BlockSpec(memory_space=pltpu.SMEM)
    part = pl.BlockSpec((2, size, W), lambda i: (0, i, 0))
    keep = pl.BlockSpec(memory_space=pl.ANY)
    call = functools.partial(
        pl.pallas_call,
        grid=(W // size,),
        out_shape=jax.ShapeDtypeStruct((2, W, 2 * W), F32),
        compiler_params=pltpu.CompilerParams(vmem_limit_bytes=16 * MIB),
        cost_estimate=pl.CostEstimate(flops=4 * MIB, bytes_accessed=8 * MIB, transcendentals=0),
    )
    tile = call(
        second_kernel,
        in_specs=[smem, part, part],
        out_specs=pl.BlockSpec((2, size, W), lambda i: (0, i, 1)),
        name="second_half",
    )(starts, up, above)
    return call(
        first_kernel,
        in_specs=[smem, part, part, part, keep, keep],
        out_specs=part,
        input_output_aliases={4: 0},
        name="first_half",
    )(starts, up, above, left, tile, after)


def chip_sum_kernel(keep_ref, got_ref, out_ref):
    upper = lax.broadcasted_iota(jnp.int32, (8, W), 0) < 4

    def body(rows):
        short = pl.ds(pl.multiple_of(rows.start // 4, 16), 16)
        for mode in range(4):
            for part in range(2):
                total = keep_ref[mode, part, rows, :].astype(F32) + got_ref[mode, part, rows, :].astype(F32)
                pieces = [total[k * 8 : k * 8 + 8] for k in range(8)]
                turned = [pltpu.roll(piece, 4, 0) for piece in pieces]
                for x in range(4):
                    group = []
                    for k in (x // 2, x // 2 + 4):
                        if x % 2 == 0:
                            group.append(jnp.where(upper, pieces[k], turned[k + 2]))
                        else:
                            group.append(jnp.where(upper, turned[k], pieces[k + 2]))
                    out_ref[x, mode, part, short, :] = jnp.concatenate(group, axis=0).astype(BF16)

    row_steps(keep_ref.shape[2], 64, body)


def chip_sum(keep, got):
    spec = pl.BlockSpec((4, 2, 64, W), lambda i: (0, 0, i, 0))
    return pl.pallas_call(
        chip_sum_kernel,
        grid=(4,),
        out_shape=jax.ShapeDtypeStruct((4, 4, 2, 64, W), BF16),
        in_specs=[spec, spec],
        out_specs=pl.BlockSpec((4, 4, 2, 16, W), lambda i: (0, 0, 0, i, 0)),
        compiler_params=pltpu.CompilerParams(vmem_limit_bytes=16 * MIB),
        cost_estimate=pl.CostEstimate(flops=WEIGHT, bytes_accessed=6 * MIB, transcendentals=0),
        name="chip_sum",
    )(keep, got)


def row_blocks_kernel(got_ref, out_ref):
    upper = lax.broadcasted_iota(jnp.int32, (8, W), 0) < 4

    def body(rows):
        totals = []
        for mode in range(4):
            for part in range(2):
                totals.append(sum(got_ref[k, mode, part, rows, :].astype(F32) for k in range(4)))
        for half in range(2):
            pieces = [total[half * 8 : half * 8 + 8] for total in totals]
            turned = [pltpu.roll(piece, 4, 0) for piece in pieces]
            for odd in range(2):
                group = []
                for k in range(0, 8, 2):
                    if odd:
                        group.append(jnp.where(upper, turned[k], pieces[k + 1]))
                    else:
                        group.append(jnp.where(upper, pieces[k], turned[k + 1]))
                place = rows.start // 4 + half * 2 + odd
                out_ref[place] = jnp.concatenate(group, axis=0).astype(BF16)

    row_steps(got_ref.shape[3], 16, body)


def row_blocks(got):
    vmem = pl.BlockSpec(memory_space=pltpu.VMEM)
    return pl.pallas_call(
        row_blocks_kernel,
        out_shape=jax.ShapeDtypeStruct((16, 32, W), BF16),
        in_specs=[vmem],
        out_specs=vmem,
        compiler_params=pltpu.CompilerParams(vmem_limit_bytes=16 * MIB),
        cost_estimate=pl.CostEstimate(flops=MIB, bytes_accessed=3 * MIB, transcendentals=0),
        name="row_blocks",
    )(got)


ROW = ("y", "z_hi")
COL = ("z_lo", "x", "core")


def last_sum_kernel(got_ref, out_ref):
    total = sum(got_ref[k].astype(F32) for k in range(got_ref.shape[0]))
    for mode in range(4):
        for part in range(2):
            start = (mode * 2 + part) * 4
            out_ref[mode, part] = total[start : start + 4]


def last_sum(got):
    vmem = pl.BlockSpec(memory_space=pltpu.VMEM)
    return pl.pallas_call(
        last_sum_kernel,
        out_shape=jax.ShapeDtypeStruct((4, 2, 4, W), F32),
        in_specs=[vmem],
        out_specs=vmem,
        compiler_params=pltpu.CompilerParams(vmem_limit_bytes=16 * MIB),
        cost_estimate=pl.CostEstimate(flops=MIB, bytes_accessed=MIB, transcendentals=0),
        name="last_sum",
    )(got)


def chips_sum(send, keep):
    got = lax.ppermute(send, "core", [(0, 1), (1, 0)])
    blocks = chip_sum(keep, got)
    return blocks, lax.all_to_all(blocks, "x", 0, 0, tiled=True)


def rows_sum(blocks):
    got = lax.all_to_all(blocks, ("y", "z_hi", "z_lo"), 0, 0, tiled=True)
    return last_sum(got)


def per_device(object_field, probe_modes, positions, amplitudes, live_slots):
    row, col = lax.axis_index(ROW), lax.axis_index(COL)
    tile_rows, tile_cols = object_field.shape[1:]
    to_left = [(i + 1, i) for i in range(15)]
    to_right = [(i, i + 1) for i in range(15)]
    to_upper = [(i + 1, i) for i in range(7)]
    to_lower = [(i, i + 1) for i in range(7)]
    upper = lax.ppermute(positions, ROW, to_lower)
    right = [lax.ppermute(left_columns(object_field, h, HALF), COL, to_left) for h in range(2)]
    anchor = jnp.reshape(col * tile_cols, (1,)).astype(jnp.int32)
    chosen = [cut_columns(upper, anchor, object_field, right[h], h) for h in range(2)]
    below = [lax.ppermute(chosen[h], ROW, to_upper) for h in range(2)]
    positions, upper, live_slots, chosen[1] = lax.optimization_barrier(
        (positions, upper, live_slots, chosen[1])
    )
    own_start = positions[:, 1] - col * tile_cols
    upper_start = jnp.clip(upper[:, 1] - col * tile_cols, 0, tile_cols - 1)
    row_start = positions[0, 0] - row * tile_rows
    own = [cut_columns(positions, anchor, object_field, right[h], h) for h in range(2)]
    amp = amplitude_parts(amplitudes[0], chosen[1])
    info = jnp.stack([row_start, lax.axis_index("core"), live_slots[0], own_start[0]]).astype(jnp.int32)
    up, low, send, keep = wave(info, *own, *below, probe_modes, amp)
    above = lax.ppermute(low, ROW, to_lower)
    chip_terms, chips_terms = chips_sum(send, keep)
    starts = jnp.concatenate([own_start, upper_start])
    over = overflow(own_start[0], up, upper_start[0], above)
    left = lax.ppermute(over, COL, to_right)
    row_terms = row_blocks(chips_terms)
    probe_grad = rows_sum(row_terms)
    return finish(starts, up, above, left, row_terms), probe_grad


def solution(mesh):
    chips = jax.sharding.Mesh(mesh.devices.reshape(4, 2, 2, 4, 2), ROW + COL)
    slots = ROW + COL
    placed = (P(None, ROW, COL), P(), P(slots, None), P(slots, None, None), P(slots))
    return jax.shard_map(
        per_device,
        mesh=chips,
        in_specs=placed,
        out_specs=(P(None, ROW, COL), P(None, None, slots, None)),
        check_vma=False,
    )
```

time: 142 us -> 128 us (0.901)
  the two profiles are of different devices: /device:TPU:56 before, /device:TPU:0 now
where the time goes in v3:
time: 128 us; the launch traced here: 127 us
  Pallas kernels  39.9 us (31%)
  waiting for transfers between devices  39.5 us (31%)
  starting transfers between devices  32.8 us (26%)
  local copies, waits for them, and re-layouts  9.35 us (7%)
  between operations  3.45 us (3%)
  other arithmetic  2.1 us (2%)
    pallas_call x1, Pallas kernels, wave(): pl.pallas_call(wave_kernel, out_shape=(jax.ShapeDtypeStruct((2, W, W), BF...  19.5 us
    ppermute x2, waiting for transfers between devices, per_device(): below = [lax.ppermute(chosen[h], ROW, to_upper) for h in range(2)]  13 us
    ppermute x1, waiting for transfers between devices, per_device(): above = lax.ppermute(low, ROW, to_lower)  12.4 us
    all_to_all x1, waiting for transfers between devices, chips_sum(): return (blocks, lax.all_to_all(blocks, 'x', 0, 0, tiled=True))  10.6 us
    unnamed x22, local copies, waits for them, and re-layouts  8.13 us
    all_to_all x1, starting transfers between devices, rows_sum(): got = lax.all_to_all(blocks, ('y', 'z_hi', 'z_lo'), 0, 0, tiled=True)  7.63 us
    pallas_call x4, Pallas kernels, cut_columns(): pl.pallas_call(columns_kernel, grid=(1,), out_shape=jax.ShapeDtypeStruct(...  7.25 us
    ppermute x1, starting transfers between devices, per_device(): upper = lax.ppermute(positions, ROW, to_lower)  5.86 us
  transfers between devices with their start and end apart: 10, of which 5 were waited for; matrix products, arithmetic and copies ran while one was open for 3% of the time, Pallas kernels for 15%

profile of v3, /device:TPU:0, one launch (start us, length us, event | category | flops | bytes accessed | tf_op | source)
XLA Modules:
  0.0 127.1 jit_solution(16396257487737711177)
XLA Ops:
  0.6 0.0 copy-start.1
  0.6 1.6 %copy-done.1 = bf16[2,512,1024]{2,1,0:T(8,128)(2,1)S(1)} copy-done((bf16[2,512,1024]{2,1,0:T(8,128)(2,1)S(1)}, bf16[2,512,1024]{2,1,0:T(8,128)(2,1)}, u32[]{:S(2)}) %copy-start.1) | copy-done | bytes 2097176
  2.3 1.4 %collective-permute-start.1 = (bf16[2,256,512]{2,1,0:T(8,128)(2,1)S(1)}, bf16[2,256,512]{2,1,0:T(8,128)(2,1)}, u32[]{:S(2)}, u32[]{:S(2)}) collective-permute-start(bf16[2,256,512]{2,1,0:T(8,128)(2,1)S(1)} %left_columns.2), channel_id=1, source_target_pairs={{1,0},{2,1},{3,2},{4,3},{5,4},{6,5},{7,6},{8,7},{9,8},{10,9},{11,1... | collective-permute-start | bytes 1572872 | tf_op jit(solution)/shard_map/ppermute | solution.py:570
  3.7 0.0 copy-done.7
  3.7 5.9 %collective-permute-start = (s32[1,2]{1,0:T(1,128)S(1)}, s32[1,2]{1,0:T(1,128)S(1)}, u32[]{:S(2)}, u32[]{:S(2)}) collective-permute-start(s32[1,2]{1,0:T(1,128)S(1)} %copy-done.7), channel_id=1, source_target_pairs={{0,16},{16,32},{32,48},{48,64},{64,80},{80,96},{96,112},{1,17},{17... | collective-permute-start | bytes 32 | tf_op jit(solution)/shard_map/ppermute | solution.py:569
  9.6 1.3 %collective-permute-start.2 = (bf16[2,256,512]{2,1,0:T(8,128)(2,1)S(1)}, bf16[2,256,512]{2,1,0:T(8,128)(2,1)}, u32[]{:S(2)}, u32[]{:S(2)}) collective-permute-start(bf16[2,256,512]{2,1,0:T(8,128)(2,1)S(1)} %left_columns.3), channel_id=1, source_target_pairs={{1,0},{2,1},{3,2},{4,3},{5,4},{6,5},{7,6},{8,7},{9,8},{10,9},{11,1... | collective-permute-start | bytes 1572872 | tf_op jit(solution)/shard_map/ppermute | solution.py:570
  11.6 0.0 collective-permute-done.corner_ref
  11.6 0.0 collective-permute-done.1.right_ref
  11.6 0.0 copy-done.2
  11.6 2.2 %cut_columns.4.after_ref = bf16[2,256,512]{2,1,0:T(8,128)(2,1)} custom-call(s32[1,2]{1,0:T(1,128)S(1)} %collective-permute-done.corner_ref, s32[1]{0:T(128)} %bitcast.anchor_ref, bf16[2,512,1024]{2,1,0:T(8,128)(2,1)S(1)} %copy-done.2, bf16[2,256,512]{2,1,0:T(8,128)(2,1)} %collective-permute-done.1.right_ref), custom_call_target="tpu_custom_call" | custom-call | flops 99999997952 | bytes 2097152 | tf_op jit(solution)/shard_map/cut_columns/pallas_call | solution.py:122
  13.8 1.3 %collective-permute-start.4 = (bf16[2,256,512]{2,1,0:T(8,128)(2,1)}, bf16[2,256,512]{2,1,0:T(8,128)(2,1)}, u32[]{:S(2)}, u32[]{:S(2)}) collective-permute-start(bf16[2,256,512]{2,1,0:T(8,128)(2,1)} %cut_columns.4.after_ref), channel_id=1, source_target_pairs={{16,0},{32,16},{48,32},{64,48},{80,64},{96,80},{112,96},{17,1},{33... | collective-permute-start | bytes 1572872 | tf_op jit(solution)/shard_map/ppermute | solution.py:573
  15.1 0.0 collective-permute-done.2.right_ref
  15.1 2.2 %cut_columns.7 = bf16[2,256,512]{2,1,0:T(8,128)(2,1)} custom-call(s32[1,2]{1,0:T(1,128)S(1)} %collective-permute-done.corner_ref, s32[1]{0:T(128)} %bitcast.anchor_ref, bf16[2,512,1024]{2,1,0:T(8,128)(2,1)S(1)} %copy-done.2, bf16[2,256,512]{2,1,0:T(8,128)(2,1)} %collective-permute-done.2.right_ref), custom_call_target="tpu_custom_call" | custom-call | flops 99999997952 | bytes 2097152 | tf_op jit(solution)/shard_map/cut_columns/pallas_call | solution.py:122
  17.3 1.3 %collective-permute-start.3 = (bf16[2,256,512]{2,1,0:T(8,128)(2,1)}, bf16[2,256,512]{2,1,0:T(8,128)(2,1)}, u32[]{:S(2)}, u32[]{:S(2)}) collective-permute-start(bf16[2,256,512]{2,1,0:T(8,128)(2,1)} %cut_columns.7), channel_id=1, source_target_pairs={{16,0},{32,16},{48,32},{64,48},{80,64},{96,80},{112,96},{17,1},{33... | collective-permute-start | bytes 1572872 | tf_op jit(solution)/shard_map/ppermute | solution.py:573
  18.6 1.4 %cut_columns.5.own0_ref = bf16[2,256,512]{2,1,0:T(8,128)(2,1)S(1)} custom-call(s32[1,2]{1,0:T(1,128)S(1)} %copy-done.7, s32[1]{0:T(128)} %bitcast.anchor_ref, bf16[2,512,1024]{2,1,0:T(8,128)(2,1)S(1)} %copy-done.2, bf16[2,256,512]{2,1,0:T(8,128)(2,1)} %collective-permute-done.2.right_ref), custom_call_target="tpu_custom_call" | custom-call | flops 99999997952 | bytes 2097152 | tf_op jit(solution)/shard_map/cut_columns/pallas_call | solution.py:122
  20.0 0.8 copy-done.9
  20.8 1.5 %cut_columns.6.own1_ref = bf16[2,256,512]{2,1,0:T(8,128)(2,1)S(1)} custom-call(s32[1,2]{1,0:T(1,128)S(1)} %copy-done.7, s32[1]{0:T(128)} %bitcast.anchor_ref, bf16[2,512,1024]{2,1,0:T(8,128)(2,1)S(1)} %copy-done.2, bf16[2,256,512]{2,1,0:T(8,128)(2,1)} %collective-permute-done.1.right_ref), custom_call_target="tpu_custom_call" | custom-call | flops 99999997952 | bytes 2097152 | tf_op jit(solution)/shard_map/cut_columns/pallas_call | solution.py:122
  22.3 0.8 copy-done.10
  23.1 0.6 fusion
  25.0 0.0 copy-start.6
  25.0 1.0 copy-done.6
  26.0 1.9 %amplitude_parts.1.amp_hbm = f32[512,512]{1,0:T(8,128)S(1)} custom-call(f32[512,512]{1,0:T(8,128)S(1)} %bitcast.9, bf16[512,512]{1,0:T(8,128)(2,1)S(1)} %copy-done.6, bf16[2,256,512]{2,1,0:T(8,128)(2,1)} %cut_columns.4.after_ref), custom_call_target="tpu_custom_call" | custom-call | flops 805306368 | bytes 3145728 | tf_op jit(solution)/shard_map/amplitude_parts/pallas_call | solution.py:73
  27.9 1.0 copy-done.5
  28.9 0.7 pad_add_fusion.1.info_ref
  29.5 1.7 %collective-permute-done.4.below1_ref = bf16[2,256,512]{2,1,0:T(8,128)(2,1)} collective-permute-done((bf16[2,256,512]{2,1,0:T(8,128)(2,1)}, bf16[2,256,512]{2,1,0:T(8,128)(2,1)}, u32[]{:S(2)}, u32[]{:S(2)}) %collective-permute-start.4) | collective-permute-done | bytes 524320 | tf_op jit(solution)/shard_map/ppermute | solution.py:573
  31.3 11.2 %collective-permute-done.3.below0_ref = bf16[2,256,512]{2,1,0:T(8,128)(2,1)} collective-permute-done((bf16[2,256,512]{2,1,0:T(8,128)(2,1)}, bf16[2,256,512]{2,1,0:T(8,128)(2,1)}, u32[]{:S(2)}, u32[]{:S(2)}) %collective-permute-start.3) | collective-permute-done | bytes 524320 | tf_op jit(solution)/shard_map/ppermute | solution.py:573
  42.5 19.5 %wave.1 = (bf16[2,512,512]{2,1,0:T(8,128)(2,1)}, bf16[2,512,512]{2,1,0:T(8,128)(2,1)}, bf16[4,2,256,512]{3,2,1,0:T(8,128)(2,1)}, bf16[4,2,256,512]{3,2,1,0:T(8,128)(2,1)}) custom-call(s32[4]{0:T(128)} %pad_add_fusion.1.info_ref, bf16[2,256,512]{2,1,0:T(8,128)(2,1)} %copy-done.9, bf16[2,256,512]{2,1,0:T(8,128)(2,1)} %copy-done.10, ...), custom_call_target="tpu_custom_call" | custom-call | flops 20000000000 | bytes 20971520 | tf_op jit(solution)/shard_map/wave/pallas_call | solution.py:358
  62.0 0.9 collective-permute-start.7
  62.9 5.9 %collective-permute-start.5 = (bf16[2,512,512]{2,1,0:T(8,128)(2,1)}, bf16[2,512,512]{2,1,0:T(8,128)(2,1)S(1)}, u32[]{:S(2)}, u32[]{:S(2)}) collective-permute-start(bf16[2,512,512]{2,1,0:T(8,128)(2,1)} %get-tuple-element.15), channel_id=1, source_target_pairs={{0,16},{16,32},{32,48},{48,64},{64,80},{80,96},{96,112},{1,17},{17... | collective-permute-start | bytes 3145736 | tf_op jit(solution)/shard_map/ppermute | solution.py:584
  68.8 0.0 collective-permute-done.7.got_ref
  68.8 1.6 %copy-done.8 = bf16[4,2,256,512]{3,2,1,0:T(8,128)(2,1)S(1)} copy-done((bf16[4,2,256,512]{3,2,1,0:T(8,128)(2,1)S(1)}, bf16[4,2,256,512]{3,2,1,0:T(8,128)(2,1)}, u32[]{:S(2)}) %copy-start.8) | copy-done | bytes 2097176
  70.4 1.2 chip_sum.1
  71.6 0.0 copy-start.3
  71.7 1.3 %copy-done.3 = bf16[4,4,2,64,512]{4,3,2,1,0:T(8,128)(2,1)} copy-done((bf16[4,4,2,64,512]{4,3,2,1,0:T(8,128)(2,1)}, bf16[4,4,2,64,512]{4,3,2,1,0:T(8,128)(2,1)S(1)}, u32[]{:S(2)}) %copy-start.3) | copy-done | bytes 2097176
  73.0 5.0 %all-to-all-start = ((bf16[4,4,2,64,512]{4,3,2,1,0:T(8,128)(2,1)}), bf16[4,4,2,64,512]{4,3,2,1,0:T(8,128)(2,1)}, u32[]{:S(2)}, u32[]{:S(2)}) async-start(bf16[4,4,2,64,512]{4,3,2,1,0:T(8,128)(2,1)} %copy-done.3), calls=%async_computation | async-start | bytes 4194304 | tf_op jit(solution)/shard_map/all_to_all | solution.py:554
  78.0 0.6 slice.10
  79.3 12.4 %collective-permute-done.5.above_ref = bf16[2,512,512]{2,1,0:T(8,128)(2,1)S(1)} collective-permute-done((bf16[2,512,512]{2,1,0:T(8,128)(2,1)}, bf16[2,512,512]{2,1,0:T(8,128)(2,1)S(1)}, u32[]{:S(2)}, u32[]{:S(2)}) %collective-permute-start.5) | collective-permute-done | bytes 1048608 | tf_op jit(solution)/shard_map/ppermute | solution.py:584
  91.6 1.4 %add_convert_fusion = bf16[2,512,512]{2,1,0:T(8,128)(2,1)} fusion(bf16[2,512,512]{2,1,0:T(8,128)(2,1)S(1)} %collective-permute-done.5.above_ref, bf16[2,512,512]{2,1,0:T(8,128)(2,1)S(1)} %copy-done, pred[512]{0:T(512)(128)(4,1)S(1)} %get-tuple-element.20, pred[512]{0:T(512)(128)(4,1)S(1)} %get-tuple-element.21), kind=kLoop, calls=%fused_computation | loop fusion | flops 3145728 | bytes 3146752 | tf_op jit(solution)/shard_map/convert_element_type | solution.py:87
  93.0 2.3 %collective-permute-start.6 = (bf16[2,512,512]{2,1,0:T(8,128)(2,1)}, bf16[2,512,512]{2,1,0:T(8,128)(2,1)}, u32[]{:S(2)}, u32[]{:S(2)}) collective-permute-start(bf16[2,512,512]{2,1,0:T(8,128)(2,1)} %add_convert_fusion), channel_id=1, source_target_pairs={{0,1},{1,2},{2,3},{3,4},{4,5},{5,6},{6,7},{7,8},{8,9},{9,10},{10,1... | collective-permute-start | bytes 3145736 | tf_op jit(solution)/shard_map/ppermute | solution.py:588
  95.3 10.6 %all-to-all-done.got_ref = bf16[4,4,2,64,512]{4,3,2,1,0:T(8,128)(2,1)} async-done(((bf16[4,4,2,64,512]{4,3,2,1,0:T(8,128)(2,1)}), bf16[4,4,2,64,512]{4,3,2,1,0:T(8,128)(2,1)}, u32[]{:S(2)}, u32[]{:S(2)}) %all-to-all-start) | async-done | bytes 2097184 | tf_op jit(solution)/shard_map/all_to_all | solution.py:554
  105.9 2.7 %row_blocks.1.after_ref = bf16[16,32,512]{2,1,0:T(8,128)(2,1)} custom-call(bf16[4,4,2,64,512]{4,3,2,1,0:T(8,128)(2,1)} %all-to-all-done.got_ref), custom_call_target="tpu_custom_call" | custom-call | flops 1048576 | bytes 3145728 | tf_op jit(solution)/shard_map/row_blocks/pallas_call | solution.py:515
  108.6 7.6 %all-to-all-start.1 = ((bf16[16,32,512]{2,1,0:T(8,128)(2,1)}), bf16[16,32,512]{2,1,0:T(8,128)(2,1)S(1)}, u32[]{:S(2)}, u32[]{:S(2)}) async-start(bf16[16,32,512]{2,1,0:T(8,128)(2,1)} %row_blocks.1.after_ref), calls=%async_computation.1 | async-start | bytes 1048576 | tf_op jit(solution)/shard_map/all_to_all | solution.py:558
  116.3 0.1 pad_add_fusion.starts_ref
  116.3 2.7 %second_half.1.tile_ref = f32[2,512,1024]{2,1,0:T(8,128)} custom-call(s32[2]{0:T(128)S(1)} %pad_add_fusion.starts_ref, bf16[2,512,512]{2,1,0:T(8,128)(2,1)S(1)} %copy-done, bf16[2,512,512]{2,1,0:T(8,128)(2,1)S(1)} %collective-permute-done.5.above_ref), custom_call_target="tpu_custom_call" | custom-call | flops 4194304 | bytes 8388608 | tf_op jit(solution)/shard_map/second_half/pallas_call | solution.py:438
  119.0 0.0 collective-permute-done.6.left_ref
  119.0 3.9 %first_half.1 = f32[2,512,1024]{2,1,0:T(8,128)} custom-call(s32[2]{0:T(128)S(1)} %pad_add_fusion.starts_ref, bf16[2,512,512]{2,1,0:T(8,128)(2,1)S(1)} %copy-done, bf16[2,512,512]{2,1,0:T(8,128)(2,1)S(1)} %collective-permute-done.5.above_ref, bf16[2,512,512]{2,1,0:T(8,128)(2,1)} %collective-permute-done.6.left_ref, ...), custom_call_target="tpu_custom_call", output_to_operand_aliasing={{}: (4, {})} | custom-call | flops 4194304 | bytes 8388608 | tf_op jit(solution)/shard_map/first_half/pallas_call | solution.py:444
  122.9 3.5 %all-to-all-done.1.got_ref = bf16[16,32,512]{2,1,0:T(8,128)(2,1)S(1)} async-done(((bf16[16,32,512]{2,1,0:T(8,128)(2,1)}), bf16[16,32,512]{2,1,0:T(8,128)(2,1)S(1)}, u32[]{:S(2)}, u32[]{:S(2)}) %all-to-all-start.1) | async-done | bytes 524320 | tf_op jit(solution)/shard_map/all_to_all | solution.py:558
  126.4 0.7 last_sum.1
  (13 shorter events, 0.1 us)
Async XLA Ops:
  0.6 1.6 %copy-start.1 = (bf16[2,512,1024]{2,1,0:T(8,128)(2,1)S(1)}, bf16[2,512,1024]{2,1,0:T(8,128)(2,1)}, u32[]{:S(2)}) copy-start(bf16[2,512,1024]{2,1,0:T(8,128)(2,1)} %tile_ref.11) | copy-start | bytes 6291460
  2.2 1.5 %copy-start.7 = (s32[1,2]{1,0:T(1,128)S(1)}, s32[1,2]{1,0:T(1,128)}, u32[]{:S(2)}) copy-start(s32[1,2]{1,0:T(1,128)} %corner_ref.1) | copy-start | bytes 28
  2.2 9.4 %copy-start.2 = (bf16[2,512,1024]{2,1,0:T(8,128)(2,1)S(1)}, bf16[2,512,1024]{2,1,0:T(8,128)(2,1)}, u32[]{:S(2)}) copy-start(bf16[2,512,1024]{2,1,0:T(8,128)(2,1)} %tile_ref.11) | copy-start | bytes 6291460
  2.3 9.3 %collective-permute-start.1 = (bf16[2,256,512]{2,1,0:T(8,128)(2,1)S(1)}, bf16[2,256,512]{2,1,0:T(8,128)(2,1)}, u32[]{:S(2)}, u32[]{:S(2)}) collective-permute-start(bf16[2,256,512]{2,1,0:T(8,128)(2,1)S(1)} %left_columns.2), channel_id=1, source_target_pairs={{1,0},{2,1},{3,2},{4,3},{5,4},{6,5},{7,6},{8,7},{9,8},{10,9},{11,1... | collective-permute-start | bytes 1572872 | tf_op jit(solution)/shard_map/ppermute | solution.py:570
  3.7 7.9 %collective-permute-start = (s32[1,2]{1,0:T(1,128)S(1)}, s32[1,2]{1,0:T(1,128)S(1)}, u32[]{:S(2)}, u32[]{:S(2)}) collective-permute-start(s32[1,2]{1,0:T(1,128)S(1)} %copy-done.7), channel_id=1, source_target_pairs={{0,16},{16,32},{32,48},{48,64},{64,80},{80,96},{96,112},{1,17},{17... | collective-permute-start | bytes 32 | tf_op jit(solution)/shard_map/ppermute | solution.py:569
  9.6 5.5 %collective-permute-start.2 = (bf16[2,256,512]{2,1,0:T(8,128)(2,1)S(1)}, bf16[2,256,512]{2,1,0:T(8,128)(2,1)}, u32[]{:S(2)}, u32[]{:S(2)}) collective-permute-start(bf16[2,256,512]{2,1,0:T(8,128)(2,1)S(1)} %left_columns.3), channel_id=1, source_target_pairs={{1,0},{2,1},{3,2},{4,3},{5,4},{6,5},{7,6},{8,7},{9,8},{10,9},{11,1... | collective-permute-start | bytes 1572872 | tf_op jit(solution)/shard_map/ppermute | solution.py:570
  13.8 17.5 %collective-permute-start.4 = (bf16[2,256,512]{2,1,0:T(8,128)(2,1)}, bf16[2,256,512]{2,1,0:T(8,128)(2,1)}, u32[]{:S(2)}, u32[]{:S(2)}) collective-permute-start(bf16[2,256,512]{2,1,0:T(8,128)(2,1)} %cut_columns.4.after_ref), channel_id=1, source_target_pairs={{16,0},{32,16},{48,32},{64,48},{80,64},{96,80},{112,96},{17,1},{33... | collective-permute-start | bytes 1572872 | tf_op jit(solution)/shard_map/ppermute | solution.py:573
  17.3 25.2 %collective-permute-start.3 = (bf16[2,256,512]{2,1,0:T(8,128)(2,1)}, bf16[2,256,512]{2,1,0:T(8,128)(2,1)}, u32[]{:S(2)}, u32[]{:S(2)}) collective-permute-start(bf16[2,256,512]{2,1,0:T(8,128)(2,1)} %cut_columns.7), channel_id=1, source_target_pairs={{16,0},{32,16},{48,32},{64,48},{80,64},{96,80},{112,96},{17,1},{33... | collective-permute-start | bytes 1572872 | tf_op jit(solution)/shard_map/ppermute | solution.py:573
  20.0 0.8 copy-start.9
  20.8 4.2 %copy-start.4 = (f32[1,512,512]{2,1,0:T(8,128)S(1)}, f32[1,512,512]{2,1,0:T(8,128)}, u32[]{:S(2)}) copy-start(f32[1,512,512]{2,1,0:T(8,128)} %param.11) | copy-start | bytes 3145732
  22.3 0.8 copy-start.10
  25.0 1.0 copy-start.6
  27.9 1.0 copy-start.5
  62.0 6.8 %collective-permute-start.7 = (bf16[4,2,256,512]{3,2,1,0:T(8,128)(2,1)}, bf16[4,2,256,512]{3,2,1,0:T(8,128)(2,1)S(1)}, u32[]{:S(2)}, u32[]{:S(2)}) collective-permute-start(bf16[4,2,256,512]{3,2,1,0:T(8,128)(2,1)} %get-tuple-element.17), channel_id=1, source_target_pairs={{0,1},{1,0},{2,3},{3,2},{4,5},{5,4},{6,7},{7,6},{8,9},{9,8},{10,11... | collective-permute-start | bytes 6291464 | tf_op jit(solution)/shard_map/ppermute | solution.py:552
  62.9 28.7 %collective-permute-start.5 = (bf16[2,512,512]{2,1,0:T(8,128)(2,1)}, bf16[2,512,512]{2,1,0:T(8,128)(2,1)S(1)}, u32[]{:S(2)}, u32[]{:S(2)}) collective-permute-start(bf16[2,512,512]{2,1,0:T(8,128)(2,1)} %get-tuple-element.15), channel_id=1, source_target_pairs={{0,16},{16,32},{32,48},{48,64},{64,80},{80,96},{96,112},{1,17},{17... | collective-permute-start | bytes 3145736 | tf_op jit(solution)/shard_map/ppermute | solution.py:584
  68.8 1.6 %copy-start.8 = (bf16[4,2,256,512]{3,2,1,0:T(8,128)(2,1)S(1)}, bf16[4,2,256,512]{3,2,1,0:T(8,128)(2,1)}, u32[]{:S(2)}) copy-start(bf16[4,2,256,512]{3,2,1,0:T(8,128)(2,1)} %get-tuple-element.16.keep_ref) | copy-start | bytes 6291460
  71.6 1.3 %copy-start.3 = (bf16[4,4,2,64,512]{4,3,2,1,0:T(8,128)(2,1)}, bf16[4,4,2,64,512]{4,3,2,1,0:T(8,128)(2,1)S(1)}, u32[]{:S(2)}) copy-start(bf16[4,4,2,64,512]{4,3,2,1,0:T(8,128)(2,1)S(1)} %chip_sum.1) | copy-start | bytes 6291460
  73.0 18.7 %copy-start = (bf16[2,512,512]{2,1,0:T(8,128)(2,1)S(1)}, bf16[2,512,512]{2,1,0:T(8,128)(2,1)}, u32[]{:S(2)}) copy-start(bf16[2,512,512]{2,1,0:T(8,128)(2,1)} %get-tuple-element.14.up_ref) | copy-start | bytes 3145732
  73.0 32.9 %all-to-all-start = ((bf16[4,4,2,64,512]{4,3,2,1,0:T(8,128)(2,1)}), bf16[4,4,2,64,512]{4,3,2,1,0:T(8,128)(2,1)}, u32[]{:S(2)}, u32[]{:S(2)}) async-start(bf16[4,4,2,64,512]{4,3,2,1,0:T(8,128)(2,1)} %copy-done.3), calls=%async_computation | async-start | bytes 4194304 | tf_op jit(solution)/shard_map/all_to_all | solution.py:554
  93.0 26.0 %collective-permute-start.6 = (bf16[2,512,512]{2,1,0:T(8,128)(2,1)}, bf16[2,512,512]{2,1,0:T(8,128)(2,1)}, u32[]{:S(2)}, u32[]{:S(2)}) collective-permute-start(bf16[2,512,512]{2,1,0:T(8,128)(2,1)} %add_convert_fusion), channel_id=1, source_target_pairs={{0,1},{1,2},{2,3},{3,4},{4,5},{5,6},{6,7},{7,8},{8,9},{9,10},{10,1... | collective-permute-start | bytes 3145736 | tf_op jit(solution)/shard_map/ppermute | solution.py:588
  108.6 17.8 %all-to-all-start.1 = ((bf16[16,32,512]{2,1,0:T(8,128)(2,1)}), bf16[16,32,512]{2,1,0:T(8,128)(2,1)S(1)}, u32[]{:S(2)}, u32[]{:S(2)}) async-start(bf16[16,32,512]{2,1,0:T(8,128)(2,1)} %row_blocks.1.after_ref), calls=%async_computation.1 | async-start | bytes 1048576 | tf_op jit(solution)/shard_map/all_to_all | solution.py:558

commit v4 on v3

--- a/solution.py
+++ b/solution.py
@@ -423,28 +423,35 @@
     row_steps(out_ref.shape[1], 16, body, 2)
 
 
-def finish(starts, up, above, left, after):
-    size = 128
-    smem = pl.BlockSpec(memory_space=pltpu.SMEM)
-    part = pl.BlockSpec((2, size, W), lambda i: (0, i, 0))
-    keep = pl.BlockSpec(memory_space=pl.ANY)
-    call = functools.partial(
-        pl.pallas_call,
-        grid=(W // size,),
+PART = pl.BlockSpec((2, 128, W), lambda i: (0, i, 0))
+
+
+def tile_call(kernel, **options):
+    return pl.pallas_call(
+        kernel,
+        grid=(4,),
         out_shape=jax.ShapeDtypeStruct((2, W, 2 * W), F32),
         compiler_params=pltpu.CompilerParams(vmem_limit_bytes=16 * MIB),
         cost_estimate=pl.CostEstimate(flops=4 * MIB, bytes_accessed=8 * MIB, transcendentals=0),
+        **options,
     )
-    tile = call(
+
+
+def second_half(starts, up, above):
+    return tile_call(
         second_kernel,
-        in_specs=[smem, part, part],
-        out_specs=pl.BlockSpec((2, size, W), lambda i: (0, i, 1)),
+        in_specs=[pl.BlockSpec(memory_space=pltpu.SMEM), PART, PART],
+        out_specs=pl.BlockSpec((2, 128, W), lambda i: (0, i, 1)),
         name="second_half",
     )(starts, up, above)
-    return call(
+
+
+def first_half(starts, up, above, left, tile, after):
+    keep = pl.BlockSpec(memory_space=pl.ANY)
+    return tile_call(
         first_kernel,
-        in_specs=[smem, part, part, part, keep, keep],
-        out_specs=part,
+        in_specs=[pl.BlockSpec(memory_space=pltpu.SMEM), PART, PART, PART, keep, keep],
+        out_specs=PART,
         input_output_aliases={4: 0},
         name="first_half",
     )(starts, up, above, left, tile, after)
@@ -586,9 +593,11 @@
     starts = jnp.concatenate([own_start, upper_start])
     over = overflow(own_start[0], up, upper_start[0], above)
     left = lax.ppermute(over, COL, to_right)
+    tile = second_half(starts, up, above)
+    chips_terms, tile = lax.optimization_barrier((chips_terms, tile))
     row_terms = row_blocks(chips_terms)
     probe_grad = rows_sum(row_terms)
-    return finish(starts, up, above, left, row_terms), probe_grad
+    return first_half(starts, up, above, left, tile, row_terms), probe_grad
 
 
 def solution(mesh):

time: 128 us -> 128 us (level)
    all_to_all x1, waiting for transfers between devices: 10.6 us -> 7.84 us  [chips_sum(): return (blocks, lax.all_to_all(blocks, 'x', 0, 0, tiled=True))]
    all_to_all x1, waiting for transfers between devices: 3.5 us -> 6.21 us  [rows_sum(): got = lax.all_to_all(blocks, ('y', 'z_hi', 'z_lo'), 0, 0, tiled=True)]
where the time goes in v4:
time: 128 us; the launch traced here: 127 us
  Pallas kernels  39.9 us (31%)
  waiting for transfers between devices  39.5 us (31%)
  starting transfers between devices  32.9 us (26%)
  local copies, waits for them, and re-layouts  9.31 us (7%)
  between operations  3.45 us (3%)
  other arithmetic  2.12 us (2%)
    pallas_call x1, Pallas kernels, wave(): pl.pallas_call(wave_kernel, out_shape=(jax.ShapeDtypeStruct((2, W, W), BF...  19.5 us
    ppermute x2, waiting for transfers between devices, per_device(): below = [lax.ppermute(chosen[h], ROW, to_upper) for h in range(2)]  13 us
    ppermute x1, waiting for transfers between devices, per_device(): above = lax.ppermute(low, ROW, to_lower)  12.4 us
    unnamed x22, local copies, waits for them, and re-layouts  8.09 us
    all_to_all x1, waiting for transfers between devices, chips_sum(): return (blocks, lax.all_to_all(blocks, 'x', 0, 0, tiled=True))  7.84 us
    all_to_all x1, starting transfers between devices, rows_sum(): got = lax.all_to_all(blocks, ('y', 'z_hi', 'z_lo'), 0, 0, tiled=True)  7.63 us
    pallas_call x4, Pallas kernels, cut_columns(): pl.pallas_call(columns_kernel, grid=(1,), out_shape=jax.ShapeDtypeStruct(...  7.25 us
    all_to_all x1, waiting for transfers between devices, rows_sum(): got = lax.all_to_all(blocks, ('y', 'z_hi', 'z_lo'), 0, 0, tiled=True)  6.21 us
  transfers between devices with their start and end apart: 10, of which 5 were waited for; matrix products, arithmetic and copies ran while one was open for 3% of the time, Pallas kernels for 15%

profile of v4, /device:TPU:0, one launch (start us, length us, event | category | flops | bytes accessed | tf_op | source)
XLA Modules:
  0.0 127.2 jit_solution(5097832478722736926)
XLA Ops:
  0.6 0.0 copy-start.1
  0.6 1.6 %copy-done.1 = bf16[2,512,1024]{2,1,0:T(8,128)(2,1)S(1)} copy-done((bf16[2,512,1024]{2,1,0:T(8,128)(2,1)S(1)}, bf16[2,512,1024]{2,1,0:T(8,128)(2,1)}, u32[]{:S(2)}) %copy-start.1) | copy-done | bytes 2097176
  2.3 1.4 %collective-permute-start.1 = (bf16[2,256,512]{2,1,0:T(8,128)(2,1)S(1)}, bf16[2,256,512]{2,1,0:T(8,128)(2,1)}, u32[]{:S(2)}, u32[]{:S(2)}) collective-permute-start(bf16[2,256,512]{2,1,0:T(8,128)(2,1)S(1)} %left_columns.2), channel_id=1, source_target_pairs={{1,0},{2,1},{3,2},{4,3},{5,4},{6,5},{7,6},{8,7},{9,8},{10,9},{11,1... | collective-permute-start | bytes 1572872 | tf_op jit(solution)/shard_map/ppermute | solution.py:577
  3.7 5.9 %collective-permute-start = (s32[1,2]{1,0:T(1,128)S(1)}, s32[1,2]{1,0:T(1,128)S(1)}, u32[]{:S(2)}, u32[]{:S(2)}) collective-permute-start(s32[1,2]{1,0:T(1,128)S(1)} %copy-done.7), channel_id=1, source_target_pairs={{0,16},{16,32},{32,48},{48,64},{64,80},{80,96},{96,112},{1,17},{17... | collective-permute-start | bytes 32 | tf_op jit(solution)/shard_map/ppermute | solution.py:576
  9.6 1.3 %collective-permute-start.2 = (bf16[2,256,512]{2,1,0:T(8,128)(2,1)S(1)}, bf16[2,256,512]{2,1,0:T(8,128)(2,1)}, u32[]{:S(2)}, u32[]{:S(2)}) collective-permute-start(bf16[2,256,512]{2,1,0:T(8,128)(2,1)S(1)} %left_columns.3), channel_id=1, source_target_pairs={{1,0},{2,1},{3,2},{4,3},{5,4},{6,5},{7,6},{8,7},{9,8},{10,9},{11,1... | collective-permute-start | bytes 1572872 | tf_op jit(solution)/shard_map/ppermute | solution.py:577
  11.6 0.0 collective-permute-done.corner_ref
  11.6 0.0 collective-permute-done.1.right_ref
  11.6 0.0 copy-done.2
  11.6 2.2 %cut_columns.4.after_ref = bf16[2,256,512]{2,1,0:T(8,128)(2,1)} custom-call(s32[1,2]{1,0:T(1,128)S(1)} %collective-permute-done.corner_ref, s32[1]{0:T(128)} %bitcast.anchor_ref, bf16[2,512,1024]{2,1,0:T(8,128)(2,1)S(1)} %copy-done.2, bf16[2,256,512]{2,1,0:T(8,128)(2,1)} %collective-permute-done.1.right_ref), custom_call_target="tpu_custom_call" | custom-call | flops 99999997952 | bytes 2097152 | tf_op jit(solution)/shard_map/cut_columns/pallas_call | solution.py:122
  13.8 1.3 %collective-permute-start.4 = (bf16[2,256,512]{2,1,0:T(8,128)(2,1)}, bf16[2,256,512]{2,1,0:T(8,128)(2,1)}, u32[]{:S(2)}, u32[]{:S(2)}) collective-permute-start(bf16[2,256,512]{2,1,0:T(8,128)(2,1)} %cut_columns.4.after_ref), channel_id=1, source_target_pairs={{16,0},{32,16},{48,32},{64,48},{80,64},{96,80},{112,96},{17,1},{33... | collective-permute-start | bytes 1572872 | tf_op jit(solution)/shard_map/ppermute | solution.py:580
  15.1 0.0 collective-permute-done.2.right_ref
  15.1 2.2 %cut_columns.7 = bf16[2,256,512]{2,1,0:T(8,128)(2,1)} custom-call(s32[1,2]{1,0:T(1,128)S(1)} %collective-permute-done.corner_ref, s32[1]{0:T(128)} %bitcast.anchor_ref, bf16[2,512,1024]{2,1,0:T(8,128)(2,1)S(1)} %copy-done.2, bf16[2,256,512]{2,1,0:T(8,128)(2,1)} %collective-permute-done.2.right_ref), custom_call_target="tpu_custom_call" | custom-call | flops 99999997952 | bytes 2097152 | tf_op jit(solution)/shard_map/cut_columns/pallas_call | solution.py:122
  17.3 1.3 %collective-permute-start.3 = (bf16[2,256,512]{2,1,0:T(8,128)(2,1)}, bf16[2,256,512]{2,1,0:T(8,128)(2,1)}, u32[]{:S(2)}, u32[]{:S(2)}) collective-permute-start(bf16[2,256,512]{2,1,0:T(8,128)(2,1)} %cut_columns.7), channel_id=1, source_target_pairs={{16,0},{32,16},{48,32},{64,48},{80,64},{96,80},{112,96},{17,1},{33... | collective-permute-start | bytes 1572872 | tf_op jit(solution)/shard_map/ppermute | solution.py:580
  18.6 1.4 %cut_columns.6.own1_ref = bf16[2,256,512]{2,1,0:T(8,128)(2,1)S(1)} custom-call(s32[1,2]{1,0:T(1,128)S(1)} %copy-done.7, s32[1]{0:T(128)} %bitcast.anchor_ref, bf16[2,512,1024]{2,1,0:T(8,128)(2,1)S(1)} %copy-done.2, bf16[2,256,512]{2,1,0:T(8,128)(2,1)} %collective-permute-done.1.right_ref), custom_call_target="tpu_custom_call" | custom-call | flops 99999997952 | bytes 2097152 | tf_op jit(solution)/shard_map/cut_columns/pallas_call | solution.py:122
  20.0 0.8 copy-done.9
  20.8 1.5 %cut_columns.5.own0_ref = bf16[2,256,512]{2,1,0:T(8,128)(2,1)S(1)} custom-call(s32[1,2]{1,0:T(1,128)S(1)} %copy-done.7, s32[1]{0:T(128)} %bitcast.anchor_ref, bf16[2,512,1024]{2,1,0:T(8,128)(2,1)S(1)} %copy-done.2, bf16[2,256,512]{2,1,0:T(8,128)(2,1)} %collective-permute-done.2.right_ref), custom_call_target="tpu_custom_call" | custom-call | flops 99999997952 | bytes 2097152 | tf_op jit(solution)/shard_map/cut_columns/pallas_call | solution.py:122
  22.3 0.8 copy-done.10
  23.1 0.6 fusion
  25.0 0.0 copy-start.6
  25.0 1.0 copy-done.6
  26.0 1.8 %amplitude_parts.1.amp_hbm = f32[512,512]{1,0:T(8,128)S(1)} custom-call(f32[512,512]{1,0:T(8,128)S(1)} %bitcast.9, bf16[512,512]{1,0:T(8,128)(2,1)S(1)} %copy-done.6, bf16[2,256,512]{2,1,0:T(8,128)(2,1)} %cut_columns.4.after_ref), custom_call_target="tpu_custom_call" | custom-call | flops 805306368 | bytes 3145728 | tf_op jit(solution)/shard_map/amplitude_parts/pallas_call | solution.py:73
  27.9 1.0 copy-done.5
  28.9 0.7 pad_add_fusion.1.info_ref
  29.5 1.8 %collective-permute-done.4.below1_ref = bf16[2,256,512]{2,1,0:T(8,128)(2,1)} collective-permute-done((bf16[2,256,512]{2,1,0:T(8,128)(2,1)}, bf16[2,256,512]{2,1,0:T(8,128)(2,1)}, u32[]{:S(2)}, u32[]{:S(2)}) %collective-permute-start.4) | collective-permute-done | bytes 524320 | tf_op jit(solution)/shard_map/ppermute | solution.py:580
  31.3 11.2 %collective-permute-done.3.below0_ref = bf16[2,256,512]{2,1,0:T(8,128)(2,1)} collective-permute-done((bf16[2,256,512]{2,1,0:T(8,128)(2,1)}, bf16[2,256,512]{2,1,0:T(8,128)(2,1)}, u32[]{:S(2)}, u32[]{:S(2)}) %collective-permute-start.3) | collective-permute-done | bytes 524320 | tf_op jit(solution)/shard_map/ppermute | solution.py:580
  42.5 19.5 %wave.1 = (bf16[2,512,512]{2,1,0:T(8,128)(2,1)}, bf16[2,512,512]{2,1,0:T(8,128)(2,1)}, bf16[4,2,256,512]{3,2,1,0:T(8,128)(2,1)}, bf16[4,2,256,512]{3,2,1,0:T(8,128)(2,1)}) custom-call(s32[4]{0:T(128)} %pad_add_fusion.1.info_ref, bf16[2,256,512]{2,1,0:T(8,128)(2,1)} %copy-done.10, bf16[2,256,512]{2,1,0:T(8,128)(2,1)} %copy-done.9, ...), custom_call_target="tpu_custom_call" | custom-call | flops 20000000000 | bytes 20971520 | tf_op jit(solution)/shard_map/wave/pallas_call | solution.py:358
  62.1 0.9 collective-permute-start.7
  63.0 5.9 %collective-permute-start.5 = (bf16[2,512,512]{2,1,0:T(8,128)(2,1)}, bf16[2,512,512]{2,1,0:T(8,128)(2,1)S(1)}, u32[]{:S(2)}, u32[]{:S(2)}) collective-permute-start(bf16[2,512,512]{2,1,0:T(8,128)(2,1)} %get-tuple-element.17), channel_id=1, source_target_pairs={{0,16},{16,32},{32,48},{48,64},{64,80},{80,96},{96,112},{1,17},{17... | collective-permute-start | bytes 3145736 | tf_op jit(solution)/shard_map/ppermute | solution.py:591
  68.8 0.0 collective-permute-done.7.got_ref
  68.9 0.0 copy-start.8
  68.9 1.6 %copy-done.8 = bf16[4,2,256,512]{3,2,1,0:T(8,128)(2,1)S(1)} copy-done((bf16[4,2,256,512]{3,2,1,0:T(8,128)(2,1)S(1)}, bf16[4,2,256,512]{3,2,1,0:T(8,128)(2,1)}, u32[]{:S(2)}) %copy-start.8) | copy-done | bytes 2097176
  70.5 1.2 chip_sum.1
  71.7 0.0 copy-start.3
  71.7 1.3 %copy-done.3 = bf16[4,4,2,64,512]{4,3,2,1,0:T(8,128)(2,1)} copy-done((bf16[4,4,2,64,512]{4,3,2,1,0:T(8,128)(2,1)}, bf16[4,4,2,64,512]{4,3,2,1,0:T(8,128)(2,1)S(1)}, u32[]{:S(2)}) %copy-start.3) | copy-done | bytes 2097176
  73.0 5.1 %all-to-all-start = ((bf16[4,4,2,64,512]{4,3,2,1,0:T(8,128)(2,1)}), bf16[4,4,2,64,512]{4,3,2,1,0:T(8,128)(2,1)}, u32[]{:S(2)}, u32[]{:S(2)}) async-start(bf16[4,4,2,64,512]{4,3,2,1,0:T(8,128)(2,1)} %copy-done.3), calls=%async_computation | async-start | bytes 4194304 | tf_op jit(solution)/shard_map/all_to_all | solution.py:561
  78.1 0.6 slice.10
  79.3 12.4 %collective-permute-done.5.above_ref = bf16[2,512,512]{2,1,0:T(8,128)(2,1)S(1)} collective-permute-done((bf16[2,512,512]{2,1,0:T(8,128)(2,1)}, bf16[2,512,512]{2,1,0:T(8,128)(2,1)S(1)}, u32[]{:S(2)}, u32[]{:S(2)}) %collective-permute-start.5) | collective-permute-done | bytes 1048608 | tf_op jit(solution)/shard_map/ppermute | solution.py:591
  91.7 1.4 %add_convert_fusion = bf16[2,512,512]{2,1,0:T(8,128)(2,1)} fusion(bf16[2,512,512]{2,1,0:T(8,128)(2,1)S(1)} %collective-permute-done.5.above_ref, bf16[2,512,512]{2,1,0:T(8,128)(2,1)S(1)} %copy-done, pred[512]{0:T(512)(128)(4,1)S(1)} %get-tuple-element.24, pred[512]{0:T(512)(128)(4,1)S(1)} %get-tuple-element.25), kind=kLoop, calls=%fused_computation | loop fusion | flops 3145728 | bytes 3146752 | tf_op jit(solution)/shard_map/convert_element_type | solution.py:87
  93.1 2.3 %collective-permute-start.6 = (bf16[2,512,512]{2,1,0:T(8,128)(2,1)}, bf16[2,512,512]{2,1,0:T(8,128)(2,1)}, u32[]{:S(2)}, u32[]{:S(2)}) collective-permute-start(bf16[2,512,512]{2,1,0:T(8,128)(2,1)} %add_convert_fusion), channel_id=1, source_target_pairs={{0,1},{1,2},{2,3},{3,4},{4,5},{5,6},{6,7},{7,8},{8,9},{9,10},{10,1... | collective-permute-start | bytes 3145736 | tf_op jit(solution)/shard_map/ppermute | solution.py:595
  95.4 0.1 pad_add_fusion.starts_ref
  95.4 2.7 %second_half.1.tile_ref = f32[2,512,1024]{2,1,0:T(8,128)} custom-call(s32[2]{0:T(128)S(1)} %pad_add_fusion.starts_ref, bf16[2,512,512]{2,1,0:T(8,128)(2,1)S(1)} %copy-done, bf16[2,512,512]{2,1,0:T(8,128)(2,1)S(1)} %collective-permute-done.5.above_ref), custom_call_target="tpu_custom_call" | custom-call | flops 4194304 | bytes 8388608 | tf_op jit(solution)/shard_map/second_half/pallas_call | solution.py:441
  98.1 7.8 %all-to-all-done.got_ref = bf16[4,4,2,64,512]{4,3,2,1,0:T(8,128)(2,1)} async-done(((bf16[4,4,2,64,512]{4,3,2,1,0:T(8,128)(2,1)}), bf16[4,4,2,64,512]{4,3,2,1,0:T(8,128)(2,1)}, u32[]{:S(2)}, u32[]{:S(2)}) %all-to-all-start) | async-done | bytes 2097184 | tf_op jit(solution)/shard_map/all_to_all | solution.py:561
  105.9 2.7 %row_blocks.1.after_ref = bf16[16,32,512]{2,1,0:T(8,128)(2,1)} custom-call(bf16[4,4,2,64,512]{4,3,2,1,0:T(8,128)(2,1)} %all-to-all-done.got_ref), custom_call_target="tpu_custom_call" | custom-call | flops 1048576 | bytes 3145728 | tf_op jit(solution)/shard_map/row_blocks/pallas_call | solution.py:522
  108.6 7.6 %all-to-all-start.1 = ((bf16[16,32,512]{2,1,0:T(8,128)(2,1)}), bf16[16,32,512]{2,1,0:T(8,128)(2,1)S(1)}, u32[]{:S(2)}, u32[]{:S(2)}) async-start(bf16[16,32,512]{2,1,0:T(8,128)(2,1)} %row_blocks.1.after_ref), calls=%async_computation.1 | async-start | bytes 1048576 | tf_op jit(solution)/shard_map/all_to_all | solution.py:565
  116.3 0.0 collective-permute-done.6.left_ref
  116.3 3.9 %first_half.1 = f32[2,512,1024]{2,1,0:T(8,128)} custom-call(s32[2]{0:T(128)S(1)} %pad_add_fusion.starts_ref, bf16[2,512,512]{2,1,0:T(8,128)(2,1)S(1)} %copy-done, bf16[2,512,512]{2,1,0:T(8,128)(2,1)S(1)} %collective-permute-done.5.above_ref, bf16[2,512,512]{2,1,0:T(8,128)(2,1)} %collective-permute-done.6.left_ref, ...), custom_call_target="tpu_custom_call", output_to_operand_aliasing={{}: (4, {})} | custom-call | flops 4194304 | bytes 8388608 | tf_op jit(solution)/shard_map/first_half/pallas_call | solution.py:451
  120.2 6.2 %all-to-all-done.1.got_ref = bf16[16,32,512]{2,1,0:T(8,128)(2,1)S(1)} async-done(((bf16[16,32,512]{2,1,0:T(8,128)(2,1)}), bf16[16,32,512]{2,1,0:T(8,128)(2,1)S(1)}, u32[]{:S(2)}, u32[]{:S(2)}) %all-to-all-start.1) | async-done | bytes 524320 | tf_op jit(solution)/shard_map/all_to_all | solution.py:565
  126.4 0.7 last_sum.1
  (13 shorter events, 0.1 us)
Async XLA Ops:
  0.6 1.6 %copy-start.1 = (bf16[2,512,1024]{2,1,0:T(8,128)(2,1)S(1)}, bf16[2,512,1024]{2,1,0:T(8,128)(2,1)}, u32[]{:S(2)}) copy-start(bf16[2,512,1024]{2,1,0:T(8,128)(2,1)} %tile_ref.11) | copy-start | bytes 6291460
  2.2 1.5 %copy-start.7 = (s32[1,2]{1,0:T(1,128)S(1)}, s32[1,2]{1,0:T(1,128)}, u32[]{:S(2)}) copy-start(s32[1,2]{1,0:T(1,128)} %corner_ref.1) | copy-start | bytes 28
  2.2 9.4 %copy-start.2 = (bf16[2,512,1024]{2,1,0:T(8,128)(2,1)S(1)}, bf16[2,512,1024]{2,1,0:T(8,128)(2,1)}, u32[]{:S(2)}) copy-start(bf16[2,512,1024]{2,1,0:T(8,128)(2,1)} %tile_ref.11) | copy-start | bytes 6291460
  2.3 9.3 %collective-permute-start.1 = (bf16[2,256,512]{2,1,0:T(8,128)(2,1)S(1)}, bf16[2,256,512]{2,1,0:T(8,128)(2,1)}, u32[]{:S(2)}, u32[]{:S(2)}) collective-permute-start(bf16[2,256,512]{2,1,0:T(8,128)(2,1)S(1)} %left_columns.2), channel_id=1, source_target_pairs={{1,0},{2,1},{3,2},{4,3},{5,4},{6,5},{7,6},{8,7},{9,8},{10,9},{11,1... | collective-permute-start | bytes 1572872 | tf_op jit(solution)/shard_map/ppermute | solution.py:577
  3.7 7.9 %collective-permute-start = (s32[1,2]{1,0:T(1,128)S(1)}, s32[1,2]{1,0:T(1,128)S(1)}, u32[]{:S(2)}, u32[]{:S(2)}) collective-permute-start(s32[1,2]{1,0:T(1,128)S(1)} %copy-done.7), channel_id=1, source_target_pairs={{0,16},{16,32},{32,48},{48,64},{64,80},{80,96},{96,112},{1,17},{17... | collective-permute-start | bytes 32 | tf_op jit(solution)/shard_map/ppermute | solution.py:576
  9.6 5.5 %collective-permute-start.2 = (bf16[2,256,512]{2,1,0:T(8,128)(2,1)S(1)}, bf16[2,256,512]{2,1,0:T(8,128)(2,1)}, u32[]{:S(2)}, u32[]{:S(2)}) collective-permute-start(bf16[2,256,512]{2,1,0:T(8,128)(2,1)S(1)} %left_columns.3), channel_id=1, source_target_pairs={{1,0},{2,1},{3,2},{4,3},{5,4},{6,5},{7,6},{8,7},{9,8},{10,9},{11,1... | collective-permute-start | bytes 1572872 | tf_op jit(solution)/shard_map/ppermute | solution.py:577
  13.8 17.5 %collective-permute-start.4 = (bf16[2,256,512]{2,1,0:T(8,128)(2,1)}, bf16[2,256,512]{2,1,0:T(8,128)(2,1)}, u32[]{:S(2)}, u32[]{:S(2)}) collective-permute-start(bf16[2,256,512]{2,1,0:T(8,128)(2,1)} %cut_columns.4.after_ref), channel_id=1, source_target_pairs={{16,0},{32,16},{48,32},{64,48},{80,64},{96,80},{112,96},{17,1},{33... | collective-permute-start | bytes 1572872 | tf_op jit(solution)/shard_map/ppermute | solution.py:580
  17.3 25.2 %collective-permute-start.3 = (bf16[2,256,512]{2,1,0:T(8,128)(2,1)}, bf16[2,256,512]{2,1,0:T(8,128)(2,1)}, u32[]{:S(2)}, u32[]{:S(2)}) collective-permute-start(bf16[2,256,512]{2,1,0:T(8,128)(2,1)} %cut_columns.7), channel_id=1, source_target_pairs={{16,0},{32,16},{48,32},{64,48},{80,64},{96,80},{112,96},{17,1},{33... | collective-permute-start | bytes 1572872 | tf_op jit(solution)/shard_map/ppermute | solution.py:580
  20.0 0.8 copy-start.9
  20.8 4.2 %copy-start.4 = (f32[1,512,512]{2,1,0:T(8,128)S(1)}, f32[1,512,512]{2,1,0:T(8,128)}, u32[]{:S(2)}) copy-start(f32[1,512,512]{2,1,0:T(8,128)} %param.11) | copy-start | bytes 3145732
  22.3 0.8 copy-start.10
  25.0 1.0 copy-start.6
  27.9 1.0 copy-start.5
  62.1 6.8 %collective-permute-start.7 = (bf16[4,2,256,512]{3,2,1,0:T(8,128)(2,1)}, bf16[4,2,256,512]{3,2,1,0:T(8,128)(2,1)S(1)}, u32[]{:S(2)}, u32[]{:S(2)}) collective-permute-start(bf16[4,2,256,512]{3,2,1,0:T(8,128)(2,1)} %get-tuple-element.19), channel_id=1, source_target_pairs={{0,1},{1,0},{2,3},{3,2},{4,5},{5,4},{6,7},{7,6},{8,9},{9,8},{10,11... | collective-permute-start | bytes 6291464 | tf_op jit(solution)/shard_map/ppermute | solution.py:559
  63.0 28.7 %collective-permute-start.5 = (bf16[2,512,512]{2,1,0:T(8,128)(2,1)}, bf16[2,512,512]{2,1,0:T(8,128)(2,1)S(1)}, u32[]{:S(2)}, u32[]{:S(2)}) collective-permute-start(bf16[2,512,512]{2,1,0:T(8,128)(2,1)} %get-tuple-element.17), channel_id=1, source_target_pairs={{0,16},{16,32},{32,48},{48,64},{64,80},{80,96},{96,112},{1,17},{17... | collective-permute-start | bytes 3145736 | tf_op jit(solution)/shard_map/ppermute | solution.py:591
  68.9 1.6 %copy-start.8 = (bf16[4,2,256,512]{3,2,1,0:T(8,128)(2,1)S(1)}, bf16[4,2,256,512]{3,2,1,0:T(8,128)(2,1)}, u32[]{:S(2)}) copy-start(bf16[4,2,256,512]{3,2,1,0:T(8,128)(2,1)} %get-tuple-element.18.keep_ref) | copy-start | bytes 6291460
  71.7 1.3 %copy-start.3 = (bf16[4,4,2,64,512]{4,3,2,1,0:T(8,128)(2,1)}, bf16[4,4,2,64,512]{4,3,2,1,0:T(8,128)(2,1)S(1)}, u32[]{:S(2)}) copy-start(bf16[4,4,2,64,512]{4,3,2,1,0:T(8,128)(2,1)S(1)} %chip_sum.1) | copy-start | bytes 6291460
  73.0 18.7 %copy-start = (bf16[2,512,512]{2,1,0:T(8,128)(2,1)S(1)}, bf16[2,512,512]{2,1,0:T(8,128)(2,1)}, u32[]{:S(2)}) copy-start(bf16[2,512,512]{2,1,0:T(8,128)(2,1)} %get-tuple-element.16.up_ref) | copy-start | bytes 3145732
  73.0 32.9 %all-to-all-start = ((bf16[4,4,2,64,512]{4,3,2,1,0:T(8,128)(2,1)}), bf16[4,4,2,64,512]{4,3,2,1,0:T(8,128)(2,1)}, u32[]{:S(2)}, u32[]{:S(2)}) async-start(bf16[4,4,2,64,512]{4,3,2,1,0:T(8,128)(2,1)} %copy-done.3), calls=%async_computation | async-start | bytes 4194304 | tf_op jit(solution)/shard_map/all_to_all | solution.py:561
  93.1 23.2 %collective-permute-start.6 = (bf16[2,512,512]{2,1,0:T(8,128)(2,1)}, bf16[2,512,512]{2,1,0:T(8,128)(2,1)}, u32[]{:S(2)}, u32[]{:S(2)}) collective-permute-start(bf16[2,512,512]{2,1,0:T(8,128)(2,1)} %add_convert_fusion), channel_id=1, source_target_pairs={{0,1},{1,2},{2,3},{3,4},{4,5},{5,6},{6,7},{7,8},{8,9},{9,10},{10,1... | collective-permute-start | bytes 3145736 | tf_op jit(solution)/shard_map/ppermute | solution.py:595
  108.6 17.8 %all-to-all-start.1 = ((bf16[16,32,512]{2,1,0:T(8,128)(2,1)}), bf16[16,32,512]{2,1,0:T(8,128)(2,1)S(1)}, u32[]{:S(2)}, u32[]{:S(2)}) async-start(bf16[16,32,512]{2,1,0:T(8,128)(2,1)} %row_blocks.1.after_ref), calls=%async_computation.1 | async-start | bytes 1048576 | tf_op jit(solution)/shard_map/all_to_all | solution.py:565
